TPU v7x, 128 devices: a whole 4x4x4 slice. The times are simulated.
128 devices in a mesh: lat: 8 (over z_lo, x), lon: 16 (over y, z_hi, core).
Axes of the slice: x: 4, y: 4, z: 4 (z_hi: 2, z_lo: 2; z = z_hi * 2 + z_lo), core: 2. Of those that a mesh axis runs over, the one named last changes fastest.
Arguments:
- hidden: bfloat16 [1, 192, 384, 1152], P(None, 'lat', 'lon'), may hold values from -6 to 6
- timestep: int32 [1], replicated, may hold values from 0 to 999
- context: bfloat16 [1, 300, 1152], replicated, may hold values from -6 to 6
- time_weight: bfloat16 [256, 3456], replicated, may hold values from -0.375 to 0.375
- modulation_bias: float32 [3, 1152], replicated, may hold values from -3 to 3
- qkv_weight: bfloat16 [1152, 3456], replicated, may hold values from -0.1875 to 0.1875
- out_weight: bfloat16 [1152, 1152], replicated, may hold values from -0.1875 to 0.1875
- cross_q: bfloat16 [1152, 1152], replicated, may hold values from -0.1875 to 0.1875
- cross_kv: bfloat16 [2, 1152, 1152], P(None, None, 'lon'), may hold values from -0.1875 to 0.1875
- cross_output_projection: bfloat16 [1152, 1152], replicated, may hold values from -0.1875 to 0.1875
Outputs:
- shifted: bfloat16 [1, 192, 384, 1152], P(None, 'lat', 'lon')
All inputs are finite; a program needn't handle non-finite values.
Results may differ from a plain program's by a relative error of at most 0.012.
Values may be sent and summed in bfloat16 or wider, within the bound.
No kernel may reach another device: no remote copies, remote signals or barrier semaphores. Data moves between devices by JAX's collectives and lax.ppermute only.
A program may use at most 128 MiB of HBM per device.

v0:
```python
import math

import jax
import jax.numpy as jnp
from jax import lax
from jax.sharding import PartitionSpec as P

HEADS = 16
HALO = 4


def extended(block, sides, width, periodic):
    for axis, dim in sides:
        count = lax.axis_size(axis)
        forward = [(i, i + 1) for i in range(count - 1)]
        if periodic:
            forward.append((count - 1, 0))
        backward = [(target, source) for source, target in forward]
        low = lax.ppermute(
            lax.slice_in_dim(block, block.shape[dim] - width, None, axis=dim), axis, forward
        )
        high = lax.ppermute(lax.slice_in_dim(block, 0, width, axis=dim), axis, backward)
        block = jnp.concatenate([low, block, high], axis=dim)
    return block


def shifted(x, axis, by):
    size = lax.axis_size(axis)
    pairs = [(i, i + by) for i in range(size) if 0 <= i + by < size]
    return lax.ppermute(x, axis, pairs)


def from_behind(value, axis, steps):
    count = lax.axis_size(axis)
    pairs = [(source, (source + steps) % count) for source in range(count)]
    return lax.ppermute(value, axis, pairs)


def modulation(timestep, time_weight, modulation_bias):
    half = time_weight.shape[0] // 2
    freqs = jnp.exp(-math.log(10000.0) * jnp.arange(half, dtype=jnp.float32) / half)
    angle = timestep.astype(jnp.float32)[:, None] * freqs[None, :]
    embed = jnp.concatenate([jnp.cos(angle), jnp.sin(angle)], axis=1)
    embed = jax.nn.silu(embed).astype(jnp.bfloat16)
    mixed = (
        jnp.dot(embed, time_weight, preferred_element_type=jnp.float32)
        + modulation_bias.reshape(-1)[None, :]
    )
    width = modulation_bias.shape[1]
    return (mixed[:, :width], mixed[:, width : 2 * width], mixed[:, 2 * width :])


def layer_norm(value_rows):
    mean = jnp.mean(value_rows, axis=-1, keepdims=True)
    centred = value_rows - mean
    var = jnp.mean(centred * centred, axis=-1, keepdims=True)
    return centred * lax.rsqrt(var + 1e-06)


def one_head(operands):
    query_rows, key_rows, value_rows = operands
    head_channels = query_rows.shape[-1]
    logit_scores = jnp.einsum(
        "ciw,cpw->cip", query_rows, key_rows, preferred_element_type=jnp.float32
    ) / math.sqrt(head_channels)
    attention_probabilities = jax.nn.softmax(logit_scores, axis=-1).astype(jnp.bfloat16)
    return jnp.einsum(
        "hmy,hyi->hmi", attention_probabilities, value_rows, preferred_element_type=jnp.float32
    ).astype(jnp.bfloat16)


def attend(query_rows, key_rows, value_rows):
    batch, count, width = query_rows.shape
    head_channels = width // HEADS
    qh = jnp.transpose(query_rows.reshape(batch, count, HEADS, head_channels), (2, 0, 1, 3))
    kh = jnp.transpose(
        key_rows.reshape(batch, key_rows.shape[1], HEADS, head_channels), (2, 0, 1, 3)
    )
    vh = jnp.transpose(
        value_rows.reshape(batch, value_rows.shape[1], HEADS, head_channels), (2, 0, 1, 3)
    )
    mixed = lax.map(one_head, (qh, kh, vh))
    return jnp.transpose(mixed, (1, 2, 0, 3)).reshape(batch, count, width)


def project(value_rows, weight):
    return jnp.einsum("bnd,de->bne", value_rows, weight, preferred_element_type=jnp.float32)


def tile_block(
    tile,
    shift,
    scale,
    gate,
    key_rows,
    value_rows,
    qkv_weight,
    out_weight,
    cross_q,
    cross_output_projection,
):
    batch, rows, cols, width = tile.shape
    x_vals = tile.reshape(batch, rows * cols, width).astype(jnp.float32)
    normed = (layer_norm(x_vals) * (1.0 + scale[:, None, :]) + shift[:, None, :]).astype(
        jnp.bfloat16
    )
    qkv = project(normed, qkv_weight).astype(jnp.bfloat16)
    attn = attend(qkv[:, :, :width], qkv[:, :, width : 2 * width], qkv[:, :, 2 * width :])
    first = x_vals + gate[:, None, :] * project(attn, out_weight)
    cross_query = project(first.astype(jnp.bfloat16), cross_q).astype(jnp.bfloat16)
    crossed = attend(cross_query, key_rows, value_rows)
    second = first + project(crossed, cross_output_projection)
    return second.reshape(batch, rows, cols, width)


def local(
    hidden,
    timestep,
    context,
    time_weight,
    modulation_bias,
    qkv_weight,
    out_weight,
    cross_q,
    cross_kv,
    cross_output_projection,
):
    batch, core, _, width = hidden.shape
    half = core // 2
    rim = HALO
    span = core + 2 * rim
    shift, scale, gate = modulation(timestep, time_weight, modulation_bias)
    extended_latent = extended(hidden, (("lat", 1),), rim, False)
    tile = extended(extended_latent, (("lon", 2),), rim, True)
    own_heads = jnp.einsum(
        "btd,sde->bste", context, cross_kv, preferred_element_type=jnp.float32
    ).astype(jnp.bfloat16)
    text_kv = lax.all_gather(own_heads, "lon", axis=3, tiled=True)
    result = tile_block(
        tile,
        shift,
        scale,
        gate,
        text_kv[:, 0],
        text_kv[:, 1],
        qkv_weight,
        out_weight,
        cross_q,
        cross_output_projection,
    )
    from_below = shifted(result[:, :rim].astype(jnp.bfloat16), "lat", -1).astype(jnp.float32)
    from_above = shifted(result[:, span - rim :].astype(jnp.bfloat16), "lat", 1).astype(jnp.float32)
    folded = result[:, rim : rim + core]
    folded = folded.at[:, core - rim :].add(from_below)
    folded = folded.at[:, :rim].add(from_above)
    lat_index = lax.axis_index("lat")
    lat_count = lax.axis_size("lat")
    row_ids = jnp.arange(core)
    lat_factor = (
        1.0
        + jnp.where((row_ids < rim) & (lat_index > 0), 1.0, 0.0)
        + jnp.where((row_ids >= core - rim) & (lat_index < lat_count - 1), 1.0, 0.0)
    ).astype(jnp.float32)
    col_ids = jnp.arange(core)
    from_right = from_behind(folded[:, :, :rim].astype(jnp.bfloat16), "lon", -1).astype(jnp.float32)
    from_left = from_behind(folded[:, :, span - rim :].astype(jnp.bfloat16), "lon", 1).astype(
        jnp.float32
    )
    inner = folded[:, :, rim : rim + core]
    inner = inner.at[:, :, core - rim :].add(from_right)
    inner = inner.at[:, :, :rim].add(from_left)
    lon_factor = (
        1.0 + jnp.where(col_ids < rim, 1.0, 0.0) + jnp.where(col_ids >= core - rim, 1.0, 0.0)
    ).astype(jnp.float32)
    averaged = (inner / (lat_factor[:, None] * lon_factor[None, :])[None, :, :, None]).astype(
        jnp.bfloat16
    )
    arrived = from_behind(averaged[:, :, :half], "lon", -1)
    return jnp.concatenate([averaged[:, :, half:], arrived], axis=2)


def solution(mesh):
    in_specs = (
        P(None, "lat", "lon", None),
        P(),
        P(),
        P(),
        P(),
        P(),
        P(),
        P(),
        P(None, None, "lon"),
        P(),
    )
    out_specs = P(None, "lat", "lon", None)
    return jax.shard_map(local, mesh=mesh, in_specs=in_specs, out_specs=out_specs, check_vma=False)
```

profile of v0, /device:TPU:33, one launch (start us, length us, event | category | flops | bytes accessed | tf_op | source)
XLA Modules:
  0.0 292.3 jit_solution(18001266512325538864)
XLA Ops:
  7.8 3.1 %collective-permute-start = (bf16[1,4,24,1152]{3,2,1,0:T(8,128)(2,1)S(1)}, bf16[1,4,24,1152]{3,2,1,0:T(8,128)(2,1)S(1)}, u32[]{:S(2)}, u32[]{:S(2)}) collective-permute-start(bf16[1,4,24,1152]{3,2,1,0:T(8,128)(2,1)S(1)} %get-tuple-element.192), channel_id=1, source_target_pairs={{0,16},{16,32},{32,48},{48,64},{64,80},{80,96},{96,112},{1,17},{17... | collective-permute-start | bytes 663560 | tf_op jit(solution)/shard_map/ppermute | solution.py:19
  10.9 4.3 %collective-permute-start.1 = (bf16[1,4,24,1152]{3,2,1,0:T(8,128)(2,1)S(1)}, bf16[1,4,24,1152]{3,2,1,0:T(8,128)(2,1)S(1)}, u32[]{:S(2)}, u32[]{:S(2)}) collective-permute-start(bf16[1,4,24,1152]{3,2,1,0:T(8,128)(2,1)S(1)} %get-tuple-element.191), channel_id=1, source_target_pairs={{16,0},{32,16},{48,32},{64,48},{80,64},{96,80},{112,96},{17,1},{33... | collective-permute-start | bytes 663560 | tf_op jit(solution)/shard_map/ppermute | solution.py:22
  15.2 2.3 fusion.36
  21.5 3.9 %collective-permute-start.2 = (bf16[1,32,4,1152]{3,1,2,0:T(8,128)(2,1)S(1)}, bf16[1,32,4,1152]{3,1,2,0:T(8,128)(2,1)S(1)}, u32[]{:S(2)}, u32[]{:S(2)}) collective-permute-start(bf16[1,32,4,1152]{3,1,2,0:T(8,128)(2,1)S(1)} %copy.63), channel_id=1, source_target_pairs={{0,1},{1,2},{2,3},{3,4},{4,5},{5,6},{6,7},{7,8},{8,9},{9,10},{10,1... | collective-permute-start | bytes 884744 | tf_op jit(solution)/shard_map/ppermute | solution.py:19
  26.0 3.1 %collective-permute-done.2 = bf16[1,32,4,1152]{3,1,2,0:T(8,128)(2,1)S(1)} collective-permute-done((bf16[1,32,4,1152]{3,1,2,0:T(8,128)(2,1)S(1)}, bf16[1,32,4,1152]{3,1,2,0:T(8,128)(2,1)S(1)}, u32[]{:S(2)}, u32[]{:S(2)}) %collective-permute-start.2) | collective-permute-done | bytes 294944 | tf_op jit(solution)/shard_map/ppermute | solution.py:19
  29.3 7.0 %collective-permute-done.3 = bf16[1,32,4,1152]{3,1,2,0:T(8,128)(2,1)S(1)} collective-permute-done((bf16[1,32,4,1152]{3,1,2,0:T(8,128)(2,1)S(1)}, bf16[1,32,4,1152]{3,1,2,0:T(8,128)(2,1)S(1)}, u32[]{:S(2)}, u32[]{:S(2)}) %collective-permute-start.3) | collective-permute-done | bytes 294944 | tf_op jit(solution)/shard_map/ppermute | solution.py:22
  36.5 2.4 convert_reduce_fusion
  39.0 2.6 fusion.30
  42.5 12.3 %fusion.28 = bf16[1,1024,3456]{2,1,0:T(8,128)(2,1)S(1)} fusion(bf16[1024,1152]{1,0:T(8,128)(2,1)S(1)} %fusion.34, bf16[1152,3456]{1,0:T(8,128)(2,1)} %param.27), kind=kOutput, calls=%fused_computation.36 | convolution fusion | flops 8157265920 | bytes 17399808 | tf_op jit(solution)/shard_map/bnd,de->bne/dot_general | solution.py:87
  54.8 3.2 %fusion.51 = (bf16[1,1024,1152]{2,1,0:T(8,128)(2,1)}, bf16[1,1024,1152]{2,1,0:T(8,128)(2,1)}, bf16[1,1024,1152]{2,1,0:T(8,128)(2,1)}) fusion(bf16[1,1024,3456]{2,1,0:T(8,128)(2,1)S(1)} %fusion.28), kind=kLoop, calls=%fused_computation.91 | loop fusion | bytes 14155776 | tf_op jit(solution)/shard_map/slice | solution.py:108
  58.0 4.3 %copy.67 = bf16[1,1024,1152]{1,2,0:T(8,128)(2,1)} copy(bf16[1,1024,1152]{2,1,0:T(8,128)(2,1)} %get-tuple-element.180) | data formatting | bytes 4718592 | tf_op jit(solution)/shard_map/slice | solution.py:108
  62.3 4.3 %copy.68 = bf16[1,1024,1152]{1,2,0:T(8,128)(2,1)} copy(bf16[1,1024,1152]{2,1,0:T(8,128)(2,1)} %get-tuple-element.179) | data formatting | bytes 4718592 | tf_op jit(solution)/shard_map/slice | solution.py:108
  66.5 4.4 %copy.69 = bf16[1,1024,1152]{1,2,0:T(8,128)(2,1)} copy(bf16[1,1024,1152]{2,1,0:T(8,128)(2,1)} %get-tuple-element.178) | data formatting | bytes 4718592 | tf_op jit(solution)/shard_map/slice | solution.py:108
  72.6 80.0 %while.24 = (s32[]{:T(128)}, bf16[16,1,1024,72]{2,3,1,0:T(8,128)(2,1)}, bf16[16,1,1024,72]{2,3,0,1:T(8,128)(2,1)}, bf16[16,1,1024,72]{2,3,0,1:T(8,128)(2,1)}, bf16[16,1,1024,72]{2,3,0,1:T(8,128)(2,1)}, /*index=5*/s32[]{:T(128)}) while((s32[]{:T(128)}, bf16[16,1,1024,72]{2,3,1,0:T(8,128)(2,1)}, bf16[16,1,1024,72]{2,3,0,1:T(8,128)(2,1)}, ...), condition=%wide.region_5.6_spmd, body=%wide.region_2.5_spmd.sunk | while | flops 311498752 | bytes 13195333 | solution.py:82
  75.1 2.5 fusion.77
  80.1 2.5 fusion.77
  85.0 2.5 fusion.77
  90.1 2.5 fusion.77
  95.0 2.5 fusion.77
  100.0 2.5 fusion.77
  105.1 2.5 fusion.77
  110.0 2.5 fusion.77
  115.1 2.5 fusion.77
  120.0 2.5 fusion.77
  125.0 2.5 fusion.77
  130.1 2.5 fusion.77
  135.1 2.5 fusion.77
  140.0 2.5 fusion.77
  145.0 2.5 fusion.77
  150.0 2.5 fusion.77
  152.5 6.1 %bitcast_add_fusion = f32[1024,1152]{1,0:T(8,128)S(1)} fusion(bf16[1,32,32,1152]{3,2,1,0:T(8,128)(2,1)} %get-tuple-element.173, bf16[1024,1152]{0,1:T(8,128)(2,1)} %bitcast.19, bf16[1152,1152]{1,0:T(8,128)(2,1)S(1)} %copy-done, f32[1152]{0:T(1024)S(1)} %get-tuple-element.149), kind=kOutput, calls=%fused_computation.41 | convolution fusion | flops 2721447936 | bytes 12096000 | tf_op jit(solution)/shard_map/bnd,de->bne/dot_general | solution.py:87
  158.7 2.1 copy-done.6
  160.8 4.8 %convolution_convert_fusion.2 = bf16[1024,1152]{1,0:T(8,128)(2,1)} fusion(bf16[1152,1152]{1,0:T(8,128)(2,1)S(1)} %copy-done.5, f32[1024,1152]{1,0:T(8,128)S(1)} %bitcast_add_fusion), kind=kOutput, calls=%fused_computation.49 | convolution fusion | flops 2720268288 | bytes 9732096 | tf_op jit(solution)/shard_map/bnd,de->bne/dot_general | solution.py:87
  165.6 4.3 %copy.73 = bf16[1024,1152]{0,1:T(8,128)(2,1)} copy(bf16[1024,1152]{1,0:T(8,128)(2,1)} %convolution_convert_fusion.2) | data formatting | bytes 4718592 | tf_op jit(solution)/shard_map/convert_element_type | solution.py:110
  169.8 2.5 fusion.54
  172.4 2.4 copy.74
  178.0 54.5 %while.25 = (s32[]{:T(128)}, bf16[16,1,1024,72]{2,3,1,0:T(8,128)(2,1)}, bf16[16,1,1024,72]{2,3,0,1:T(8,128)(2,1)}, bf16[16,1,300,72]{3,2,1,0:T(8,128)(2,1)}, bf16[16,1,300,72]{3,2,1,0:T(8,128)(2,1)}, /*index=5*/s32[]{:T(128)}) while((s32[]{:T(128)}, bf16[16,1,1024,72]{2,3,1,0:T(8,128)(2,1)}, bf16[16,1,1024,72]{2,3,0,1:T(8,128)(2,1)}, ...), condition=%wide.region_9.10_spmd, body=%wide.region_6.9_spmd.sunk | while | flops 90695680 | bytes 4159557 | solution.py:82
  203.2 1.9 fusion.81
  206.6 1.9 fusion.81
  213.5 1.9 fusion.81
  227.1 1.9 fusion.81
  232.4 7.4 %convolution_add_fusion = f32[1024,1152]{1,0:T(8,128)S(1)} fusion(f32[1024,1152]{1,0:T(8,128)} %copy-done.6, bf16[1024,1152]{0,1:T(8,128)(2,1)} %bitcast.31, bf16[1152,1152]{1,0:T(8,128)(2,1)} %param.31), kind=kOutput, calls=%fused_computation.48 | convolution fusion | flops 2719088640 | bytes 14450688 | tf_op jit(solution)/shard_map/bnd,de->bne/dot_general | solution.py:87
  242.0 4.5 %collective-permute-start.4 = (bf16[1,4,32,1152]{3,2,1,0:T(8,128)(2,1)S(1)}, bf16[1,4,32,1152]{3,2,1,0:T(8,128)(2,1)S(1)}, u32[]{:S(2)}, u32[]{:S(2)}) collective-permute-start(bf16[1,4,32,1152]{3,2,1,0:T(8,128)(2,1)S(1)} %get-tuple-element.182), channel_id=1, source_target_pairs={{16,0},{32,16},{48,32},{64,48},{80,64},{96,80},{112,96},{17,1},{33... | collective-permute-start | bytes 884744 | tf_op jit(solution)/shard_map/ppermute | solution.py:30
  246.5 2.2 slice.219
  251.8 9.5 %collective-permute-done.5 = bf16[1,4,32,1152]{3,2,1,0:T(8,128)(2,1)S(1)} collective-permute-done((bf16[1,4,32,1152]{3,2,1,0:T(8,128)(2,1)S(1)}, bf16[1,4,32,1152]{3,2,1,0:T(8,128)(2,1)S(1)}, u32[]{:S(2)}, u32[]{:S(2)}) %collective-permute-start.5) | collective-permute-done | bytes 294944 | tf_op jit(solution)/shard_map/ppermute | solution.py:30
  262.2 3.3 %collective-permute-start.7 = (bf16[1,24,4,1152]{3,2,1,0:T(4,128)(2,1)S(1)}, bf16[1,24,4,1152]{3,2,1,0:T(4,128)(2,1)S(1)}, u32[]{:S(2)}, u32[]{:S(2)}) collective-permute-start(bf16[1,24,4,1152]{3,2,1,0:T(4,128)(2,1)S(1)} %get-tuple-element.183), channel_id=1, source_target_pairs={{0,1},{1,2},{2,3},{3,4},{4,5},{5,6},{6,7},{7,8},{8,9},{9,10},{10,1... | collective-permute-start | bytes 663560 | tf_op jit(solution)/shard_map/ppermute | solution.py:36
  265.5 5.6 %collective-permute-done.6 = bf16[1,24,4,1152]{3,2,1,0:T(4,128)(2,1)S(1)} collective-permute-done((bf16[1,24,4,1152]{3,2,1,0:T(4,128)(2,1)S(1)}, bf16[1,24,4,1152]{3,2,1,0:T(4,128)(2,1)S(1)}, u32[]{:S(2)}, u32[]{:S(2)}) %collective-permute-start.6) | collective-permute-done | bytes 221216 | tf_op jit(solution)/shard_map/ppermute | solution.py:36
  272.4 11.6 %collective-permute-done.8 = bf16[1,24,12,1152]{3,1,2,0:T(8,128)(2,1)S(1)} collective-permute-done((bf16[1,24,12,1152]{3,1,2,0:T(8,128)(2,1)S(1)}, bf16[1,24,12,1152]{3,1,2,0:T(8,128)(2,1)S(1)}, u32[]{:S(2)}, u32[]{:S(2)}) %collective-permute-start.8) | collective-permute-done | bytes 663584 | tf_op jit(solution)/shard_map/ppermute | solution.py:36
  (140 shorter events, 106.2 us)
Async XLA Ops:
  6.5 146.0 %copy-start = (bf16[1152,1152]{1,0:T(8,128)(2,1)S(1)}, bf16[1152,1152]{1,0:T(8,128)(2,1)}, u32[]{:S(2)}) copy-start(bf16[1152,1152]{1,0:T(8,128)(2,1)} %param.28) | copy-start | bytes 7962628
  6.5 163.3 %all-gather.2.cloned.1.call-start = ((), (), s32[]{:S(2)}) async-start(), calls=%async_computation | async-start | bytes 1880064 | tf_op jit(solution)/shard_map/all_gather | solution.py:138
  7.8 11.8 %collective-permute-start = (bf16[1,4,24,1152]{3,2,1,0:T(8,128)(2,1)S(1)}, bf16[1,4,24,1152]{3,2,1,0:T(8,128)(2,1)S(1)}, u32[]{:S(2)}, u32[]{:S(2)}) collective-permute-start(bf16[1,4,24,1152]{3,2,1,0:T(8,128)(2,1)S(1)} %get-tuple-element.192), channel_id=1, source_target_pairs={{0,16},{16,32},{32,48},{48,64},{64,80},{80,96},{96,112},{1,17},{17... | collective-permute-start | bytes 663560 | tf_op jit(solution)/shard_map/ppermute | solution.py:19
  10.9 10.3 %collective-permute-start.1 = (bf16[1,4,24,1152]{3,2,1,0:T(8,128)(2,1)S(1)}, bf16[1,4,24,1152]{3,2,1,0:T(8,128)(2,1)S(1)}, u32[]{:S(2)}, u32[]{:S(2)}) collective-permute-start(bf16[1,4,24,1152]{3,2,1,0:T(8,128)(2,1)S(1)} %get-tuple-element.191), channel_id=1, source_target_pairs={{16,0},{32,16},{48,32},{64,48},{80,64},{96,80},{112,96},{17,1},{33... | collective-permute-start | bytes 663560 | tf_op jit(solution)/shard_map/ppermute | solution.py:22
  19.6 6.0 %copy-start.3 = (bf16[256,3456]{1,0:T(8,128)(2,1)S(1)}, bf16[256,3456]{1,0:T(8,128)(2,1)}, u32[]{:S(2)}) copy-start(bf16[256,3456]{1,0:T(8,128)(2,1)} %param.25) | copy-start | bytes 5308420
  19.6 6.0 %copy-start.4 = (bf16[256,1]{0,1:T(2,128)(2,1)S(1)}, bf16[256,1]{0,1:T(2,128)(2,1)}, u32[]{:S(2)}) copy-start(bf16[256,1]{0,1:T(2,128)(2,1)} %reshape.506) | copy-start | bytes 1540
  21.5 7.6 %collective-permute-start.2 = (bf16[1,32,4,1152]{3,1,2,0:T(8,128)(2,1)S(1)}, bf16[1,32,4,1152]{3,1,2,0:T(8,128)(2,1)S(1)}, u32[]{:S(2)}, u32[]{:S(2)}) collective-permute-start(bf16[1,32,4,1152]{3,1,2,0:T(8,128)(2,1)S(1)} %copy.63), channel_id=1, source_target_pairs={{0,1},{1,2},{2,3},{3,4},{4,5},{5,6},{6,7},{7,8},{8,9},{9,10},{10,1... | collective-permute-start | bytes 884744 | tf_op jit(solution)/shard_map/ppermute | solution.py:19
  25.5 10.8 %collective-permute-start.3 = (bf16[1,32,4,1152]{3,1,2,0:T(8,128)(2,1)S(1)}, bf16[1,32,4,1152]{3,1,2,0:T(8,128)(2,1)S(1)}, u32[]{:S(2)}, u32[]{:S(2)}) collective-permute-start(bf16[1,32,4,1152]{3,1,2,0:T(8,128)(2,1)S(1)} %copy.64), channel_id=1, source_target_pairs={{1,0},{2,1},{3,2},{4,3},{5,4},{6,5},{7,6},{8,7},{9,8},{10,9},{11,1... | collective-permute-start | bytes 884744 | tf_op jit(solution)/shard_map/ppermute | solution.py:22
  39.0 2.6 copy-start.1
  152.5 8.2 %copy-start.5 = (bf16[1152,1152]{1,0:T(8,128)(2,1)S(1)}, bf16[1152,1152]{1,0:T(8,128)(2,1)}, u32[]{:S(2)}) copy-start(bf16[1152,1152]{1,0:T(8,128)(2,1)} %param.29) | copy-start | bytes 7962628
  158.6 2.1 copy-start.6
  239.8 2.1 copy-start.2
  242.0 8.7 %collective-permute-start.4 = (bf16[1,4,32,1152]{3,2,1,0:T(8,128)(2,1)S(1)}, bf16[1,4,32,1152]{3,2,1,0:T(8,128)(2,1)S(1)}, u32[]{:S(2)}, u32[]{:S(2)}) collective-permute-start(bf16[1,4,32,1152]{3,2,1,0:T(8,128)(2,1)S(1)} %get-tuple-element.182), channel_id=1, source_target_pairs={{16,0},{32,16},{48,32},{64,48},{80,64},{96,80},{112,96},{17,1},{33... | collective-permute-start | bytes 884744 | tf_op jit(solution)/shard_map/ppermute | solution.py:30
  248.8 12.6 %collective-permute-start.5 = (bf16[1,4,32,1152]{3,2,1,0:T(8,128)(2,1)S(1)}, bf16[1,4,32,1152]{3,2,1,0:T(8,128)(2,1)S(1)}, u32[]{:S(2)}, u32[]{:S(2)}) collective-permute-start(bf16[1,4,32,1152]{3,2,1,0:T(8,128)(2,1)S(1)} %get-tuple-element.181), channel_id=1, source_target_pairs={{0,16},{16,32},{32,48},{48,64},{64,80},{80,96},{96,112},{1,17},{17... | collective-permute-start | bytes 884744 | tf_op jit(solution)/shard_map/ppermute | solution.py:30
  261.9 9.3 %collective-permute-start.6 = (bf16[1,24,4,1152]{3,2,1,0:T(4,128)(2,1)S(1)}, bf16[1,24,4,1152]{3,2,1,0:T(4,128)(2,1)S(1)}, u32[]{:S(2)}, u32[]{:S(2)}) collective-permute-start(bf16[1,24,4,1152]{3,2,1,0:T(4,128)(2,1)S(1)} %get-tuple-element.184), channel_id=1, source_target_pairs={{0,15},{1,0},{2,1},{3,2},{4,3},{5,4},{6,5},{7,6},{8,7},{9,8},{10,9... | collective-permute-start | bytes 663560 | tf_op jit(solution)/shard_map/ppermute | solution.py:36
  262.2 9.1 %collective-permute-start.7 = (bf16[1,24,4,1152]{3,2,1,0:T(4,128)(2,1)S(1)}, bf16[1,24,4,1152]{3,2,1,0:T(4,128)(2,1)S(1)}, u32[]{:S(2)}, u32[]{:S(2)}) collective-permute-start(bf16[1,24,4,1152]{3,2,1,0:T(4,128)(2,1)S(1)} %get-tuple-element.183), channel_id=1, source_target_pairs={{0,1},{1,2},{2,3},{3,4},{4,5},{5,6},{6,7},{7,8},{8,9},{9,10},{10,1... | collective-permute-start | bytes 663560 | tf_op jit(solution)/shard_map/ppermute | solution.py:36
  272.3 11.7 %collective-permute-start.8 = (bf16[1,24,12,1152]{3,1,2,0:T(8,128)(2,1)S(1)}, bf16[1,24,12,1152]{3,1,2,0:T(8,128)(2,1)S(1)}, u32[]{:S(2)}, u32[]{:S(2)}) collective-permute-start(bf16[1,24,12,1152]{3,1,2,0:T(8,128)(2,1)S(1)} %copy.77), channel_id=1, source_target_pairs={{0,15},{1,0},{2,1},{3,2},{4,3},{5,4},{6,5},{7,6},{8,7},{9,8},{10,9... | collective-permute-start | bytes 1990664 | tf_op jit(solution)/shard_map/ppermute | solution.py:36
Sparse Core Ops, SparseCore 0:
  17.6 49.9 all-gather.1
where the time goes:
time: 295 us; the launch traced here: 292 us
  matrix products  152 us (52%)
  local copies, waits for them, and re-layouts  42.2 us (14%)
  waiting for transfers between devices  36.9 us (13%)
  other arithmetic  24.8 us (8%)
  starting transfers between devices  21.2 us (7%)
  between operations  14.4 us (5%)
    dot_general x32, matrix products, one_head(): jnp.einsum('hmy,hyi->hmi', attention_probabilities, value_rows, preferred...  71.1 us
    dot_general x32, matrix products, one_head(): jnp.einsum('ciw,cpw->cip', query_rows, key_rows, preferred_element_type=j...  48.2 us
    dot_general x4, matrix products, project(): jnp.einsum('bnd,de->bne', value_rows, weight, preferred_element_type=jnp....  30.5 us
    ppermute x3, waiting for transfers between devices, from_behind(): return lax.ppermute(value, axis, pairs)  17.2 us
    reduce_sum x32, other arithmetic, one_head(): jax.nn.softmax(logit_scores, axis=-1).astype(jnp.bfloat16)  14.9 us
    ppermute x2, waiting for transfers between devices, shifted(): return lax.ppermute(x, axis, pairs)  9.53 us
    slice x2, local copies, waits for them, and re-layouts, tile_block(): qkv[:, :, 2 * width:]  7.55 us
    ppermute x2, waiting for transfers between devices, extended(): lax.ppermute(lax.slice_in_dim(block, 0, width, axis=dim), axis, backward)  7.05 us
  transfers between devices with their start and end apart: 10, of which 5 were waited for; matrix products, arithmetic and copies ran while one was open for 48% of the time, Pallas kernels for 0%

commit v1 on v0

v1 whole, which is shorter than its diff:
```python
import functools
import math

import jax
import jax.numpy as jnp
from jax import lax
from jax.experimental import pallas as pl
from jax.experimental.pallas import tpu as pltpu
from jax.sharding import PartitionSpec as P

HEADS = 16
HALO = 4
WIN = 256
QKV_COLS = 384
TEXT_PAD = 384
VMEM = 56 * 1024 * 1024


def modulation(timestep, time_weight, modulation_bias):
    half = time_weight.shape[0] // 2
    freqs = jnp.exp(-math.log(10000.0) * jnp.arange(half, dtype=jnp.float32) / half)
    angle = timestep.astype(jnp.float32)[:, None] * freqs[None, :]
    embed = jnp.concatenate([jnp.cos(angle), jnp.sin(angle)], axis=1)
    embed = jax.nn.silu(embed).astype(jnp.bfloat16)
    mixed = (
        jnp.dot(embed, time_weight, preferred_element_type=jnp.float32)
        + modulation_bias.reshape(-1)[None, :]
    )
    width = modulation_bias.shape[1]
    return (mixed[:, :width], mixed[:, width : 2 * width], mixed[:, 2 * width :])


def qkv_kernel(q_factor, x_ref, shift_ref, scale_ref, w_ref, out_ref, u_ref):
    step = pl.program_id(0)
    count, width = x_ref.shape
    rows = 32

    @pl.when(step == 0)
    def _():
        gain = 1.0 + scale_ref[...]
        shift = shift_ref[...]

        def norm(i, carry):
            part = pl.ds(pl.multiple_of(i * rows, rows), rows)
            x = x_ref[part, :].astype(jnp.float32)
            mean = jnp.mean(x, axis=-1, keepdims=True)
            centred = x - mean
            var = jnp.mean(centred * centred, axis=-1, keepdims=True)
            normed = centred * lax.rsqrt(var + 1e-06)
            u_ref[part, :] = (normed * gain + shift).astype(jnp.bfloat16)
            return carry

        lax.fori_loop(0, count // rows, norm, 0, unroll=2)

    factor = jnp.where(step < width // QKV_COLS, jnp.float32(q_factor), jnp.float32(1.0))
    out_ref[...] = (
        jnp.dot(u_ref[...], w_ref[...], preferred_element_type=jnp.float32) * factor
    ).astype(jnp.bfloat16)


def qkv_of(x, shift, scale, weight):
    count, width = x.shape
    total = weight.shape[1]
    q_factor = math.log2(math.e) / math.sqrt(width // HEADS)
    return pl.pallas_call(
        functools.partial(qkv_kernel, q_factor),
        out_shape=jax.ShapeDtypeStruct((count, total), jnp.bfloat16),
        grid=(total // QKV_COLS,),
        in_specs=[
            pl.BlockSpec((count, width), lambda i: (0, 0)),
            pl.BlockSpec((1, width), lambda i: (0, 0)),
            pl.BlockSpec((1, width), lambda i: (0, 0)),
            pl.BlockSpec((width, QKV_COLS), lambda i: (0, i)),
        ],
        out_specs=pl.BlockSpec((count, QKV_COLS), lambda i: (0, i)),
        scratch_shapes=[pltpu.VMEM((count, width), jnp.bfloat16)],
        compiler_params=pltpu.CompilerParams(vmem_limit_bytes=VMEM),
        cost_estimate=pl.CostEstimate(
            flops=2 * count * width * total,
            bytes_accessed=2 * (width * total + count * (width + total)),
            transcendentals=0,
        ),
    )(x, shift, scale, weight)


def window(h, width, channels):
    start = jnp.minimum((h * channels) // 128, (width - WIN) // 128)
    start = pl.multiple_of(start * 128, 128)
    return start, h * channels - start


def lane_mask(offset, channels, dims, axis):
    ids = lax.broadcasted_iota(jnp.int32, dims, axis)
    return (ids >= offset) & (ids < offset + channels)


def soft_rows(s, valid):
    if valid < s.shape[1]:
        ids = lax.broadcasted_iota(jnp.int32, s.shape, 1)
        s = jnp.where(ids < valid, s, -jnp.inf)
    m = jnp.max(s, axis=-1, keepdims=True)
    return jnp.exp2(s - m).astype(jnp.bfloat16)


NT = (((1,), (1,)), ((), ()))


def heads_loop(channels, chunk, q_ref, load_keys, load_values, key_dims, value_dims, value_axis, valid, s_refs, out_ref):
    count, width = q_ref.shape
    chunks = [slice(c, c + chunk) for c in range(0, count, chunk)]

    def masked_q(h):
        start, offset = window(h, width, channels)
        keep = lane_mask(offset, channels, (1, WIN), 1).astype(jnp.float32).astype(jnp.bfloat16)
        return start, keep

    def scores(h, s_ref, part):
        start, keep = masked_q(h)
        q = q_ref[part, pl.ds(start, WIN)] * keep
        s_ref[part, :] = lax.dot_general(
            q, load_keys(start), key_dims, preferred_element_type=jnp.float32
        )

    def finish(h, s_ref, part):
        start, offset = window(h, width, channels)
        v = load_values(start)
        dims = (1, WIN) if value_axis == 1 else (WIN, 1)
        keep = lane_mask(offset, channels, dims, value_axis).astype(jnp.float32).astype(jnp.bfloat16)
        v = v * keep + (1 - keep)
        p = soft_rows(s_ref[part, :], valid)
        o = lax.dot_general(p, v, value_dims, preferred_element_type=jnp.float32)
        inside = lane_mask(offset, channels, (1, WIN), 1)
        total = jnp.max(jnp.where(inside, 0.0, o), axis=-1, keepdims=True)
        o = o / total
        old = out_ref[part, pl.ds(start, WIN)].astype(jnp.float32)
        out_ref[part, pl.ds(start, WIN)] = jnp.where(inside, o, old).astype(jnp.bfloat16)

    first, second = s_refs
    for part in chunks:
        scores(jnp.int32(0), first, part)

    def step(t, carry):
        h = 2 * t
        for part in chunks:
            scores(h + 1, second, part)
            finish(h, first, part)
        after = jnp.minimum(h + 2, HEADS - 1)
        for part in chunks:
            scores(after, first, part)
            finish(h + 1, second, part)
        return carry

    lax.fori_loop(0, HEADS // 2, step, 0)


def attention_kernel(
    segments,
    parts,
    text,
    chunk,
    x_core,
    x_rim,
    qkv_core,
    qkv_rim,
    text_kv,
    gate_ref,
    out_weight,
    cross_q,
    cross_out,
    *rest,
):
    outs = rest[: len(parts)]
    (x_s, q_s, k_s, v_s, kv_s, wo_s, wq_s, wc_s, attn_s, h1_s, s_a, s_b, c_a, c_b, sems) = rest[
        len(parts) :
    ]
    core_count, width = x_core.shape
    channels = width // HEADS
    sources = {"core": (x_core, qkv_core), "rim": (x_rim, qkv_rim)}
    rim_count = x_rim.shape[0]

    def copies(pairs, sem):
        made = [pltpu.make_async_copy(a, b, sems.at[sem, n]) for n, (a, b) in enumerate(pairs)]
        for c in made:
            c.start()
        return made

    q_pairs, x_pairs = [], []
    for name, src, dst, n in segments:
        x, qkv = sources[name]
        q_pairs.append((qkv.at[pl.ds(src, n), pl.ds(0, width)], q_s.at[pl.ds(dst, n)]))
        x_pairs.append((x.at[pl.ds(src, n)], x_s.at[pl.ds(dst, n)]))
    waits_q = copies(q_pairs, 0)
    waits_k = copies(
        [
            (qkv_core.at[:, pl.ds(width, width)], k_s.at[pl.ds(0, core_count)]),
            (qkv_rim.at[:, pl.ds(width, width)], k_s.at[pl.ds(core_count, rim_count)]),
        ],
        1,
    )
    waits_v = copies(
        [
            (qkv_core.at[:, pl.ds(2 * width, width)], v_s.at[pl.ds(0, core_count)]),
            (qkv_rim.at[:, pl.ds(2 * width, width)], v_s.at[pl.ds(core_count, rim_count)]),
        ],
        2,
    )
    waits_later = copies(
        [(out_weight, wo_s), (cross_q, wq_s), (cross_out, wc_s), (text_kv, kv_s)], 3
    )
    waits_x = copies(x_pairs, 4)
    for c in waits_q + waits_k + waits_v:
        c.wait()

    attn_s[...] = jnp.zeros_like(attn_s)
    heads_loop(
        channels,
        chunk,
        q_s,
        lambda start: k_s[:, pl.ds(start, WIN)],
        lambda start: v_s[:, pl.ds(start, WIN)],
        NT,
        (((1,), (0,)), ((), ())),
        1,
        k_s.shape[0],
        (s_a, s_b),
        attn_s,
    )
    for c in waits_later + waits_x:
        c.wait()
    cols = 384
    q_factor = math.log2(math.e) / math.sqrt(channels)
    for n in range(0, width, cols):
        part = slice(n, n + cols)
        mixed = jnp.dot(attn_s[...], wo_s[:, part], preferred_element_type=jnp.float32)
        h1_s[:, part] = x_s[:, part].astype(jnp.float32) + gate_ref[:, part] * mixed
    x_s[...] = h1_s[...].astype(jnp.bfloat16)
    for n in range(0, width, cols):
        part = slice(n, n + cols)
        q_s[:, part] = (
            jnp.dot(x_s[...], wq_s[:, part], preferred_element_type=jnp.float32) * q_factor
        ).astype(jnp.bfloat16)
    heads_loop(
        channels,
        chunk,
        q_s,
        lambda start: kv_s[0, pl.ds(start, WIN), :],
        lambda start: kv_s[1, pl.ds(start, WIN), :],
        (((1,), (0,)), ((), ())),
        NT,
        0,
        text,
        (c_a, c_b),
        attn_s,
    )
    for n in range(0, width, cols):
        part = slice(n, n + cols)
        h1_s[:, part] += jnp.dot(attn_s[...], wc_s[:, part], preferred_element_type=jnp.float32)
    at = 0
    for out, n in zip(outs, parts):
        out[...] = h1_s[at : at + n, :].astype(jnp.bfloat16)
        at += n


def attention_of(segments, parts, text, chunk, x_core, x_rim, qkv_core, qkv_rim, text_kv, gate, out_weight, cross_q, cross_out):
    width = x_core.shape[1]
    count = sum(parts)
    keys = x_core.shape[0] + x_rim.shape[0]
    anywhere = pl.BlockSpec(memory_space=pl.ANY)
    local = pl.BlockSpec(memory_space=pltpu.VMEM)
    bf16, f32 = jnp.bfloat16, jnp.float32
    padded = text_kv.shape[-1]
    return pl.pallas_call(
        functools.partial(attention_kernel, segments, parts, text, chunk),
        out_shape=[jax.ShapeDtypeStruct((n, width), bf16) for n in parts],
        in_specs=[anywhere] * 5 + [local] + [anywhere] * 3,
        out_specs=[local] * len(parts),
        scratch_shapes=[
            pltpu.VMEM((count, width), bf16),
            pltpu.VMEM((count, width), bf16),
            pltpu.VMEM((keys, width), bf16),
            pltpu.VMEM((keys, width), bf16),
            pltpu.VMEM(text_kv.shape, bf16),
            pltpu.VMEM((width, width), bf16),
            pltpu.VMEM((width, width), bf16),
            pltpu.VMEM((width, width), bf16),
            pltpu.VMEM((count, width), bf16),
            pltpu.VMEM((count, width), f32),
            pltpu.VMEM((count, keys), f32),
            pltpu.VMEM((count, keys), f32),
            pltpu.VMEM((count, padded), f32),
            pltpu.VMEM((count, padded), f32),
            pltpu.SemaphoreType.DMA((5, 8)),
        ],
        compiler_params=pltpu.CompilerParams(vmem_limit_bytes=VMEM),
        cost_estimate=pl.CostEstimate(
            flops=16 * count * width * (keys + padded) + 6 * count * width * width,
            bytes_accessed=2 * (3 * width * width + 3 * keys * width),
            transcendentals=HEADS * count * (keys + text),
        ),
    )(x_core, x_rim, qkv_core, qkv_rim, text_kv, gate, out_weight, cross_q, cross_out)


def send(value, mesh_sizes, down, right):
    rows, cols = mesh_sizes
    pairs = [
        (r * cols + c, (r + down) * cols + (c + right) % cols)
        for r in range(rows)
        for c in range(cols)
        if 0 <= r + down < rows
    ]
    return lax.ppermute(value, ("lat", "lon"), pairs)


def local(
    sizes,
    hidden,
    timestep,
    context,
    time_weight,
    modulation_bias,
    qkv_weight,
    out_weight,
    cross_q,
    cross_kv,
    cross_output_projection,
):
    batch, core, _, width = hidden.shape
    half = core // 2
    rim = HALO
    text = context.shape[1]
    to = functools.partial(send, mesh_sizes=sizes)

    x = jnp.transpose(hidden[0], (1, 0, 2))
    left = to(x[core - rim :], down=0, right=1)
    right = to(x[:rim], down=0, right=-1)
    last, first = x[:, core - rim :], x[:, :rim]
    top = to(last, down=1, right=0)
    bottom = to(first, down=-1, right=0)
    top_left = to(last[core - rim :], down=1, right=1)
    top_right = to(last[:rim], down=1, right=-1)
    bottom_left = to(first[core - rim :], down=-1, right=1)
    bottom_right = to(first[:rim], down=-1, right=-1)

    padded = jnp.pad(context[0], ((0, TEXT_PAD - text), (0, 0)))
    own_heads = jnp.einsum(
        "td,sde->set", padded, cross_kv, preferred_element_type=jnp.float32
    ).astype(jnp.bfloat16)
    text_kv = lax.all_gather(own_heads, "lon", axis=1, tiled=True)

    shift, scale, gate = modulation(timestep, time_weight, modulation_bias)
    x_core = x.reshape(core * core, width)
    qkv_core = qkv_of(x_core, shift, scale, qkv_weight)

    flat = lambda a: a.reshape(-1, width)
    x_rim = jnp.concatenate(
        [
            flat(left),
            flat(right),
            flat(top_left),
            flat(top[:half]),
            flat(bottom_left),
            flat(bottom[:half]),
            flat(top[half:]),
            flat(top_right),
            flat(bottom[half:]),
            flat(bottom_right),
        ],
        axis=0,
    )
    qkv_rim = qkv_of(x_rim, shift, scale, qkv_weight)

    side = rim * core
    inner = half * core
    edge = (half + rim) * rim
    weights = (out_weight, cross_q, cross_output_projection)
    operands = (x_core, x_rim, qkv_core, qkv_rim, text_kv, gate) + weights
    sent = attention_of(
        (("rim", 0, 0, side), ("core", 0, side, inner), ("rim", 2 * side, side + inner, 4 * edge)),
        (side + inner, edge, edge, edge, edge),
        text,
        320,
        *operands,
    )
    main = to(sent[0], down=0, right=-1)
    up_left = to(sent[1], down=-1, right=-1)
    down_left = to(sent[2], down=1, right=-1)
    up = to(sent[3], down=-1, right=0)
    down = to(sent[4], down=1, right=0)
    (own,) = attention_of(
        (("core", inner, 0, inner), ("rim", side, inner, side)),
        (inner + side,),
        text,
        384,
        *operands,
    )

    span = half + rim
    f32 = jnp.float32

    def placed(inside, low, high):
        body = inside.reshape(span, core, width).astype(f32)
        low = low.reshape(span, rim, width).astype(f32)
        high = high.reshape(span, rim, width).astype(f32)
        edges = jnp.concatenate(
            [low, jnp.zeros((span, core - 2 * rim, width), f32), high], axis=1
        )
        return body + edges

    near = placed(own, down, up)
    far = placed(main, down_left, up_left)
    rest = core - span
    total = jnp.concatenate([near[:rest], near[rest:] + far[: span - rest], far[span - rest :]], axis=0)
    lat_index = lax.axis_index("lat")
    ids = jnp.arange(core)
    lat_factor = (
        1.0
        + jnp.where((ids < rim) & (lat_index > 0), 1.0, 0.0)
        + jnp.where((ids >= core - rim) & (lat_index < sizes[0] - 1), 1.0, 0.0)
    ).astype(f32)
    lon_factor = jnp.where((ids >= rest) & (ids < span), 2.0, 1.0).astype(f32)
    averaged = total / (lon_factor[:, None] * lat_factor[None, :])[:, :, None]
    return jnp.transpose(averaged.astype(jnp.bfloat16), (1, 0, 2))[None]


def solution(mesh):
    in_specs = (
        P(None, "lat", "lon", None),
        P(),
        P(),
        P(),
        P(),
        P(),
        P(),
        P(),
        P(None, None, "lon"),
        P(),
    )
    out_specs = P(None, "lat", "lon", None)
    sizes = (mesh.shape["lat"], mesh.shape["lon"])
    return jax.shard_map(
        functools.partial(local, sizes), mesh=mesh, in_specs=in_specs, out_specs=out_specs, check_vma=False
    )
```

time: 295 us -> 196 us (0.66)
  matrix products: 152 us -> 1.95 us
  Pallas kernels: 0 us -> 91.8 us
  waiting for transfers between devices: 36.9 us -> 4.3 us
  starting transfers between devices: 21.2 us -> 48.9 us
  other arithmetic: 24.8 us -> 5.69 us
  local copies, waits for them, and re-layouts: 42.2 us -> 27.3 us
    dot_general x69 -> x0, matrix products: 152 us -> none  [the longest x32 71.1 us: one_head(): jnp.einsum('hmy,hyi->hmi', attention_probabilities, value_rows, preferred...]
    pallas_call x0 -> x4, Pallas kernels: none -> 91.8 us  [the longest x2 64.5 us: attention_of(): pl.pallas_call(functools.partial(attention_kernel, segments, parts, text,...]
    ppermute x9 -> x13, waiting for transfers between devices: 36.9 us -> 4.28 us  [send(): return lax.ppermute(value, ('lat', 'lon'), pairs)]
    ppermute x9 -> x13, starting transfers between devices: 21.2 us -> 48.9 us  [send(): return lax.ppermute(value, ('lat', 'lon'), pairs)]
    reduce_sum x34 -> x0, other arithmetic: 19.9 us -> none  [the longest x32 14.9 us: one_head(): jax.nn.softmax(logit_scores, axis=-1).astype(jnp.bfloat16)]
    slice x15 -> x10, local copies, waits for them, and re-layouts: 23.2 us -> 4.37 us  [the longest x1 1.86 us: local(): bottom_right = to(first[:rim], down=-1, right=-1)]
    convert_element_type x1 -> x8, local copies, waits for them, and re-layouts: 4.26 us -> 12.9 us  [the longest x4 6.79 us: placed(): low = low.reshape(span, rim, width).astype(f32)]
    another operation x4 -> x1, local copies, waits for them, and re-layouts: 7.3 us -> 0.01 us
  transfers between devices with their start and end apart: 10 -> 14, of which waited for: 5 -> 1; matrix products, arithmetic and copies ran while one was open for 48% -> 15% of each run, Pallas kernels for 0% -> 28%
where the time goes in v1:
time: 196 us; the launch traced here: 194 us
  Pallas kernels  91.8 us (47%)
  starting transfers between devices  48.9 us (25%)
  local copies, waits for them, and re-layouts  27.3 us (14%)
  between operations  14.5 us (7%)
  other arithmetic  5.69 us (3%)
  waiting for transfers between devices  4.3 us (2%)
    pallas_call x2, Pallas kernels, attention_of(): pl.pallas_call(functools.partial(attention_kernel, segments, parts, text,...  64.5 us
    ppermute x13, starting transfers between devices, send(): return lax.ppermute(value, ('lat', 'lon'), pairs)  48.9 us
    pallas_call x2, Pallas kernels, qkv_of(): pl.pallas_call(functools.partial(qkv_kernel, q_factor), out_shape=jax.Sha...  27.3 us
    convert_element_type x4, local copies, waits for them, and re-layouts, placed(): low = low.reshape(span, rim, width).astype(f32)  6.79 us
    convert_element_type x4, local copies, waits for them, and re-layouts, placed(): high = high.reshape(span, rim, width).astype(f32)  6.14 us
    ppermute x13, waiting for transfers between devices, send(): return lax.ppermute(value, ('lat', 'lon'), pairs)  4.28 us
    ppermute x6, local copies, waits for them, and re-layouts, send(): return lax.ppermute(value, ('lat', 'lon'), pairs)  4.13 us
  transfers between devices with their start and end apart: 14, of which 1 were waited for; matrix products, arithmetic and copies ran while one was open for 15% of the time, Pallas kernels for 28%

profile of v1, /device:TPU:33, one launch (start us, length us, event | category | flops | bytes accessed | tf_op | source)
XLA Modules:
  0.0 194.4 jit_solution(793814193364005843)
XLA Ops:
  6.5 1.9 fusion.10
  8.4 4.5 %collective-permute-start.7 = (bf16[4,4,1152]{2,0,1:T(4,128)(2,1)}, bf16[4,4,1152]{2,0,1:T(4,128)(2,1)}, u32[]{:S(2)}, u32[]{:S(2)}) collective-permute-start(bf16[4,4,1152]{2,0,1:T(4,128)(2,1)} %get-tuple-element.18), channel_id=1, source_target_pairs={{16,15},{17,0},{18,1},{19,2},{20,3},{21,4},{22,5},{23,6},{24,7},{2... | collective-permute-start | bytes 110600 | tf_op jit(solution)/shard_map/ppermute | solution.py:311
  12.9 5.9 %collective-permute-start.6 = (bf16[4,4,1152]{2,0,1:T(4,128)(2,1)}, bf16[4,4,1152]{2,0,1:T(4,128)(2,1)}, u32[]{:S(2)}, u32[]{:S(2)}) collective-permute-start(bf16[4,4,1152]{2,0,1:T(4,128)(2,1)} %get-tuple-element.19), channel_id=1, source_target_pairs={{0,31},{1,16},{2,17},{3,18},{4,19},{5,20},{6,21},{7,22},{8,23},{9,... | collective-permute-start | bytes 110600 | tf_op jit(solution)/shard_map/ppermute | solution.py:311
  18.8 1.9 collective-permute-start.4
  20.8 2.3 %collective-permute-start.2 = (bf16[4,4,1152]{2,0,1:T(4,128)(2,1)}, bf16[4,4,1152]{2,0,1:T(4,128)(2,1)}, u32[]{:S(2)}, u32[]{:S(2)}) collective-permute-start(bf16[4,4,1152]{2,0,1:T(4,128)(2,1)} %get-tuple-element.21), channel_id=1, source_target_pairs={{0,17},{1,18},{2,19},{3,20},{4,21},{5,22},{6,23},{7,24},{8,25},{9,... | collective-permute-start | bytes 110600 | tf_op jit(solution)/shard_map/ppermute | solution.py:311
  23.1 1.6 fusion.2
  24.7 0.7 convert_bitcast_fusion
  25.4 0.8 fusion.11
  26.2 5.8 %collective-permute-start.5 = (bf16[24,4,1152]{2,0,1:T(8,128)(2,1)}, bf16[24,4,1152]{2,0,1:T(8,128)(2,1)S(1)}, u32[]{:S(2)}, u32[]{:S(2)}) collective-permute-start(bf16[24,4,1152]{2,0,1:T(8,128)(2,1)} %get-tuple-element.22), channel_id=1, source_target_pairs={{16,0},{17,1},{18,2},{19,3},{20,4},{21,5},{22,6},{23,7},{24,8},{25... | collective-permute-start | bytes 663560 | tf_op jit(solution)/shard_map/ppermute | solution.py:311
  32.0 0.9 fusion.12
  32.9 1.2 copy.11
  34.8 0.7 broadcast_in_dim_reshape.3
  35.6 0.4 convolution_reduce_fusion
  36.0 0.6 fusion.15
  36.6 14.4 %shard_map.100.qkv_core = bf16[576,3456]{1,0:T(8,128)(2,1)} custom-call(bf16[576,1152]{1,0:T(8,128)(2,1)} %bitcast.29, f32[1,1152]{1,0:T(1,128)} %get-tuple-element.32.shift_ref, f32[1,1152]{1,0:T(1,128)} %get-tuple-element.31.scale_ref, bf16[1152,3456]{1,0:T(8,128)(2,1)} %w_ref.3), custom_call_target="tpu_custom_call" | custom-call | flops 4586471424 | bytes 13271040 | tf_op jit(solution)/shard_map/pallas_call | solution.py:65
  51.2 0.8 collective-permute-start.1
  51.9 0.8 copy.21
  52.7 0.6 reshape.142
  53.4 4.0 %collective-permute-start = (bf16[4,24,1152]{2,0,1:T(4,128)(2,1)S(1)}, bf16[4,24,1152]{2,0,1:T(4,128)(2,1)}, u32[]{:S(2)}, u32[]{:S(2)}) collective-permute-start(bf16[4,24,1152]{2,0,1:T(4,128)(2,1)S(1)} %get-tuple-element.25), channel_id=1, source_target_pairs={{0,1},{1,2},{2,3},{3,4},{4,5},{5,6},{6,7},{7,8},{8,9},{9,10},{10,1... | collective-permute-start | bytes 663560 | tf_op jit(solution)/shard_map/ppermute | solution.py:311
  57.3 0.8 copy.19
  58.1 0.6 reshape.140
  58.8 2.1 %collective-permute-start.3 = (bf16[24,4,1152]{2,0,1:T(8,128)(2,1)S(1)}, bf16[24,4,1152]{2,0,1:T(8,128)(2,1)S(1)}, u32[]{:S(2)}, u32[]{:S(2)}) collective-permute-start(bf16[24,4,1152]{2,0,1:T(8,128)(2,1)S(1)} %copy-done.6), channel_id=1, source_target_pairs={{0,16},{1,17},{2,18},{3,19},{4,20},{5,21},{6,22},{7,23},{8,24},{9,... | collective-permute-start | bytes 663560 | tf_op jit(solution)/shard_map/ppermute | solution.py:311
  60.9 0.8 copy.16
  61.7 0.6 reshape.137
  62.3 0.8 copy.14
  63.1 0.6 reshape.135
  63.7 4.2 %collective-permute-done.3 = bf16[24,4,1152]{2,0,1:T(8,128)(2,1)S(1)} collective-permute-done((bf16[24,4,1152]{2,0,1:T(8,128)(2,1)S(1)}, bf16[24,4,1152]{2,0,1:T(8,128)(2,1)S(1)}, u32[]{:S(2)}, u32[]{:S(2)}) %collective-permute-start.3) | collective-permute-done | bytes 221216 | tf_op jit(solution)/shard_map/ppermute | solution.py:311
  68.5 1.0 copy.12
  69.7 1.0 copy-done.11
  70.6 12.9 %shard_map.101.qkv_rim = bf16[448,3456]{1,0:T(8,128)(2,1)} custom-call(bf16[448,1152]{1,0:T(8,128)(2,1)} %copy-done.11, f32[1,1152]{1,0:T(1,128)} %get-tuple-element.32.shift_ref, f32[1,1152]{1,0:T(1,128)} %get-tuple-element.31.scale_ref, bf16[1152,3456]{1,0:T(8,128)(2,1)} %w_ref.3), custom_call_target="tpu_custom_call" | custom-call | flops 3567255552 | bytes 12091392 | tf_op jit(solution)/shard_map/pallas_call | solution.py:65
  83.5 38.3 %shard_map.103 = (bf16[384,1152]{1,0:T(8,128)(2,1)}, bf16[64,1152]{1,0:T(8,128)(2,1)}, bf16[64,1152]{1,0:T(8,128)(2,1)}, bf16[64,1152]{1,0:T(8,128)(2,1)}, bf16[64,1152]{1,0:T(8,128)(2,1)}) custom-call(bf16[576,1152]{1,0:T(8,128)(2,1)} %bitcast.30, bf16[448,1152]{1,0:T(8,128)(2,1)} %copy-done.11, bf16[576,3456]{1,0:T(8,128)(2,1)} %shard_map.100.qkv_core, ...), custom_call_target="tpu_custom_call" | custom-call | flops 21705523200 | bytes 15040512 | tf_op jit(solution)/shard_map/pallas_call | solution.py:272
  121.8 1.9 collective-permute-start.8
  123.8 5.5 %collective-permute-start.9 = (bf16[64,1152]{1,0:T(8,128)(2,1)}, bf16[64,1152]{1,0:T(8,128)(2,1)}, u32[]{:S(2)}, u32[]{:S(2)}) collective-permute-start(bf16[64,1152]{1,0:T(8,128)(2,1)} %get-tuple-element.11), channel_id=1, source_target_pairs={{16,0},{17,1},{18,2},{19,3},{20,4},{21,5},{22,6},{23,7},{24,8},{25... | collective-permute-start | bytes 442376 | tf_op jit(solution)/shard_map/ppermute | solution.py:311
  129.2 2.7 %collective-permute-start.11 = (bf16[64,1152]{1,0:T(8,128)(2,1)}, bf16[64,1152]{1,0:T(8,128)(2,1)}, u32[]{:S(2)}, u32[]{:S(2)}) collective-permute-start(bf16[64,1152]{1,0:T(8,128)(2,1)} %get-tuple-element.13), channel_id=1, source_target_pairs={{0,31},{1,16},{2,17},{3,18},{4,19},{5,20},{6,21},{7,22},{8,23},{9,... | collective-permute-start | bytes 442376 | tf_op jit(solution)/shard_map/ppermute | solution.py:311
  131.9 11.2 %collective-permute-start.12 = (bf16[64,1152]{1,0:T(8,128)(2,1)}, bf16[64,1152]{1,0:T(8,128)(2,1)}, u32[]{:S(2)}, u32[]{:S(2)}) collective-permute-start(bf16[64,1152]{1,0:T(8,128)(2,1)} %get-tuple-element.14), channel_id=1, source_target_pairs={{16,15},{17,0},{18,1},{19,2},{20,3},{21,4},{22,5},{23,6},{24,7},{2... | collective-permute-start | bytes 442376 | tf_op jit(solution)/shard_map/ppermute | solution.py:311
  143.4 26.2 %shard_map.102 = bf16[384,1152]{1,0:T(8,128)(2,1)} custom-call(bf16[576,1152]{1,0:T(8,128)(2,1)} %bitcast.31, bf16[448,1152]{1,0:T(8,128)(2,1)} %copy-done.11, bf16[576,3456]{1,0:T(8,128)(2,1)} %shard_map.100.qkv_core, bf16[448,3456]{1,0:T(8,128)(2,1)} %shard_map.101.qkv_rim, bf16[2,1152,384]{2,1,0:T(8,128)(2,1)} %all-gather.2.cloned.1.call-done.text_kv, ...), custom_call_target="tpu_custom_call" | custom-call | flops 13023313920 | bytes 15040512 | tf_op jit(solution)/shard_map/pallas_call | solution.py:272
  169.6 1.3 convert.6
  170.9 1.7 reshape.144
  172.6 1.7 copy.22
  174.3 1.7 reshape.145
  176.0 1.7 copy.23
  177.7 1.7 reshape.147
  179.4 1.7 copy.25
  181.1 1.7 reshape.148
  182.8 1.1 copy.26
  183.9 1.3 convert.7
  185.2 0.7 maximum_add_fusion
  186.2 1.4 fusion.1
  (70 shorter events, 1.4 us)
Async XLA Ops:
  6.5 29.0 %copy-start = (bf16[256,3456]{1,0:T(8,128)(2,1)S(1)}, bf16[256,3456]{1,0:T(8,128)(2,1)}, u32[]{:S(2)}) copy-start(bf16[256,3456]{1,0:T(8,128)(2,1)} %param.13) | copy-start | bytes 5308420
  6.5 18.9 %copy-start.1 = (bf16[1,24,24,1152]{3,2,1,0:T(8,128)(2,1)S(1)}, bf16[1,24,24,1152]{3,2,1,0:T(8,128)(2,1)}, u32[]{:S(2)}) copy-start(bf16[1,24,24,1152]{3,2,1,0:T(8,128)(2,1)} %param.10) | copy-start | bytes 3981316
  6.5 77.0 %all-gather.2.cloned.1.call-start = ((), (), s32[]{:S(2)}) async-start(), calls=%async_computation | async-start | bytes 1880064 | tf_op jit(solution)/shard_map/all_gather | solution.py:348
  8.4 42.8 %collective-permute-start.7 = (bf16[4,4,1152]{2,0,1:T(4,128)(2,1)}, bf16[4,4,1152]{2,0,1:T(4,128)(2,1)}, u32[]{:S(2)}, u32[]{:S(2)}) collective-permute-start(bf16[4,4,1152]{2,0,1:T(4,128)(2,1)} %get-tuple-element.18), channel_id=1, source_target_pairs={{16,15},{17,0},{18,1},{19,2},{20,3},{21,4},{22,5},{23,6},{24,7},{2... | collective-permute-start | bytes 110600 | tf_op jit(solution)/shard_map/ppermute | solution.py:311
  12.9 40.5 %collective-permute-start.6 = (bf16[4,4,1152]{2,0,1:T(4,128)(2,1)}, bf16[4,4,1152]{2,0,1:T(4,128)(2,1)}, u32[]{:S(2)}, u32[]{:S(2)}) collective-permute-start(bf16[4,4,1152]{2,0,1:T(4,128)(2,1)} %get-tuple-element.19), channel_id=1, source_target_pairs={{0,31},{1,16},{2,17},{3,18},{4,19},{5,20},{6,21},{7,22},{8,23},{9,... | collective-permute-start | bytes 110600 | tf_op jit(solution)/shard_map/ppermute | solution.py:311
  18.8 39.9 %collective-permute-start.4 = (bf16[4,4,1152]{2,0,1:T(4,128)(2,1)}, bf16[4,4,1152]{2,0,1:T(4,128)(2,1)}, u32[]{:S(2)}, u32[]{:S(2)}) collective-permute-start(bf16[4,4,1152]{2,0,1:T(4,128)(2,1)} %get-tuple-element.20), channel_id=1, source_target_pairs={{16,1},{17,2},{18,3},{19,4},{20,5},{21,6},{22,7},{23,8},{24,9},{25... | collective-permute-start | bytes 110600 | tf_op jit(solution)/shard_map/ppermute | solution.py:311
  20.8 41.5 %collective-permute-start.2 = (bf16[4,4,1152]{2,0,1:T(4,128)(2,1)}, bf16[4,4,1152]{2,0,1:T(4,128)(2,1)}, u32[]{:S(2)}, u32[]{:S(2)}) collective-permute-start(bf16[4,4,1152]{2,0,1:T(4,128)(2,1)} %get-tuple-element.21), channel_id=1, source_target_pairs={{0,17},{1,18},{2,19},{3,20},{4,21},{5,22},{6,23},{7,24},{8,25},{9,... | collective-permute-start | bytes 110600 | tf_op jit(solution)/shard_map/ppermute | solution.py:311
  26.2 37.5 %collective-permute-start.5 = (bf16[24,4,1152]{2,0,1:T(8,128)(2,1)}, bf16[24,4,1152]{2,0,1:T(8,128)(2,1)S(1)}, u32[]{:S(2)}, u32[]{:S(2)}) collective-permute-start(bf16[24,4,1152]{2,0,1:T(8,128)(2,1)} %get-tuple-element.22), channel_id=1, source_target_pairs={{16,0},{17,1},{18,2},{19,3},{20,4},{21,5},{22,6},{23,7},{24,8},{25... | collective-permute-start | bytes 663560 | tf_op jit(solution)/shard_map/ppermute | solution.py:311
  36.6 14.6 %copy-start.5 = (bf16[4,24,1152]{2,0,1:T(4,128)(2,1)S(1)}, bf16[4,24,1152]{2,0,1:T(4,128)(2,1)}, u32[]{:S(2)}) copy-start(bf16[4,24,1152]{2,0,1:T(4,128)(2,1)} %get-tuple-element.24) | copy-start | bytes 663556
  36.6 22.2 %copy-start.6 = (bf16[24,4,1152]{2,0,1:T(8,128)(2,1)S(1)}, bf16[24,4,1152]{2,0,1:T(8,128)(2,1)}, u32[]{:S(2)}) copy-start(bf16[24,4,1152]{2,0,1:T(8,128)(2,1)} %get-tuple-element.23) | copy-start | bytes 663556
  51.2 17.3 %collective-permute-start.1 = (bf16[4,24,1152]{2,0,1:T(4,128)(2,1)S(1)}, bf16[4,24,1152]{2,0,1:T(4,128)(2,1)S(1)}, u32[]{:S(2)}, u32[]{:S(2)}) collective-permute-start(bf16[4,24,1152]{2,0,1:T(4,128)(2,1)S(1)} %copy-done.5), channel_id=1, source_target_pairs={{0,15},{1,0},{2,1},{3,2},{4,3},{5,4},{6,5},{7,6},{8,7},{9,8},{10,9... | collective-permute-start | bytes 663560 | tf_op jit(solution)/shard_map/ppermute | solution.py:311
  53.4 15.1 %collective-permute-start = (bf16[4,24,1152]{2,0,1:T(4,128)(2,1)S(1)}, bf16[4,24,1152]{2,0,1:T(4,128)(2,1)}, u32[]{:S(2)}, u32[]{:S(2)}) collective-permute-start(bf16[4,24,1152]{2,0,1:T(4,128)(2,1)S(1)} %get-tuple-element.25), channel_id=1, source_target_pairs={{0,1},{1,2},{2,3},{3,4},{4,5},{5,6},{6,7},{7,8},{8,9},{9,10},{10,1... | collective-permute-start | bytes 663560 | tf_op jit(solution)/shard_map/ppermute | solution.py:311
  58.8 9.2 %collective-permute-start.3 = (bf16[24,4,1152]{2,0,1:T(8,128)(2,1)S(1)}, bf16[24,4,1152]{2,0,1:T(8,128)(2,1)S(1)}, u32[]{:S(2)}, u32[]{:S(2)}) collective-permute-start(bf16[24,4,1152]{2,0,1:T(8,128)(2,1)S(1)} %copy-done.6), channel_id=1, source_target_pairs={{0,16},{1,17},{2,18},{3,19},{4,20},{5,21},{6,22},{7,23},{8,24},{9,... | collective-permute-start | bytes 663560 | tf_op jit(solution)/shard_map/ppermute | solution.py:311
  68.1 1.4 copy-start.10
  68.1 1.4 copy-start.9
  68.2 1.4 copy-start.8
  68.3 1.4 copy-start.7
  69.7 1.0 copy-start.11
  121.8 49.1 %collective-permute-start.8 = (bf16[64,1152]{1,0:T(8,128)(2,1)}, bf16[64,1152]{1,0:T(8,128)(2,1)}, u32[]{:S(2)}, u32[]{:S(2)}) collective-permute-start(bf16[64,1152]{1,0:T(8,128)(2,1)} %get-tuple-element.10), channel_id=1, source_target_pairs={{0,16},{1,17},{2,18},{3,19},{4,20},{5,21},{6,22},{7,23},{8,24},{9,... | collective-permute-start | bytes 442376 | tf_op jit(solution)/shard_map/ppermute | solution.py:311
  123.8 50.6 %collective-permute-start.9 = (bf16[64,1152]{1,0:T(8,128)(2,1)}, bf16[64,1152]{1,0:T(8,128)(2,1)}, u32[]{:S(2)}, u32[]{:S(2)}) collective-permute-start(bf16[64,1152]{1,0:T(8,128)(2,1)} %get-tuple-element.11), channel_id=1, source_target_pairs={{16,0},{17,1},{18,2},{19,3},{20,4},{21,5},{22,6},{23,7},{24,8},{25... | collective-permute-start | bytes 442376 | tf_op jit(solution)/shard_map/ppermute | solution.py:311
  129.2 48.5 %collective-permute-start.11 = (bf16[64,1152]{1,0:T(8,128)(2,1)}, bf16[64,1152]{1,0:T(8,128)(2,1)}, u32[]{:S(2)}, u32[]{:S(2)}) collective-permute-start(bf16[64,1152]{1,0:T(8,128)(2,1)} %get-tuple-element.13), channel_id=1, source_target_pairs={{0,31},{1,16},{2,17},{3,18},{4,19},{5,20},{6,21},{7,22},{8,23},{9,... | collective-permute-start | bytes 442376 | tf_op jit(solution)/shard_map/ppermute | solution.py:311
  131.9 49.2 %collective-permute-start.12 = (bf16[64,1152]{1,0:T(8,128)(2,1)}, bf16[64,1152]{1,0:T(8,128)(2,1)}, u32[]{:S(2)}, u32[]{:S(2)}) collective-permute-start(bf16[64,1152]{1,0:T(8,128)(2,1)} %get-tuple-element.14), channel_id=1, source_target_pairs={{16,15},{17,0},{18,1},{19,2},{20,3},{21,4},{22,5},{23,6},{24,7},{2... | collective-permute-start | bytes 442376 | tf_op jit(solution)/shard_map/ppermute | solution.py:311
  143.1 40.8 %collective-permute-start.10 = (bf16[384,1152]{1,0:T(8,128)(2,1)}, bf16[384,1152]{1,0:T(8,128)(2,1)}, u32[]{:S(2)}, u32[]{:S(2)}) collective-permute-start(bf16[384,1152]{1,0:T(8,128)(2,1)} %get-tuple-element.12), channel_id=1, source_target_pairs={{0,15},{1,0},{2,1},{3,2},{4,3},{5,4},{6,5},{7,6},{8,7},{9,8},{10,9... | collective-permute-start | bytes 2654216 | tf_op jit(solution)/shard_map/ppermute | solution.py:311
  182.8 2.4 %copy-start.2 = (f32[16,4,1152]{2,0,1:T(8,128)S(1)}, f32[16,4,1152]{2,0,1:T(8,128)}, u32[]{:S(2)}) copy-start(f32[16,4,1152]{2,0,1:T(8,128)} %copy.22) | copy-start | bytes 884740
  182.8 2.4 %copy-start.3 = (f32[16,4,1152]{2,0,1:T(8,128)S(1)}, f32[16,4,1152]{2,0,1:T(8,128)}, u32[]{:S(2)}) copy-start(f32[16,4,1152]{2,0,1:T(8,128)} %copy.23) | copy-start | bytes 884740
  182.8 2.4 %copy-start.4 = (f32[16,4,1152]{2,0,1:T(8,128)S(1)}, f32[16,4,1152]{2,0,1:T(8,128)}, u32[]{:S(2)}) copy-start(f32[16,4,1152]{2,0,1:T(8,128)} %copy.25) | copy-start | bytes 884740
Sparse Core Ops, SparseCore 0:
  25.5 53.8 all-gather.1

commit v2 on v0

v2 whole, which is shorter than its diff:
```python
import functools
import math

import jax
import jax.numpy as jnp
from jax import lax
from jax.experimental import pallas as pl
from jax.experimental.pallas import tpu as pltpu
from jax.sharding import PartitionSpec as P

HEADS = 16
PAIRS = HEADS // 2
HALO = 4
LANES = 128
WIN = 256
TEXT_PAD = 384
VMEM = 60 * 1024 * 1024
NN = (((1,), (0,)), ((), ()))
NT = (((1,), (1,)), ((), ()))
BF16, F32 = jnp.bfloat16, jnp.float32
ANY = pl.BlockSpec(memory_space=pl.ANY)
LOCAL = pl.BlockSpec(memory_space=pltpu.VMEM)


def modulation(timestep, time_weight, modulation_bias):
    half = time_weight.shape[0] // 2
    freqs = jnp.exp(-math.log(10000.0) * jnp.arange(half, dtype=F32) / half)
    angle = timestep.astype(F32)[:, None] * freqs[None, :]
    embed = jnp.concatenate([jnp.cos(angle), jnp.sin(angle)], axis=1)
    embed = jax.nn.silu(embed).astype(BF16)
    mixed = jnp.dot(embed, time_weight, preferred_element_type=F32) + modulation_bias.reshape(-1)[None, :]
    width = modulation_bias.shape[1]
    return (mixed[:, :width], mixed[:, width : 2 * width], mixed[:, 2 * width :])


def begin(pairs, sems, first):
    made = [pltpu.make_async_copy(a, b, sems.at[first + n]) for n, (a, b) in enumerate(pairs)]
    for c in made:
        c.start()
    return made


def finish_all(made):
    for c in made:
        c.wait()


def normalise(x_ref, at, count, shift_ref, scale_ref, u_ref):
    rows = 32
    gain = 1.0 + scale_ref[...]
    shift = shift_ref[...]

    def norm(i, carry):
        x = x_ref[pl.ds(pl.multiple_of(at + i * rows, rows), rows), :].astype(F32)
        mean = jnp.mean(x, axis=-1, keepdims=True)
        centred = x - mean
        var = jnp.mean(centred * centred, axis=-1, keepdims=True)
        normed = centred * lax.rsqrt(var + 1e-06)
        u_ref[pl.ds(pl.multiple_of(i * rows, rows), rows), :] = (normed * gain + shift).astype(BF16)
        return carry

    lax.fori_loop(0, count // rows, norm, 0, unroll=2)


def column_parts(total, size):
    return [(c, min(size, total - c)) for c in range(0, total, size)]


def weight_pairs(w_hbm, w_s, size):
    return [
        (w_hbm.at[:, pl.ds(c, n)], w_s.at[:, pl.ds(c, n)]) for c, n in column_parts(w_hbm.shape[1], size)
    ]


def project_qkv(u_ref, w_s, waits, size, width, q_factor, out_ref, at):
    count = u_ref.shape[0]
    for wait, (c, n) in zip(waits, column_parts(w_s.shape[1], size)):
        wait.wait()
        made = jnp.dot(u_ref[...], w_s[:, c : c + n], preferred_element_type=F32)
        if c < width:
            ids = lax.broadcasted_iota(jnp.int32, (1, n), 1)
            made = made * jnp.where(ids < width - c, q_factor, 1.0)
        out_ref[at : at + count, c : c + n] = made.astype(BF16)


def band(low, high, dims, axis):
    ids = lax.broadcasted_iota(jnp.int32, dims, axis)
    return ((ids >= low) & (ids < high)).astype(F32).astype(BF16)


def pair_start(t):
    return pl.multiple_of(t * LANES, LANES)


def spare_columns(t, channels):
    gap = 2 * channels - LANES
    return jnp.where(t * gap + 2 * channels <= WIN - 64, WIN - 64, 0)


def pairs_unshifted(channels, q_ref, scores, values, p_refs, bad_ref, rows, out_ref):
    count = q_ref.shape[0]
    parts = [slice(c, c + rows) for c in range(0, count, rows)]
    gap = 2 * channels - LANES

    def close(t, p_ref, v, part):
        spare = spare_columns(t, channels)
        o = lax.dot_general(p_ref[part, :], v[0], v[1], preferred_element_type=F32)
        ids = lax.broadcasted_iota(jnp.int32, (1, WIN), 1)
        sum_a = jnp.max(jnp.where((ids >= spare) & (ids < spare + 32), o, 0.0), axis=-1, keepdims=True)
        sum_b = jnp.max(jnp.where((ids >= spare + 32) & (ids < spare + 64), o, 0.0), axis=-1, keepdims=True)
        low, high = 2.0**-100, 2.0**100
        good = (sum_a >= low) & (sum_a <= high) & (sum_b >= low) & (sum_b <= high)
        bad_ref[...] = jnp.maximum(bad_ref[...], jnp.max(jnp.where(good, 0.0, 1.0), axis=0, keepdims=True))
        start = gap * t
        scale = jnp.where(ids < start + channels, 1.0 / sum_a, 1.0 / sum_b)
        cols = pl.ds(pair_start(t), WIN)
        old = out_ref[part, cols].astype(F32)
        inside = (ids >= start) & (ids < start + 2 * channels)
        out_ref[part, cols] = jnp.where(inside, o * scale, old).astype(BF16)

    def both(t, now, after):
        v = values(t, gap * t)
        for part in parts:
            scores(t + 1, gap * (t + 1), part, after)
            close(t, now, v, part)

    first, second = p_refs
    bad_ref[...] = jnp.zeros_like(bad_ref)
    for part in parts:
        scores(jnp.int32(0), jnp.int32(0), part, first)

    def step(i, carry):
        both(2 * i, first, second)
        both(2 * i + 1, second, first)
        return carry

    lax.fori_loop(0, PAIRS // 2 - 1, step, 0)
    both(jnp.int32(PAIRS - 2), first, second)
    v = values(jnp.int32(PAIRS - 1), jnp.int32(gap * (PAIRS - 1)))
    for part in parts:
        close(jnp.int32(PAIRS - 1), second, v, part)


def heads_shifted(channels, q_ref, keys, key_dims, values, value_dims, valid, out_ref):
    count, width = q_ref.shape
    rows = 64

    def one(n, carry):
        h = n // (count // rows)
        part = pl.ds(pl.multiple_of((n % (count // rows)) * rows, rows), rows)
        t = jnp.minimum((h * channels) // LANES, (width - WIN) // LANES)
        start = pair_start(t)
        offset = h * channels - start
        cols = pl.ds(start, WIN)
        q = q_ref[part, cols] * band(offset, offset + channels, (1, WIN), 1)
        s = lax.dot_general(q, keys(start), key_dims, preferred_element_type=F32)
        if valid < s.shape[1]:
            s = jnp.where(lax.broadcasted_iota(jnp.int32, s.shape, 1) < valid, s, -jnp.inf)
        p = jnp.exp2(s - jnp.max(s, axis=-1, keepdims=True))
        total = jnp.sum(p, axis=-1, keepdims=True)
        o = lax.dot_general(p.astype(BF16), values(start), value_dims, preferred_element_type=F32) / total
        ids = lax.broadcasted_iota(jnp.int32, (1, WIN), 1)
        old = out_ref[part, cols].astype(F32)
        inside = (ids >= offset) & (ids < offset + channels)
        out_ref[part, cols] = jnp.where(inside, o, old).astype(BF16)
        return carry

    lax.fori_loop(0, HEADS * (count // rows), one, 0)


def attend_self(channels, q_ref, k_ref, v_ref, vv_ref, p_refs, bad_ref, rows, out_ref):
    n = k_ref.shape[0]

    def scores(t, start, part, p_ref):
        cols = pl.ds(pair_start(t), WIN)
        q = q_ref[part, cols]
        for j in range(2):
            low = start + j * channels
            s = lax.dot_general(
                q * band(low, low + channels, (1, WIN), 1), k_ref[:, cols], NT, preferred_element_type=F32
            )
            p_ref[part, j * n : (j + 1) * n] = jnp.exp2(s).astype(BF16)

    def values(t, start):
        v = v_ref[:, pl.ds(pair_start(t), WIN)]
        spare = spare_columns(t, channels)
        for j in range(2):
            low, mark = start + j * channels, spare + 32 * j
            vv_ref[j * n : (j + 1) * n, :] = v * band(low, low + channels, (1, WIN), 1) + band(
                mark, mark + 32, (1, WIN), 1
            )
        return vv_ref[...], NN

    out_ref[...] = jnp.zeros_like(out_ref)
    pairs_unshifted(channels, q_ref, scores, values, p_refs, bad_ref, rows, out_ref)

    @pl.when(jnp.max(bad_ref[...]) > 0.0)
    def _():
        heads_shifted(
            channels,
            q_ref,
            lambda start: k_ref[:, pl.ds(start, WIN)],
            NT,
            lambda start: v_ref[:, pl.ds(start, WIN)],
            NN,
            n,
            out_ref,
        )


def attend_text(channels, text, q_ref, kv_ref, p_refs, bad_ref, rows, out_ref):
    n = kv_ref.shape[2]

    def scores(t, start, part, p_ref):
        k = kv_ref[0, pl.ds(pair_start(t), WIN), :]
        pair = [
            k * band(start + j * channels, start + (j + 1) * channels, (WIN, 1), 0) for j in range(2)
        ]
        s = lax.dot_general(
            q_ref[part, pl.ds(pair_start(t), WIN)],
            jnp.concatenate(pair, axis=1),
            NN,
            preferred_element_type=F32,
        )
        p_ref[part, :] = jnp.exp2(s).astype(BF16)

    def values(t, start):
        v = kv_ref[1, pl.ds(pair_start(t), WIN), :]
        valid = band(0, text, (1, n), 1)
        spare = spare_columns(t, channels)
        pair = [
            v * band(start + j * channels, start + (j + 1) * channels, (WIN, 1), 0)
            + band(spare + 32 * j, spare + 32 * j + 32, (WIN, 1), 0) * valid
            for j in range(2)
        ]
        return jnp.concatenate(pair, axis=1), NT

    out_ref[...] = jnp.zeros_like(out_ref)
    pairs_unshifted(channels, q_ref, scores, values, p_refs, bad_ref, rows, out_ref)

    @pl.when(jnp.max(bad_ref[...]) > 0.0)
    def _():
        heads_shifted(
            channels,
            q_ref,
            lambda start: kv_ref[0, pl.ds(start, WIN), :],
            NN,
            lambda start: kv_ref[1, pl.ds(start, WIN), :],
            NT,
            text,
            out_ref,
        )


QKV_PART = 512


def core_kernel(q_factor, x_ref, shift_ref, scale_ref, w_hbm, out_ref, u_s, w_s, sems):
    waits = begin(weight_pairs(w_hbm, w_s, QKV_PART), sems, 0)
    count, width = x_ref.shape
    normalise(x_ref, 0, count, shift_ref, scale_ref, u_s)
    project_qkv(u_s, w_s, waits, QKV_PART, width, q_factor, out_ref, 0)


def core_qkv(q_factor, x, shift, scale, weight):
    count, width = x.shape
    total = weight.shape[1]
    return pl.pallas_call(
        functools.partial(core_kernel, q_factor),
        out_shape=jax.ShapeDtypeStruct((count, total), BF16),
        in_specs=[LOCAL, LOCAL, LOCAL, ANY],
        out_specs=LOCAL,
        scratch_shapes=[
            pltpu.VMEM((count, width), BF16),
            pltpu.VMEM((width, total), BF16),
            pltpu.SemaphoreType.DMA((8,)),
        ],
        compiler_params=pltpu.CompilerParams(vmem_limit_bytes=VMEM),
        cost_estimate=pl.CostEstimate(
            flops=2 * count * width * total,
            bytes_accessed=2 * (width * total + count * (width + total)),
            transcendentals=0,
        ),
    )(x, shift, scale, weight)


def regroup(core, rim, source_ref, target_ref):
    half = core // 2
    inner = core * core
    side = core * rim
    edge = side + 2 * rim * rim
    at = 0

    def take(*pieces):
        nonlocal at
        for start, n in pieces:
            target_ref[at : at + n, :] = source_ref[start : start + n, :]
            at += n

    for r in range(core):
        take((inner + rim * r, rim), (core * r, half))
    for base in (inner + 2 * side, inner + 2 * side + edge):
        for a in range(rim):
            take((base + rim * a, rim), (base + rim * rim + core * a, half))
    for base in (inner + 2 * side, inner + 2 * side + edge):
        for a in range(rim):
            take((base + rim * rim + core * a + half, half), (base + rim * rim + side + rim * a, rim))
    for r in range(core):
        take((core * r + half, half), (inner + side + rim * r, rim))


def tile_kernel(
    core,
    rim,
    rows,
    q_factor,
    x_core,
    left,
    right,
    top,
    bottom,
    qkv_core,
    shift_ref,
    scale_ref,
    gate_ref,
    w_hbm,
    wo_hbm,
    wq_hbm,
    h1_out,
    cq_out,
    x_s,
    qkv_s,
    u_s,
    w_s,
    wo_s,
    wq_s,
    vv_s,
    p_a,
    p_b,
    attn_s,
    h1_s,
    hg_s,
    bad_s,
    sems,
):
    width = x_core.shape[1]
    channels = width // HEADS
    inner = x_core.shape[0]
    outer = sum(a.shape[0] for a in (left, right, top, bottom))
    total = inner + outer
    pairs, at = [], inner
    for part in (left, right, top, bottom):
        pairs.append((part, x_s.at[pl.ds(at, part.shape[0])]))
        at += part.shape[0]
    waits_x = begin(pairs, sems, 0)
    waits_w = begin(weight_pairs(w_hbm, w_s, QKV_PART), sems, 4)
    waits_qkv = begin([(qkv_core, qkv_s.at[pl.ds(0, inner)])], sems, 12)
    waits_later = begin([(x_core, x_s.at[pl.ds(0, inner)]), (wo_hbm, wo_s), (wq_hbm, wq_s)], sems, 13)
    finish_all(waits_x)
    normalise(x_s, inner, outer, shift_ref, scale_ref, u_s)
    project_qkv(u_s, w_s, waits_w, QKV_PART, width, q_factor, qkv_s, inner)
    finish_all(waits_qkv)
    attend_self(
        channels,
        qkv_s.at[:, pl.ds(0, width)],
        qkv_s.at[:, pl.ds(width, width)],
        qkv_s.at[:, pl.ds(2 * width, width)],
        vv_s,
        (p_a, p_b),
        bad_s,
        rows,
        attn_s,
    )
    finish_all(waits_later)
    step = total // 2
    for r in range(0, total, step):
        part = slice(r, r + step)
        mixed = jnp.dot(attn_s[part, :], wo_s[...], preferred_element_type=F32)
        h1_s[part, :] = x_s[part, :].astype(F32) + gate_ref[...] * mixed
    regroup(core, rim, h1_s, hg_s)
    waits_h = begin([(hg_s, h1_out)], sems, 16)
    for r in range(0, total, step):
        part = slice(r, r + step)
        made = jnp.dot(hg_s[part, :].astype(BF16), wq_s[...], preferred_element_type=F32)
        attn_s[part, :] = (made * q_factor).astype(BF16)
        waits_h += begin([(attn_s.at[pl.ds(r, step)], cq_out.at[pl.ds(r, step)])], sems, 17 + r // step)
    finish_all(waits_h)


def tile_self(core, rim, q_factor, x_core, rims, qkv_core, mod, qkv_weight, out_weight, cross_q):
    inner, width = x_core.shape
    outer = sum(a.shape[0] for a in rims)
    total = inner + outer
    wide = qkv_weight.shape[1]
    return pl.pallas_call(
        functools.partial(tile_kernel, core, rim, 512, q_factor),
        out_shape=[
            jax.ShapeDtypeStruct((total, width), F32),
            jax.ShapeDtypeStruct((total, width), BF16),
        ],
        in_specs=[ANY] * 6 + [LOCAL] * 3 + [ANY] * 3,
        out_specs=[ANY, ANY],
        scratch_shapes=[
            pltpu.VMEM((total, width), BF16),
            pltpu.VMEM((total, wide), BF16),
            pltpu.VMEM((outer, width), BF16),
            pltpu.VMEM((width, wide), BF16),
            pltpu.VMEM((width, width), BF16),
            pltpu.VMEM((width, width), BF16),
            pltpu.VMEM((2 * total, WIN), BF16),
            pltpu.VMEM((total, 2 * total), BF16),
            pltpu.VMEM((total, 2 * total), BF16),
            pltpu.VMEM((total, width), BF16),
            pltpu.VMEM((total, width), F32),
            pltpu.VMEM((total, width), F32),
            pltpu.VMEM((1, LANES), F32),
            pltpu.SemaphoreType.DMA((20,)),
        ],
        compiler_params=pltpu.CompilerParams(vmem_limit_bytes=VMEM),
        cost_estimate=pl.CostEstimate(
            flops=2 * outer * width * wide + 16 * total * width * total + 4 * total * width * width,
            bytes_accessed=2 * width * (wide + 2 * width) + 2 * inner * wide + 6 * total * width,
            transcendentals=HEADS * total * total,
        ),
    )(x_core, *rims, qkv_core, *mod, qkv_weight, out_weight, cross_q)


def text_kernel(text, first, parts, rows, column_ref, h1, cq, t0, t1, t2, t3, wc_hbm, *rest):
    outs = rest[: len(parts)]
    q_s, h_s, kv_s, wc_s, p_a, p_b, attn_s, bad_s, sems = rest[len(parts) :]
    count, width = q_s.shape
    waits = begin([(cq.at[pl.ds(first, count)], q_s)], sems, 0)
    pairs = []
    for k, arrived in enumerate((t0, t1, t2, t3)):
        size = arrived.shape[1]
        where = pl.multiple_of(lax.rem(column_ref[0] + k, 4) * size, size)
        for j in range(2):
            pairs.append((arrived.at[j], kv_s.at[j, pl.ds(where, size), :]))
    waits += begin(pairs, sems, 1)
    waits_later = begin([(wc_hbm, wc_s), (h1.at[pl.ds(first, count)], h_s)], sems, 9)
    finish_all(waits)
    attend_text(width // HEADS, text, q_s, kv_s, (p_a, p_b), bad_s, rows, attn_s)
    finish_all(waits_later)
    at = 0
    for out, n in zip(outs, parts):
        at_end = at + n
        made = jnp.dot(attn_s[at:at_end, :], wc_s[...], preferred_element_type=F32)
        out[...] = (h_s[at:at_end, :] + made).astype(BF16)
        at = at_end


def tile_text(text, first, parts, column, h1, cq, arrived, weight):
    count = sum(parts)
    width = h1.shape[1]
    padded = arrived[0].shape[2]
    return pl.pallas_call(
        functools.partial(text_kernel, text, first, parts, count),
        out_shape=[jax.ShapeDtypeStruct((n, width), BF16) for n in parts],
        in_specs=[pl.BlockSpec(memory_space=pltpu.SMEM)] + [ANY] * 7,
        out_specs=[LOCAL] * len(parts),
        scratch_shapes=[
            pltpu.VMEM((count, width), BF16),
            pltpu.VMEM((count, width), F32),
            pltpu.VMEM((2, width, padded), BF16),
            pltpu.VMEM((width, width), BF16),
            pltpu.VMEM((count, 2 * padded), BF16),
            pltpu.VMEM((count, 2 * padded), BF16),
            pltpu.VMEM((count, width), BF16),
            pltpu.VMEM((1, LANES), F32),
            pltpu.SemaphoreType.DMA((11,)),
        ],
        compiler_params=pltpu.CompilerParams(vmem_limit_bytes=VMEM),
        cost_estimate=pl.CostEstimate(
            flops=16 * count * width * padded + 2 * count * width * width,
            bytes_accessed=2 * width * (width + 2 * padded) + 8 * count * width,
            transcendentals=HEADS * count * padded,
        ),
    )(column, h1, cq, *arrived, weight)


def merge_kernel(lat_count, lat_ref, near, far, dn_near, dn_far, up_near, up_far, out_ref):
    step = pl.program_id(0)
    last = pl.num_programs(0) - 1
    lat = lat_ref[0]
    low = jnp.where(step == 0, 1.0, 0.0)
    high = jnp.where(step == last, 1.0, 0.0)
    shared = ((step == 0) & (lat > 0)) | ((step == last) & (lat < lat_count - 1))
    scale = jnp.where(shared, 0.5, 1.0)

    def total(body, dn, up):
        return (body[...].astype(F32) + low * dn[...].astype(F32) + high * up[...].astype(F32)) * scale

    a, b = total(near, dn_near, up_near), total(far, dn_far, up_far)
    out_ref[...] = jnp.concatenate([a[:, :8], (a[:, 8:] + b[:, :8]) * 0.5, b[:, 8:]], axis=1).astype(BF16)


def merge(lat_count, lat, core, rim, near, far, down, down_left, up, up_left):
    span, width = near.shape[1:]
    whole = pl.BlockSpec((rim, span, width), lambda i: (0, 0, 0))
    rows = pl.BlockSpec((rim, span, width), lambda i: (i, 0, 0))
    return pl.pallas_call(
        functools.partial(merge_kernel, lat_count),
        out_shape=jax.ShapeDtypeStruct((core, core, width), BF16),
        grid=(core // rim,),
        in_specs=[pl.BlockSpec(memory_space=pltpu.SMEM), rows, rows, whole, whole, whole, whole],
        out_specs=pl.BlockSpec((rim, core, width), lambda i: (i, 0, 0)),
        cost_estimate=pl.CostEstimate(
            flops=4 * core * core * width, bytes_accessed=8 * core * core * width, transcendentals=0
        ),
    )(lat, near, far, down, down_left, up, up_left)


def send(value, mesh_sizes, down, right):
    rows, cols = mesh_sizes
    pairs = [
        (r * cols + c, (r + down) * cols + (c + right) % cols)
        for r in range(rows)
        for c in range(cols)
        if 0 <= r + down < rows
    ]
    return lax.ppermute(value, ("lat", "lon"), pairs)


def local(
    sizes,
    hidden,
    timestep,
    context,
    time_weight,
    modulation_bias,
    qkv_weight,
    out_weight,
    cross_q,
    cross_kv,
    cross_output_projection,
):
    core, width = hidden.shape[1], hidden.shape[3]
    half = core // 2
    rim = HALO
    text = context.shape[1]
    lon_count = sizes[1]
    lon = lax.axis_index("lon")
    to = functools.partial(send, mesh_sizes=sizes)
    q_factor = math.log2(math.e) / math.sqrt(width // HEADS)

    def among(value, partner):
        return lax.ppermute(value, "lon", [(partner(i), i) for i in range(lon_count)])

    padded = jnp.pad(context[0], ((0, TEXT_PAD - text), (0, 0)))
    own_head = jnp.einsum("td,sde->set", padded, cross_kv, preferred_element_type=F32).astype(BF16)
    x = hidden[0]
    x, own_head = lax.optimization_barrier((x, own_head))
    other = among(own_head, lambda i: i ^ 1)
    left = to(x[:, core - rim :].reshape(-1, width), down=0, right=1)
    right = to(x[:, :rim].reshape(-1, width), down=0, right=-1)

    def joined(bit, mine, theirs):
        low = (lon // bit) % 2 == 0
        return jnp.concatenate([jnp.where(low, mine, theirs), jnp.where(low, theirs, mine)], axis=1)

    two = joined(1, own_head, other)
    four = joined(2, two, among(two, lambda i: i ^ 2))
    arrived = [four] + [among(four, lambda i, k=k: (i + 4 * k) % lon_count) for k in (1, 2, 3)]
    column = (lon // 4).astype(jnp.int32)[None]

    shift, scale, gate = modulation(timestep, time_weight, modulation_bias)
    x_core = x.reshape(core * core, width)
    qkv_core = core_qkv(q_factor, x_core, shift, scale, qkv_weight)

    corner = rim * rim
    low_edge = jnp.concatenate([left[-corner:], x[core - rim :].reshape(-1, width), right[-corner:]], axis=0)
    high_edge = jnp.concatenate([left[:corner], x[:rim].reshape(-1, width), right[:corner]], axis=0)
    top = to(low_edge, down=1, right=0)
    bottom = to(high_edge, down=-1, right=0)

    h1, cq = tile_self(
        core,
        rim,
        q_factor,
        x_core,
        (left, right, top, bottom),
        qkv_core,
        (shift, scale, gate),
        qkv_weight,
        out_weight,
        cross_q,
    )
    span = half + rim
    block, edge = core * span, rim * span
    main, top_left, bottom_left, top_right, bottom_right = tile_text(
        text, 0, (block, edge, edge, edge, edge), column, h1, cq, arrived, cross_output_projection
    )
    far = to(main, down=0, right=-1)
    up_left = to(top_left, down=-1, right=-1)
    down_left = to(bottom_left, down=1, right=-1)
    up = to(top_right, down=-1, right=0)
    down = to(bottom_right, down=1, right=0)
    (near,) = tile_text(
        text, block + 4 * edge, (block,), column, h1, cq, arrived, cross_output_projection
    )
    shape = lambda a: a.reshape(-1, span, width)
    lat = lax.axis_index("lat").astype(jnp.int32)[None]
    out = merge(
        sizes[0], lat, core, rim, *(shape(a) for a in (near, far, down, down_left, up, up_left))
    )
    return out[None]


def solution(mesh):
    in_specs = (
        P(None, "lat", "lon", None),
        P(),
        P(),
        P(),
        P(),
        P(),
        P(),
        P(),
        P(None, None, "lon"),
        P(),
    )
    out_specs = P(None, "lat", "lon", None)
    sizes = (mesh.shape["lat"], mesh.shape["lon"])
    return jax.shard_map(
        functools.partial(local, sizes), mesh=mesh, in_specs=in_specs, out_specs=out_specs, check_vma=False
    )
```

time: 295 us -> 130 us (0.44)
  matrix products: 152 us -> 2.11 us
  Pallas kernels: 0 us -> 77.7 us
  waiting for transfers between devices: 36.9 us -> 1.81 us
  local copies, waits for them, and re-layouts: 42.2 us -> 7.47 us
  other arithmetic: 24.8 us -> 1.86 us
  starting transfers between devices: 21.2 us -> 37.3 us
  between operations: 14.4 us -> 1.04 us
    dot_general x70 -> x1, matrix products: 152 us -> 0.36 us  [modulation(): jnp.dot(embed, time_weight, preferred_element_type=F32)]
    pallas_call x0 -> x5, Pallas kernels: none -> 77.7 us  [the longest x1 38 us: tile_self(): pl.pallas_call(functools.partial(tile_kernel, core, rim, 512, q_factor),...]
    ppermute x9 -> x14, waiting for transfers between devices: 36.9 us -> 1.81 us  [the longest x9 1.8 us: send(): return lax.ppermute(value, ('lat', 'lon'), pairs)]
    slice x15 -> x5, local copies, waits for them, and re-layouts: 23.2 us -> 2.4 us  [the longest x1 0.79 us: local(): left[:corner]]
    reduce_sum x34 -> x0, other arithmetic: 19.9 us -> none  [the longest x32 14.9 us: one_head(): jax.nn.softmax(logit_scores, axis=-1).astype(jnp.bfloat16)]
    ppermute x9 -> x14, starting transfers between devices: 21.2 us -> 37.3 us  [the longest x9 30 us: send(): return lax.ppermute(value, ('lat', 'lon'), pairs)]
    another operation x4 -> x0, local copies, waits for them, and re-layouts: 7.3 us -> none
    convert_element_type x2 -> x1, local copies, waits for them, and re-layouts: 4.83 us -> 0.01 us  [modulation(): embed = jax.nn.silu(embed).astype(BF16)]
  transfers between devices with their start and end apart: 10 -> 14, of which waited for: 5 -> 2; matrix products, arithmetic and copies ran while one was open for 48% -> 4% of each run, Pallas kernels for 0% -> 46%
where the time goes in v2:
time: 130 us; the launch traced here: 129 us
  Pallas kernels  77.7 us (60%)
  starting transfers between devices  37.3 us (29%)
  local copies, waits for them, and re-layouts  7.47 us (6%)
  matrix products  2.11 us (2%)
  other arithmetic  1.86 us (1%)
  waiting for transfers between devices  1.81 us (1%)
    pallas_call x1, Pallas kernels, tile_self(): pl.pallas_call(functools.partial(tile_kernel, core, rim, 512, q_factor),...  38 us
    ppermute x9, starting transfers between devices, send(): return lax.ppermute(value, ('lat', 'lon'), pairs)  30 us
    pallas_call x2, Pallas kernels, tile_text(): pl.pallas_call(functools.partial(text_kernel, text, first, parts, count),...  22.4 us
    pallas_call x1, Pallas kernels, core_qkv(): pl.pallas_call(functools.partial(core_kernel, q_factor), out_shape=jax.Sh...  12 us
    ppermute x5, starting transfers between devices, among(): lax.ppermute(value, 'lon', [(partner(i), i) for i in range(lon_count)])  7.28 us
    pallas_call x1, Pallas kernels, merge(): pl.pallas_call(functools.partial(merge_kernel, lat_count), out_shape=jax....  5.28 us
    unnamed x28, local copies, waits for them, and re-layouts  2.83 us
  transfers between devices with their start and end apart: 14, of which 2 were waited for; matrix products, arithmetic and copies ran while one was open for 4% of the time, Pallas kernels for 46%

profile of v2, /device:TPU:33, one launch (start us, length us, event | category | flops | bytes accessed | tf_op | source)
XLA Modules:
  0.0 129.3 jit_solution(5498903384644523208)
XLA Ops:
  0.0 1.8 %fusion = f32[384,144]{0,1:S(1)} fusion(bf16[1152,144]{0,1:T(8,128)(2,1)} %bitcast.34, bf16[300,1152]{1,0:T(8,128)(2,1)} %bitcast.29), kind=kOutput, calls=%fused_computation.1 | convolution fusion | flops 127401984 | bytes 1244160
  1.8 0.7 convert_bitcast_fusion
  2.4 0.2 fusion.7
  2.6 0.7 reshape.68
  3.3 3.3 %collective-permute-start = (bf16[96,1152]{1,0:T(8,128)(2,1)}, bf16[96,1152]{1,0:T(8,128)(2,1)}, u32[]{:S(2)}, u32[]{:S(2)}) collective-permute-start(bf16[96,1152]{1,0:T(8,128)(2,1)} %reshape.68), channel_id=1, source_target_pairs={{0,1},{1,2},{2,3},{3,4},{4,5},{5,6},{6,7},{7,8},{8,9},{9,10},{10,1... | collective-permute-start | bytes 663560 | tf_op jit(solution)/shard_map/ppermute | solution.py:521
  6.6 0.7 reshape.69
  7.3 0.0 collective-permute-start.1
  7.3 2.8 %collective-permute-start.4 = (bf16[2,72,384]{2,1,0:T(8,128)(2,1)}, bf16[2,72,384]{2,1,0:T(8,128)(2,1)}, u32[]{:S(2)}, u32[]{:S(2)}) collective-permute-start(bf16[2,72,384]{2,1,0:T(8,128)(2,1)} %convert_bitcast_fusion), channel_id=1, source_target_pairs={{1,0},{0,1},{3,2},{2,3},{5,4},{4,5},{7,6},{6,7},{9,8},{8,9},{11,10... | collective-permute-start | bytes 331784 | tf_op jit(solution)/shard_map/ppermute | solution.py:547
  10.9 0.7 broadcast_in_dim_reshape.3
  11.6 0.4 convolution_reduce_fusion
  12.0 0.6 fusion.10
  12.6 12.0 %shard_map.100.qkv_core = bf16[576,3456]{1,0:T(8,128)(2,1)} custom-call(bf16[576,1152]{1,0:T(8,128)(2,1)} %bitcast.30, f32[1,1152]{1,0:T(1,128)} %get-tuple-element.37.shift_ref, f32[1,1152]{1,0:T(1,128)} %get-tuple-element.36.scale_ref, bf16[1152,3456]{1,0:T(8,128)(2,1)} %w_hbm.3), custom_call_target="tpu_custom_call" | custom-call | flops 4586471424 | bytes 13271040 | tf_op jit(solution)/shard_map/pallas_call | solution.py:268
  24.7 0.0 collective-permute-done.4
  24.7 0.9 broadcast_select_fusion.3
  25.7 0.7 collective-permute-start.5
  26.3 0.8 fusion.9
  27.1 0.8 fusion.8
  28.0 3.1 %collective-permute-start.2 = (bf16[128,1152]{1,0:T(8,128)(2,1)S(1)}, bf16[128,1152]{1,0:T(8,128)(2,1)S(1)}, u32[]{:S(2)}, u32[]{:S(2)}) collective-permute-start(bf16[128,1152]{1,0:T(8,128)(2,1)S(1)} %pad_maximum_fusion.1), channel_id=1, source_target_pairs={{0,16},{1,17},{2,18},{3,19},{4,20},{5,21},{6,22},{7,23},{8,24},{9,... | collective-permute-start | bytes 884744 | tf_op jit(solution)/shard_map/ppermute | solution.py:521
  31.1 4.3 %collective-permute-start.3 = (bf16[128,1152]{1,0:T(8,128)(2,1)S(1)}, bf16[128,1152]{1,0:T(8,128)(2,1)S(1)}, u32[]{:S(2)}, u32[]{:S(2)}) collective-permute-start(bf16[128,1152]{1,0:T(8,128)(2,1)S(1)} %pad_maximum_fusion.2), channel_id=1, source_target_pairs={{16,0},{17,1},{18,2},{19,3},{20,4},{21,5},{22,6},{23,7},{24,8},{25... | collective-permute-start | bytes 884744 | tf_op jit(solution)/shard_map/ppermute | solution.py:521
  35.4 0.1 broadcast_select_fusion.1
  35.6 2.8 %collective-permute-start.6 = (bf16[2,288,384]{2,1,0:T(8,128)(2,1)S(1)}, bf16[2,288,384]{2,1,0:T(8,128)(2,1)S(1)}, u32[]{:S(2)}, u32[]{:S(2)}) collective-permute-start(bf16[2,288,384]{2,1,0:T(8,128)(2,1)S(1)} %pad_maximum_fusion.t0), channel_id=1, source_target_pairs={{4,0},{5,1},{6,2},{7,3},{8,4},{9,5},{10,6},{11,7},{12,8},{13,9},{1... | collective-permute-start | bytes 1327112 | tf_op jit(solution)/shard_map/ppermute | solution.py:547
  38.4 0.4 collective-permute-start.7
  38.7 0.7 collective-permute-start.8
  39.4 0.9 collective-permute-done.2.top
  40.3 0.9 collective-permute-done.3.bottom
  41.2 0.7 copy-done.13
  41.9 38.0 %shard_map.101 = (f32[1024,1152]{1,0:T(8,128)}, bf16[1024,1152]{1,0:T(8,128)(2,1)}) custom-call(bf16[576,1152]{1,0:T(8,128)(2,1)} %bitcast.31, bf16[96,1152]{1,0:T(8,128)(2,1)} %collective-permute-done.left, bf16[96,1152]{1,0:T(8,128)(2,1)} %collective-permute-done.1.right, bf16[128,1152]{1,0:T(8,128)(2,1)} %copy-done.12, bf16[128,1152]{1,0:T(8,128)(2,1)} %copy-done.13, ...), custom_call_target="tpu_custom_call" | custom-call | flops 28330426368 | bytes 24330240 | tf_op jit(solution)/shard_map/pallas_call | solution.py:395
  79.9 0.0 collective-permute-done.7.t2
  79.9 0.0 collective-permute-done.8.t3
  80.0 0.7 copy-done.9
  80.7 0.1 copy-done.10
  80.8 0.2 copy-done.11
  81.0 13.2 %shard_map.103 = (bf16[384,1152]{1,0:T(8,128)(2,1)}, bf16[64,1152]{1,0:T(8,128)(2,1)}, bf16[64,1152]{1,0:T(8,128)(2,1)}, bf16[64,1152]{1,0:T(8,128)(2,1)}, bf16[64,1152]{1,0:T(8,128)(2,1)}) custom-call(s32[1]{0:T(128)} %bitcast.1.column_ref, f32[1024,1152]{1,0:T(8,128)} %get-tuple-element.15.h1, bf16[1024,1152]{1,0:T(8,128)(2,1)} %get-tuple-element.16.cq, ...), custom_call_target="tpu_custom_call" | custom-call | flops 6228541440 | bytes 10321920 | tf_op jit(solution)/shard_map/pallas_call | solution.py:456
  94.2 1.5 %collective-permute-start.9 = (bf16[384,1152]{1,0:T(8,128)(2,1)}, bf16[384,1152]{1,0:T(8,128)(2,1)S(1)}, u32[]{:S(2)}, u32[]{:S(2)}) collective-permute-start(bf16[384,1152]{1,0:T(8,128)(2,1)} %get-tuple-element.18), channel_id=1, source_target_pairs={{0,15},{1,0},{2,1},{3,2},{4,3},{5,4},{6,5},{7,6},{8,7},{9,8},{10,9... | collective-permute-start | bytes 2654216 | tf_op jit(solution)/shard_map/ppermute | solution.py:521
  95.6 2.9 %collective-permute-start.10 = (bf16[64,1152]{1,0:T(8,128)(2,1)}, bf16[64,1152]{1,0:T(8,128)(2,1)S(1)}, u32[]{:S(2)}, u32[]{:S(2)}) collective-permute-start(bf16[64,1152]{1,0:T(8,128)(2,1)} %get-tuple-element.19), channel_id=1, source_target_pairs={{0,16},{1,17},{2,18},{3,19},{4,20},{5,21},{6,22},{7,23},{8,24},{9,... | collective-permute-start | bytes 442376 | tf_op jit(solution)/shard_map/ppermute | solution.py:521
  98.6 5.6 %collective-permute-start.11 = (bf16[64,1152]{1,0:T(8,128)(2,1)}, bf16[64,1152]{1,0:T(8,128)(2,1)S(1)}, u32[]{:S(2)}, u32[]{:S(2)}) collective-permute-start(bf16[64,1152]{1,0:T(8,128)(2,1)} %get-tuple-element.20), channel_id=1, source_target_pairs={{0,31},{1,16},{2,17},{3,18},{4,19},{5,20},{6,21},{7,22},{8,23},{9,... | collective-permute-start | bytes 442376 | tf_op jit(solution)/shard_map/ppermute | solution.py:521
  104.2 4.6 %collective-permute-start.12 = (bf16[64,1152]{1,0:T(8,128)(2,1)}, bf16[64,1152]{1,0:T(8,128)(2,1)S(1)}, u32[]{:S(2)}, u32[]{:S(2)}) collective-permute-start(bf16[64,1152]{1,0:T(8,128)(2,1)} %get-tuple-element.21), channel_id=1, source_target_pairs={{16,0},{17,1},{18,2},{19,3},{20,4},{21,5},{22,6},{23,7},{24,8},{25... | collective-permute-start | bytes 442376 | tf_op jit(solution)/shard_map/ppermute | solution.py:521
  108.8 4.8 %collective-permute-start.13 = (bf16[64,1152]{1,0:T(8,128)(2,1)}, bf16[64,1152]{1,0:T(8,128)(2,1)S(1)}, u32[]{:S(2)}, u32[]{:S(2)}) collective-permute-start(bf16[64,1152]{1,0:T(8,128)(2,1)} %get-tuple-element.22), channel_id=1, source_target_pairs={{16,15},{17,0},{18,1},{19,2},{20,3},{21,4},{22,5},{23,6},{24,7},{2... | collective-permute-start | bytes 442376 | tf_op jit(solution)/shard_map/ppermute | solution.py:521
  113.6 9.3 %shard_map.102 = bf16[384,1152]{1,0:T(8,128)(2,1)} custom-call(s32[1]{0:T(128)} %bitcast.1.column_ref, f32[1024,1152]{1,0:T(8,128)} %get-tuple-element.15.h1, bf16[1024,1152]{1,0:T(8,128)(2,1)} %get-tuple-element.16.cq, bf16[2,288,384]{2,1,0:T(8,128)(2,1)} %copy-done.3, bf16[2,288,384]{2,1,0:T(8,128)(2,1)} %copy-done.9, bf16[2,288,384]{2,1,0:T(8,128)(2,1)} %copy-done.10, ...), custom_call_target="tpu_custom_call" | custom-call | flops 3737124864 | bytes 7962624 | tf_op jit(solution)/shard_map/pallas_call | solution.py:456
  122.9 0.0 collective-permute-done.11
  122.9 0.0 collective-permute-done.12
  122.9 0.0 collective-permute-done.9
  122.9 0.6 copy-done.5
  123.5 0.0 copy-done.6
  123.6 0.1 copy-done.7
  123.6 0.0 copy-done.8
  123.6 0.4 copy-done.1
  124.0 5.3 %shard_map.104 = bf16[24,24,1152]{2,1,0:T(8,128)(2,1)} custom-call(s32[1]{0:T(128)} %bitcast.lat_ref, bf16[24,16,1152]{2,1,0:T(8,128)(2,1)} %bitcast.28, bf16[24,16,1152]{2,1,0:T(8,128)(2,1)} %bitcast.27, bf16[4,16,1152]{2,1,0:T(8,128)(2,1)} %bitcast.35, bf16[4,16,1152]{2,1,0:T(8,128)(2,1)} %bitcast.36, bf16[4,16,1152]{2,1,0:T(8,128)(2,1)} %bitcast.37, ...), custom_call_target="tpu_custom_call" | custom-call | flops 2654208 | bytes 5308416 | tf_op jit(solution)/shard_map/pallas_call | solution.py:501
  (35 shorter events, 0.3 us)
Async XLA Ops:
  0.0 11.6 %copy-start = (bf16[256,3456]{1,0:T(8,128)(2,1)S(1)}, bf16[256,3456]{1,0:T(8,128)(2,1)}, u32[]{:S(2)}) copy-start(bf16[256,3456]{1,0:T(8,128)(2,1)} %param.13) | copy-start | bytes 5308420
  0.0 2.4 %copy-start.2 = (bf16[1,24,24,1152]{3,2,1,0:T(8,128)(2,1)S(1)}, bf16[1,24,24,1152]{3,2,1,0:T(8,128)(2,1)}, u32[]{:S(2)}) copy-start(bf16[1,24,24,1152]{3,2,1,0:T(8,128)(2,1)} %param.10) | copy-start | bytes 3981316
  3.3 23.8 %collective-permute-start = (bf16[96,1152]{1,0:T(8,128)(2,1)}, bf16[96,1152]{1,0:T(8,128)(2,1)}, u32[]{:S(2)}, u32[]{:S(2)}) collective-permute-start(bf16[96,1152]{1,0:T(8,128)(2,1)} %reshape.68), channel_id=1, source_target_pairs={{0,1},{1,2},{2,3},{3,4},{4,5},{5,6},{6,7},{7,8},{8,9},{9,10},{10,1... | collective-permute-start | bytes 663560 | tf_op jit(solution)/shard_map/ppermute | solution.py:521
  7.3 19.0 %collective-permute-start.1 = (bf16[96,1152]{1,0:T(8,128)(2,1)}, bf16[96,1152]{1,0:T(8,128)(2,1)}, u32[]{:S(2)}, u32[]{:S(2)}) collective-permute-start(bf16[96,1152]{1,0:T(8,128)(2,1)} %reshape.69), channel_id=1, source_target_pairs={{0,15},{1,0},{2,1},{3,2},{4,3},{5,4},{6,5},{7,6},{8,7},{9,8},{10,9... | collective-permute-start | bytes 663560 | tf_op jit(solution)/shard_map/ppermute | solution.py:521
  7.3 17.3 %collective-permute-start.4 = (bf16[2,72,384]{2,1,0:T(8,128)(2,1)}, bf16[2,72,384]{2,1,0:T(8,128)(2,1)}, u32[]{:S(2)}, u32[]{:S(2)}) collective-permute-start(bf16[2,72,384]{2,1,0:T(8,128)(2,1)} %convert_bitcast_fusion), channel_id=1, source_target_pairs={{1,0},{0,1},{3,2},{2,3},{5,4},{4,5},{7,6},{6,7},{9,8},{8,9},{11,10... | collective-permute-start | bytes 331784 | tf_op jit(solution)/shard_map/ppermute | solution.py:547
  12.6 12.1 %copy-start.4 = (bf16[2,72,384]{2,1,0:T(8,128)(2,1)S(1)}, bf16[2,72,384]{2,1,0:T(8,128)(2,1)}, u32[]{:S(2)}) copy-start(bf16[2,72,384]{2,1,0:T(8,128)(2,1)} %convert_bitcast_fusion) | copy-start | bytes 331780
  25.7 9.7 %collective-permute-start.5 = (bf16[2,144,384]{2,1,0:T(8,128)(2,1)S(1)}, bf16[2,144,384]{2,1,0:T(8,128)(2,1)S(1)}, u32[]{:S(2)}, u32[]{:S(2)}) collective-permute-start(bf16[2,144,384]{2,1,0:T(8,128)(2,1)S(1)} %pad_maximum_fusion.3), channel_id=1, source_target_pairs={{2,0},{3,1},{0,2},{1,3},{6,4},{7,5},{4,6},{5,7},{10,8},{11,9},{8,1... | collective-permute-start | bytes 663560 | tf_op jit(solution)/shard_map/ppermute | solution.py:547
  28.0 12.3 %collective-permute-start.2 = (bf16[128,1152]{1,0:T(8,128)(2,1)S(1)}, bf16[128,1152]{1,0:T(8,128)(2,1)S(1)}, u32[]{:S(2)}, u32[]{:S(2)}) collective-permute-start(bf16[128,1152]{1,0:T(8,128)(2,1)S(1)} %pad_maximum_fusion.1), channel_id=1, source_target_pairs={{0,16},{1,17},{2,18},{3,19},{4,20},{5,21},{6,22},{7,23},{8,24},{9,... | collective-permute-start | bytes 884744 | tf_op jit(solution)/shard_map/ppermute | solution.py:521
  31.1 10.1 %collective-permute-start.3 = (bf16[128,1152]{1,0:T(8,128)(2,1)S(1)}, bf16[128,1152]{1,0:T(8,128)(2,1)S(1)}, u32[]{:S(2)}, u32[]{:S(2)}) collective-permute-start(bf16[128,1152]{1,0:T(8,128)(2,1)S(1)} %pad_maximum_fusion.2), channel_id=1, source_target_pairs={{16,0},{17,1},{18,2},{19,3},{20,4},{21,5},{22,6},{23,7},{24,8},{25... | collective-permute-start | bytes 884744 | tf_op jit(solution)/shard_map/ppermute | solution.py:521
  35.6 44.3 %copy-start.3 = (bf16[2,288,384]{2,1,0:T(8,128)(2,1)}, bf16[2,288,384]{2,1,0:T(8,128)(2,1)S(1)}, u32[]{:S(2)}) copy-start(bf16[2,288,384]{2,1,0:T(8,128)(2,1)S(1)} %pad_maximum_fusion.t0) | copy-start | bytes 1327108
  35.6 44.3 %collective-permute-start.6 = (bf16[2,288,384]{2,1,0:T(8,128)(2,1)S(1)}, bf16[2,288,384]{2,1,0:T(8,128)(2,1)S(1)}, u32[]{:S(2)}, u32[]{:S(2)}) collective-permute-start(bf16[2,288,384]{2,1,0:T(8,128)(2,1)S(1)} %pad_maximum_fusion.t0), channel_id=1, source_target_pairs={{4,0},{5,1},{6,2},{7,3},{8,4},{9,5},{10,6},{11,7},{12,8},{13,9},{1... | collective-permute-start | bytes 1327112 | tf_op jit(solution)/shard_map/ppermute | solution.py:547
  38.4 41.6 %collective-permute-start.7 = (bf16[2,288,384]{2,1,0:T(8,128)(2,1)S(1)}, bf16[2,288,384]{2,1,0:T(8,128)(2,1)S(1)}, u32[]{:S(2)}, u32[]{:S(2)}) collective-permute-start(bf16[2,288,384]{2,1,0:T(8,128)(2,1)S(1)} %pad_maximum_fusion.t0), channel_id=1, source_target_pairs={{8,0},{9,1},{10,2},{11,3},{12,4},{13,5},{14,6},{15,7},{0,8},{1,9},... | collective-permute-start | bytes 1327112 | tf_op jit(solution)/shard_map/ppermute | solution.py:547
  38.7 41.2 %collective-permute-start.8 = (bf16[2,288,384]{2,1,0:T(8,128)(2,1)S(1)}, bf16[2,288,384]{2,1,0:T(8,128)(2,1)S(1)}, u32[]{:S(2)}, u32[]{:S(2)}) collective-permute-start(bf16[2,288,384]{2,1,0:T(8,128)(2,1)S(1)} %pad_maximum_fusion.t0), channel_id=1, source_target_pairs={{12,0},{13,1},{14,2},{15,3},{0,4},{1,5},{2,6},{3,7},{4,8},{5,9},{6... | collective-permute-start | bytes 1327112 | tf_op jit(solution)/shard_map/ppermute | solution.py:547
  40.3 1.6 %copy-start.12 = (bf16[128,1152]{1,0:T(8,128)(2,1)}, bf16[128,1152]{1,0:T(8,128)(2,1)S(1)}, u32[]{:S(2)}) copy-start(bf16[128,1152]{1,0:T(8,128)(2,1)S(1)} %collective-permute-done.2.top) | copy-start | bytes 884740
  41.2 0.7 copy-start.13
  79.9 0.8 copy-start.9
  79.9 0.9 copy-start.10
  79.9 1.0 copy-start.11
  94.2 28.8 %collective-permute-start.9 = (bf16[384,1152]{1,0:T(8,128)(2,1)}, bf16[384,1152]{1,0:T(8,128)(2,1)S(1)}, u32[]{:S(2)}, u32[]{:S(2)}) collective-permute-start(bf16[384,1152]{1,0:T(8,128)(2,1)} %get-tuple-element.18), channel_id=1, source_target_pairs={{0,15},{1,0},{2,1},{3,2},{4,3},{5,4},{6,5},{7,6},{8,7},{9,8},{10,9... | collective-permute-start | bytes 2654216 | tf_op jit(solution)/shard_map/ppermute | solution.py:521
  95.6 27.2 %collective-permute-start.10 = (bf16[64,1152]{1,0:T(8,128)(2,1)}, bf16[64,1152]{1,0:T(8,128)(2,1)S(1)}, u32[]{:S(2)}, u32[]{:S(2)}) collective-permute-start(bf16[64,1152]{1,0:T(8,128)(2,1)} %get-tuple-element.19), channel_id=1, source_target_pairs={{0,16},{1,17},{2,18},{3,19},{4,20},{5,21},{6,22},{7,23},{8,24},{9,... | collective-permute-start | bytes 442376 | tf_op jit(solution)/shard_map/ppermute | solution.py:521
  98.6 24.3 %collective-permute-start.11 = (bf16[64,1152]{1,0:T(8,128)(2,1)}, bf16[64,1152]{1,0:T(8,128)(2,1)S(1)}, u32[]{:S(2)}, u32[]{:S(2)}) collective-permute-start(bf16[64,1152]{1,0:T(8,128)(2,1)} %get-tuple-element.20), channel_id=1, source_target_pairs={{0,31},{1,16},{2,17},{3,18},{4,19},{5,20},{6,21},{7,22},{8,23},{9,... | collective-permute-start | bytes 442376 | tf_op jit(solution)/shard_map/ppermute | solution.py:521
  104.2 18.7 %collective-permute-start.12 = (bf16[64,1152]{1,0:T(8,128)(2,1)}, bf16[64,1152]{1,0:T(8,128)(2,1)S(1)}, u32[]{:S(2)}, u32[]{:S(2)}) collective-permute-start(bf16[64,1152]{1,0:T(8,128)(2,1)} %get-tuple-element.21), channel_id=1, source_target_pairs={{16,0},{17,1},{18,2},{19,3},{20,4},{21,5},{22,6},{23,7},{24,8},{25... | collective-permute-start | bytes 442376 | tf_op jit(solution)/shard_map/ppermute | solution.py:521
  108.8 14.2 %collective-permute-start.13 = (bf16[64,1152]{1,0:T(8,128)(2,1)}, bf16[64,1152]{1,0:T(8,128)(2,1)S(1)}, u32[]{:S(2)}, u32[]{:S(2)}) collective-permute-start(bf16[64,1152]{1,0:T(8,128)(2,1)} %get-tuple-element.22), channel_id=1, source_target_pairs={{16,15},{17,0},{18,1},{19,2},{20,3},{21,4},{22,5},{23,6},{24,7},{2... | collective-permute-start | bytes 442376 | tf_op jit(solution)/shard_map/ppermute | solution.py:521
  122.9 0.7 copy-start.5
  122.9 0.7 copy-start.6
  122.9 0.7 copy-start.7
  122.9 0.7 copy-start.8
  122.9 1.1 copy-start.1

commit v3 on v2

--- a/solution.py
+++ b/solution.py
@@ -72,7 +72,7 @@
     ]
 
 
-def project_qkv(u_ref, w_s, waits, size, width, q_factor, out_ref, at):
+def project_qkv(u_ref, w_s, waits, size, width, q_factor, out_ref, at, done=lambda c, n: None):
     count = u_ref.shape[0]
     for wait, (c, n) in zip(waits, column_parts(w_s.shape[1], size)):
         wait.wait()
@@ -81,6 +81,7 @@
             ids = lax.broadcasted_iota(jnp.int32, (1, n), 1)
             made = made * jnp.where(ids < width - c, q_factor, 1.0)
         out_ref[at : at + count, c : c + n] = made.astype(BF16)
+        done(c, n)
 
 
 def band(low, high, dims, axis):
@@ -255,11 +256,18 @@
 QKV_PART = 512
 
 
-def core_kernel(q_factor, x_ref, shift_ref, scale_ref, w_hbm, out_ref, u_s, w_s, sems):
+def core_kernel(q_factor, x_ref, shift_ref, scale_ref, w_hbm, out_hbm, u_s, w_s, out_s, sems):
     waits = begin(weight_pairs(w_hbm, w_s, QKV_PART), sems, 0)
     count, width = x_ref.shape
     normalise(x_ref, 0, count, shift_ref, scale_ref, u_s)
-    project_qkv(u_s, w_s, waits, QKV_PART, width, q_factor, out_ref, 0)
+    sent = []
+
+    def done(c, n):
+        cols = pl.ds(c, n)
+        sent.extend(begin([(out_s.at[:, cols], out_hbm.at[:, cols])], sems, 8 + len(sent)))
+
+    project_qkv(u_s, w_s, waits, QKV_PART, width, q_factor, out_s, 0, done)
+    finish_all(sent)
 
 
 def core_qkv(q_factor, x, shift, scale, weight):
@@ -269,11 +277,12 @@
         functools.partial(core_kernel, q_factor),
         out_shape=jax.ShapeDtypeStruct((count, total), BF16),
         in_specs=[LOCAL, LOCAL, LOCAL, ANY],
-        out_specs=LOCAL,
+        out_specs=ANY,
         scratch_shapes=[
             pltpu.VMEM((count, width), BF16),
             pltpu.VMEM((width, total), BF16),
-            pltpu.SemaphoreType.DMA((8,)),
+            pltpu.VMEM((count, total), BF16),
+            pltpu.SemaphoreType.DMA((16,)),
         ],
         compiler_params=pltpu.CompilerParams(vmem_limit_bytes=VMEM),
         cost_estimate=pl.CostEstimate(
@@ -297,14 +306,13 @@
             target_ref[at : at + n, :] = source_ref[start : start + n, :]
             at += n
 
-    for r in range(core):
-        take((inner + rim * r, rim), (core * r, half))
     for base in (inner + 2 * side, inner + 2 * side + edge):
         for a in range(rim):
             take((base + rim * a, rim), (base + rim * rim + core * a, half))
-    for base in (inner + 2 * side, inner + 2 * side + edge):
         for a in range(rim):
             take((base + rim * rim + core * a + half, half), (base + rim * rim + side + rim * a, rim))
+    for r in range(core):
+        take((inner + rim * r, rim), (core * r, half))
     for r in range(core):
         take((core * r + half, half), (inner + side + rim * r, rim))
 
@@ -313,6 +321,7 @@
     core,
     rim,
     rows,
+    text,
     q_factor,
     x_core,
     left,
@@ -326,14 +335,20 @@
     w_hbm,
     wo_hbm,
     wq_hbm,
+    wc_hbm,
+    kv_hbm,
     h1_out,
     cq_out,
+    top_out,
+    bottom_out,
     x_s,
     qkv_s,
     u_s,
     w_s,
     wo_s,
     wq_s,
+    wc_s,
+    kv_s,
     vv_s,
     p_a,
     p_b,
@@ -355,7 +370,11 @@
     waits_x = begin(pairs, sems, 0)
     waits_w = begin(weight_pairs(w_hbm, w_s, QKV_PART), sems, 4)
     waits_qkv = begin([(qkv_core, qkv_s.at[pl.ds(0, inner)])], sems, 12)
-    waits_later = begin([(x_core, x_s.at[pl.ds(0, inner)]), (wo_hbm, wo_s), (wq_hbm, wq_s)], sems, 13)
+    waits_later = begin(
+        [(x_core, x_s.at[pl.ds(0, inner)]), (wo_hbm, wo_s), (wq_hbm, wq_s), (wc_hbm, wc_s), (kv_hbm, kv_s)],
+        sems,
+        13,
+    )
     finish_all(waits_x)
     normalise(x_s, inner, outer, shift_ref, scale_ref, u_s)
     project_qkv(u_s, w_s, waits_w, QKV_PART, width, q_factor, qkv_s, inner)
@@ -378,28 +397,41 @@
         mixed = jnp.dot(attn_s[part, :], wo_s[...], preferred_element_type=F32)
         h1_s[part, :] = x_s[part, :].astype(F32) + gate_ref[...] * mixed
     regroup(core, rim, h1_s, hg_s)
-    waits_h = begin([(hg_s, h1_out)], sems, 16)
+    edges = top_out.shape[0] + bottom_out.shape[0]
+    kept = pl.ds(edges, total - edges)
+    waits_h = begin([(hg_s.at[kept], h1_out)], sems, 18)
     for r in range(0, total, step):
         part = slice(r, r + step)
         made = jnp.dot(hg_s[part, :].astype(BF16), wq_s[...], preferred_element_type=F32)
-        attn_s[part, :] = (made * q_factor).astype(BF16)
-        waits_h += begin([(attn_s.at[pl.ds(r, step)], cq_out.at[pl.ds(r, step)])], sems, 17 + r // step)
+        x_s[part, :] = (made * q_factor).astype(BF16)
+    waits_h += begin([(x_s.at[kept], cq_out)], sems, 19)
+    outer_rows = pl.ds(0, edges)
+    found = attn_s.at[outer_rows]
+    room = (outer_rows, pl.ds(0, 2 * kv_s.shape[2]))
+    attend_text(channels, text, x_s.at[outer_rows], kv_s, (p_a.at[room], p_b.at[room]), bad_s, edges, found)
+    made = hg_s[:edges, :] + jnp.dot(found[...], wc_s[...], preferred_element_type=F32)
+    top_out[...] = made[: edges // 2].astype(BF16)
+    bottom_out[...] = made[edges // 2 :].astype(BF16)
     finish_all(waits_h)
 
 
-def tile_self(core, rim, q_factor, x_core, rims, qkv_core, mod, qkv_weight, out_weight, cross_q):
+def tile_self(core, rim, text, q_factor, x_core, rims, qkv_core, mod, weights, text_kv):
     inner, width = x_core.shape
     outer = sum(a.shape[0] for a in rims)
     total = inner + outer
-    wide = qkv_weight.shape[1]
+    wide = weights[0].shape[1]
+    edge = rim * (core + 2 * rim)
+    kept = total - 2 * edge
     return pl.pallas_call(
-        functools.partial(tile_kernel, core, rim, 512, q_factor),
+        functools.partial(tile_kernel, core, rim, 512, text, q_factor),
         out_shape=[
-            jax.ShapeDtypeStruct((total, width), F32),
-            jax.ShapeDtypeStruct((total, width), BF16),
+            jax.ShapeDtypeStruct((kept, width), F32),
+            jax.ShapeDtypeStruct((kept, width), BF16),
+            jax.ShapeDtypeStruct((edge, width), BF16),
+            jax.ShapeDtypeStruct((edge, width), BF16),
         ],
-        in_specs=[ANY] * 6 + [LOCAL] * 3 + [ANY] * 3,
-        out_specs=[ANY, ANY],
+        in_specs=[ANY] * 6 + [LOCAL] * 3 + [ANY] * 5,
+        out_specs=[ANY, ANY, LOCAL, LOCAL],
         scratch_shapes=[
             pltpu.VMEM((total, width), BF16),
             pltpu.VMEM((total, wide), BF16),
@@ -407,6 +439,8 @@
             pltpu.VMEM((width, wide), BF16),
             pltpu.VMEM((width, width), BF16),
             pltpu.VMEM((width, width), BF16),
+            pltpu.VMEM((width, width), BF16),
+            pltpu.VMEM(text_kv.shape, BF16),
             pltpu.VMEM((2 * total, WIN), BF16),
             pltpu.VMEM((total, 2 * total), BF16),
             pltpu.VMEM((total, 2 * total), BF16),
@@ -422,42 +456,34 @@
             bytes_accessed=2 * width * (wide + 2 * width) + 2 * inner * wide + 6 * total * width,
             transcendentals=HEADS * total * total,
         ),
-    )(x_core, *rims, qkv_core, *mod, qkv_weight, out_weight, cross_q)
-
-
-def text_kernel(text, first, parts, rows, column_ref, h1, cq, t0, t1, t2, t3, wc_hbm, *rest):
-    outs = rest[: len(parts)]
-    q_s, h_s, kv_s, wc_s, p_a, p_b, attn_s, bad_s, sems = rest[len(parts) :]
+    )(x_core, *rims, qkv_core, *mod, *weights, text_kv)
+
+
+def text_kernel(text, first, h1, cq, kv_hbm, wc_hbm, *rest):
+    *added, out, q_s, h_s, kv_s, wc_s, p_a, p_b, attn_s, bad_s, sems = rest
     count, width = q_s.shape
-    waits = begin([(cq.at[pl.ds(first, count)], q_s)], sems, 0)
-    pairs = []
-    for k, arrived in enumerate((t0, t1, t2, t3)):
-        size = arrived.shape[1]
-        where = pl.multiple_of(lax.rem(column_ref[0] + k, 4) * size, size)
-        for j in range(2):
-            pairs.append((arrived.at[j], kv_s.at[j, pl.ds(where, size), :]))
-    waits += begin(pairs, sems, 1)
-    waits_later = begin([(wc_hbm, wc_s), (h1.at[pl.ds(first, count)], h_s)], sems, 9)
+    rows = pl.ds(first, count)
+    waits = begin([(cq.at[rows], q_s), (kv_hbm, kv_s)], sems, 0)
+    waits_later = begin([(wc_hbm, wc_s), (h1.at[rows], h_s)], sems, 2)
     finish_all(waits)
-    attend_text(width // HEADS, text, q_s, kv_s, (p_a, p_b), bad_s, rows, attn_s)
+    attend_text(width // HEADS, text, q_s, kv_s, (p_a, p_b), bad_s, count, attn_s)
     finish_all(waits_later)
-    at = 0
-    for out, n in zip(outs, parts):
-        at_end = at + n
-        made = jnp.dot(attn_s[at:at_end, :], wc_s[...], preferred_element_type=F32)
-        out[...] = (h_s[at:at_end, :] + made).astype(BF16)
-        at = at_end
-
-
-def tile_text(text, first, parts, column, h1, cq, arrived, weight):
-    count = sum(parts)
+    made = h_s[...] + jnp.dot(attn_s[...], wc_s[...], preferred_element_type=F32)
+    if added:
+        low, high = (a[a.shape[0] // 2 :, :].astype(F32) for a in added)
+        n = low.shape[0]
+        made = jnp.concatenate([made[:n] + low, made[n:-n], made[-n:] + high], axis=0)
+    out[...] = made.astype(BF16)
+
+
+def tile_text(text, first, count, h1, cq, text_kv, weight, *added):
     width = h1.shape[1]
-    padded = arrived[0].shape[2]
+    padded = text_kv.shape[2]
     return pl.pallas_call(
-        functools.partial(text_kernel, text, first, parts, count),
-        out_shape=[jax.ShapeDtypeStruct((n, width), BF16) for n in parts],
-        in_specs=[pl.BlockSpec(memory_space=pltpu.SMEM)] + [ANY] * 7,
-        out_specs=[LOCAL] * len(parts),
+        functools.partial(text_kernel, text, first),
+        out_shape=jax.ShapeDtypeStruct((count, width), BF16),
+        in_specs=[ANY] * 4 + [LOCAL] * len(added),
+        out_specs=LOCAL,
         scratch_shapes=[
             pltpu.VMEM((count, width), BF16),
             pltpu.VMEM((count, width), F32),
@@ -467,7 +493,7 @@
             pltpu.VMEM((count, 2 * padded), BF16),
             pltpu.VMEM((count, width), BF16),
             pltpu.VMEM((1, LANES), F32),
-            pltpu.SemaphoreType.DMA((11,)),
+            pltpu.SemaphoreType.DMA((4,)),
         ],
         compiler_params=pltpu.CompilerParams(vmem_limit_bytes=VMEM),
         cost_estimate=pl.CostEstimate(
@@ -475,39 +501,34 @@
             bytes_accessed=2 * width * (width + 2 * padded) + 8 * count * width,
             transcendentals=HEADS * count * padded,
         ),
-    )(column, h1, cq, *arrived, weight)
-
-
-def merge_kernel(lat_count, lat_ref, near, far, dn_near, dn_far, up_near, up_far, out_ref):
-    step = pl.program_id(0)
-    last = pl.num_programs(0) - 1
+    )(h1, cq, text_kv, weight, *added)
+
+
+def merge_kernel(lat_count, rim, lat_ref, near, far, out_ref):
     lat = lat_ref[0]
-    low = jnp.where(step == 0, 1.0, 0.0)
-    high = jnp.where(step == last, 1.0, 0.0)
-    shared = ((step == 0) & (lat > 0)) | ((step == last) & (lat < lat_count - 1))
+    rows = near.shape[0]
+    ids = lax.broadcasted_iota(jnp.int32, (rows, 1, 1), 0) + pl.program_id(0) * rows
+    core = pl.num_programs(0) * rows
+    shared = ((ids < rim) & (lat > 0)) | ((ids >= core - rim) & (lat < lat_count - 1))
     scale = jnp.where(shared, 0.5, 1.0)
-
-    def total(body, dn, up):
-        return (body[...].astype(F32) + low * dn[...].astype(F32) + high * up[...].astype(F32)) * scale
-
-    a, b = total(near, dn_near, up_near), total(far, dn_far, up_far)
+    a, b = near[...].astype(F32) * scale, far[...].astype(F32) * scale
     out_ref[...] = jnp.concatenate([a[:, :8], (a[:, 8:] + b[:, :8]) * 0.5, b[:, 8:]], axis=1).astype(BF16)
 
 
-def merge(lat_count, lat, core, rim, near, far, down, down_left, up, up_left):
-    span, width = near.shape[1:]
-    whole = pl.BlockSpec((rim, span, width), lambda i: (0, 0, 0))
-    rows = pl.BlockSpec((rim, span, width), lambda i: (i, 0, 0))
+def merge(lat_count, lat, rim, near, far):
+    core, span, width = near.shape
+    rows = 8
+    part = pl.BlockSpec((rows, span, width), lambda i: (i, 0, 0))
     return pl.pallas_call(
-        functools.partial(merge_kernel, lat_count),
+        functools.partial(merge_kernel, lat_count, rim),
         out_shape=jax.ShapeDtypeStruct((core, core, width), BF16),
-        grid=(core // rim,),
-        in_specs=[pl.BlockSpec(memory_space=pltpu.SMEM), rows, rows, whole, whole, whole, whole],
-        out_specs=pl.BlockSpec((rim, core, width), lambda i: (i, 0, 0)),
+        grid=(core // rows,),
+        in_specs=[pl.BlockSpec(memory_space=pltpu.SMEM), part, part],
+        out_specs=pl.BlockSpec((rows, core, width), lambda i: (i, 0, 0)),
         cost_estimate=pl.CostEstimate(
             flops=4 * core * core * width, bytes_accessed=8 * core * core * width, transcendentals=0
         ),
-    )(lat, near, far, down, down_left, up, up_left)
+    )(lat, near, far)
 
 
 def send(value, mesh_sizes, down, right):
@@ -539,71 +560,52 @@
     rim = HALO
     text = context.shape[1]
     lon_count = sizes[1]
-    lon = lax.axis_index("lon")
     to = functools.partial(send, mesh_sizes=sizes)
     q_factor = math.log2(math.e) / math.sqrt(width // HEADS)
-
-    def among(value, partner):
-        return lax.ppermute(value, "lon", [(partner(i), i) for i in range(lon_count)])
 
     padded = jnp.pad(context[0], ((0, TEXT_PAD - text), (0, 0)))
     own_head = jnp.einsum("td,sde->set", padded, cross_kv, preferred_element_type=F32).astype(BF16)
     x = hidden[0]
     x, own_head = lax.optimization_barrier((x, own_head))
-    other = among(own_head, lambda i: i ^ 1)
+    copies = jnp.broadcast_to(own_head[None], (lon_count,) + own_head.shape)
+    all_heads = lax.all_to_all(copies, "lon", 0, 0, tiled=True)
     left = to(x[:, core - rim :].reshape(-1, width), down=0, right=1)
     right = to(x[:, :rim].reshape(-1, width), down=0, right=-1)
-
-    def joined(bit, mine, theirs):
-        low = (lon // bit) % 2 == 0
-        return jnp.concatenate([jnp.where(low, mine, theirs), jnp.where(low, theirs, mine)], axis=1)
-
-    two = joined(1, own_head, other)
-    four = joined(2, two, among(two, lambda i: i ^ 2))
-    arrived = [four] + [among(four, lambda i, k=k: (i + 4 * k) % lon_count) for k in (1, 2, 3)]
-    column = (lon // 4).astype(jnp.int32)[None]
-
     shift, scale, gate = modulation(timestep, time_weight, modulation_bias)
-    x_core = x.reshape(core * core, width)
-    qkv_core = core_qkv(q_factor, x_core, shift, scale, qkv_weight)
-
     corner = rim * rim
     low_edge = jnp.concatenate([left[-corner:], x[core - rim :].reshape(-1, width), right[-corner:]], axis=0)
     high_edge = jnp.concatenate([left[:corner], x[:rim].reshape(-1, width), right[:corner]], axis=0)
+    x, low_edge, high_edge = lax.optimization_barrier((x, low_edge, high_edge))
     top = to(low_edge, down=1, right=0)
     bottom = to(high_edge, down=-1, right=0)
-
-    h1, cq = tile_self(
+    x_core = x.reshape(core * core, width)
+    qkv_core = core_qkv(q_factor, x_core, shift, scale, qkv_weight)
+    text_kv = jnp.transpose(all_heads, (1, 0, 2, 3)).reshape(2, width, TEXT_PAD)
+
+    h1, cq, top_made, bottom_made = tile_self(
         core,
         rim,
+        text,
         q_factor,
         x_core,
         (left, right, top, bottom),
         qkv_core,
         (shift, scale, gate),
-        qkv_weight,
-        out_weight,
-        cross_q,
+        (qkv_weight, out_weight, cross_q, cross_output_projection),
+        text_kv,
     )
     span = half + rim
     block, edge = core * span, rim * span
-    main, top_left, bottom_left, top_right, bottom_right = tile_text(
-        text, 0, (block, edge, edge, edge, edge), column, h1, cq, arrived, cross_output_projection
-    )
+    high = to(top_made, down=-1, right=0)
+    low = to(bottom_made, down=1, right=0)
+    main = tile_text(text, 0, block, h1, cq, text_kv, cross_output_projection)
+    main = main.at[:edge].add(low[:edge])
+    main = main.at[block - edge :].add(high[:edge])
     far = to(main, down=0, right=-1)
-    up_left = to(top_left, down=-1, right=-1)
-    down_left = to(bottom_left, down=1, right=-1)
-    up = to(top_right, down=-1, right=0)
-    down = to(bottom_right, down=1, right=0)
-    (near,) = tile_text(
-        text, block + 4 * edge, (block,), column, h1, cq, arrived, cross_output_projection
-    )
-    shape = lambda a: a.reshape(-1, span, width)
+    near = tile_text(text, block, block, h1, cq, text_kv, cross_output_projection, low, high)
+    shape = lambda a: a.reshape(core, span, width)
     lat = lax.axis_index("lat").astype(jnp.int32)[None]
-    out = merge(
-        sizes[0], lat, core, rim, *(shape(a) for a in (near, far, down, down_left, up, up_left))
-    )
-    return out[None]
+    return merge(sizes[0], lat, rim, shape(near), shape(far))[None]
 
 
 def solution(mesh):

time: 130 us -> 129 us (level)
  starting transfers between devices: 37.3 us -> 27.6 us
  local copies, waits for them, and re-layouts: 7.47 us -> 12.1 us
  other arithmetic: 1.86 us -> 4.38 us
  waiting for transfers between devices: 1.81 us -> 3.29 us
    ppermute x9 -> x7, starting transfers between devices: 30 us -> 20 us  [send(): return lax.ppermute(value, ('lat', 'lon'), pairs)]
    all_to_all x0 -> x1, starting transfers between devices: none -> 7.56 us  [local(): all_heads = lax.all_to_all(copies, 'lon', 0, 0, tiled=True)]
    ppermute x5 -> x0, starting transfers between devices: 7.28 us -> none  [among(): lax.ppermute(value, 'lon', [(partner(i), i) for i in range(lon_count)])]
    scatter-add x0 -> x2, other arithmetic: none -> 3.43 us  [the longest x1 1.72 us: local(): main = main.at[:edge].add(low[:edge])]
    unnamed x28 -> x12, local copies, waits for them, and re-layouts: 2.83 us -> 1 us
    slice x1, local copies, waits for them, and re-layouts: 0.03 us -> 1.84 us  [local(): x[:rim].reshape(-1, width)]
    ppermute x9 -> x7, waiting for transfers between devices: 1.8 us -> 3.29 us  [send(): return lax.ppermute(value, ('lat', 'lon'), pairs)]
    transpose x0 -> x1, local copies, waits for them, and re-layouts: none -> 1.48 us  [local(): text_kv = jnp.transpose(all_heads, (1, 0, 2, 3)).reshape(2, width, TEXT_PAD)]
  transfers between devices with their start and end apart: 14 -> 8, of which waited for: 2 -> 1; matrix products, arithmetic and copies ran while one was open for 4% -> 10% of each run, Pallas kernels for 46% -> 24%
where the time goes in v3:
time: 129 us; the launch traced here: 128 us
  Pallas kernels  76.7 us (59%)
  starting transfers between devices  27.6 us (21%)
  local copies, waits for them, and re-layouts  12.1 us (9%)
  other arithmetic  4.38 us (3%)
  waiting for transfers between devices  3.29 us (3%)
  matrix products  2.81 us (2%)
    pallas_call x1, Pallas kernels, tile_self(): pl.pallas_call(functools.partial(tile_kernel, core, rim, 512, text, q_fac...  43.1 us
    ppermute x7, starting transfers between devices, send(): return lax.ppermute(value, ('lat', 'lon'), pairs)  20 us
    pallas_call x2, Pallas kernels, tile_text(): pl.pallas_call(functools.partial(text_kernel, text, first), out_shape=jax...  19.3 us
    pallas_call x1, Pallas kernels, core_qkv(): pl.pallas_call(functools.partial(core_kernel, q_factor), out_shape=jax.Sh...  10.9 us
    all_to_all x1, starting transfers between devices, local(): all_heads = lax.all_to_all(copies, 'lon', 0, 0, tiled=True)  7.56 us
    pallas_call x1, Pallas kernels, merge(): pl.pallas_call(functools.partial(merge_kernel, lat_count, rim), out_shape...  3.44 us
    ppermute x7, waiting for transfers between devices, send(): return lax.ppermute(value, ('lat', 'lon'), pairs)  3.29 us
  transfers between devices with their start and end apart: 8, of which 1 were waited for; matrix products, arithmetic and copies ran while one was open for 10% of the time, Pallas kernels for 24%

profile of v3, /device:TPU:33, one launch (start us, length us, event | category | flops | bytes accessed | tf_op | source)
XLA Modules:
  0.0 127.7 jit_solution(6227157780363442561)
XLA Ops:
  0.0 0.0 copy-start
  0.0 1.7 %fusion = f32[384,144]{0,1:S(1)} fusion(bf16[1152,144]{0,1:T(8,128)(2,1)} %bitcast.35, bf16[300,1152]{1,0:T(8,128)(2,1)} %bitcast.30), kind=kOutput, calls=%fused_computation.1 | convolution fusion | flops 127401984 | bytes 1244160
  1.8 1.3 %fusion.9 = (bf16[24,4,1152]{2,1,0:T(4,128)(2,1)S(1)}, bf16[24,4,1152]{2,1,0:T(4,128)(2,1)S(1)}) fusion(bf16[24,24,1152]{2,1,0:T(8,128)(2,1)} %bitcast.31), kind=kLoop, calls=%fused_computation.18 | loop fusion | bytes 884736 | tf_op jit(solution)/shard_map/slice | solution.py:572
  3.1 0.7 reshape.108
  3.8 3.3 %collective-permute-start = (bf16[96,1152]{1,0:T(8,128)(2,1)}, bf16[96,1152]{1,0:T(8,128)(2,1)}, u32[]{:S(2)}, u32[]{:S(2)}) collective-permute-start(bf16[96,1152]{1,0:T(8,128)(2,1)} %reshape.108), channel_id=1, source_target_pairs={{0,1},{1,2},{2,3},{3,4},{4,5},{5,6},{6,7},{7,8},{8,9},{9,10},{10,1... | collective-permute-start | bytes 663560 | tf_op jit(solution)/shard_map/ppermute | solution.py:542
  7.1 0.7 reshape.110
  7.8 0.0 collective-permute-start.1
  7.8 1.4 %broadcast_in_dim.7 = bf16[16,2,72,384]{3,2,1,0:T(8,128)(2,1)} broadcast(bf16[2,72,384]{2,1,0:T(8,128)(2,1)S(1)} %convert_bitcast_fusion), dimensions={1,2,3} | broadcast | bytes 1880064 | tf_op jit(solution)/shard_map/broadcast_in_dim | solution.py:570
  9.3 7.6 %all-to-all-start = ((bf16[16,2,72,384]{3,2,1,0:T(8,128)(2,1)}), bf16[16,2,72,384]{3,2,1,0:T(8,128)(2,1)S(1)}, u32[]{:S(2)}, u32[]{:S(2)}) async-start(bf16[16,2,72,384]{3,2,1,0:T(8,128)(2,1)} %broadcast_in_dim.7), calls=%async_computation | async-start | bytes 3538944 | tf_op jit(solution)/shard_map/all_to_all | solution.py:571
  16.8 1.8 %fusion.8 = (bf16[4,24,1152]{2,1,0:T(8,128)(2,1)}, bf16[4,24,1152]{2,1,0:T(8,128)(2,1)}) fusion(bf16[24,24,1152]{2,1,0:T(8,128)(2,1)} %bitcast.32), kind=kLoop, calls=%fused_computation.17 | loop fusion | bytes 884736 | tf_op jit(solution)/shard_map/slice | solution.py:577
  19.4 0.6 reshape.118
  20.0 0.7 broadcast_in_dim_reshape.3
  20.7 0.0 copy-done
  20.7 0.0 copy-start.1
  20.7 0.0 copy-start.2
  20.7 1.1 convolution_reduce_fusion
  21.9 0.6 fusion.12
  22.5 0.0 collective-permute-done.left
  22.5 0.8 fusion.10
  23.3 0.0 collective-permute-done.1.right
  23.3 0.8 fusion.11
  24.1 0.0 copy-done.1
  24.1 0.0 copy-done.2
  24.1 0.9 pad_maximum_fusion
  24.9 3.1 %collective-permute-start.2 = (bf16[128,1152]{1,0:T(8,128)(2,1)}, bf16[128,1152]{1,0:T(8,128)(2,1)}, u32[]{:S(2)}, u32[]{:S(2)}) collective-permute-start(bf16[128,1152]{1,0:T(8,128)(2,1)} %get-tuple-element.40), channel_id=1, source_target_pairs={{0,16},{1,17},{2,18},{3,19},{4,20},{5,21},{6,22},{7,23},{8,24},{9,... | collective-permute-start | bytes 884744 | tf_op jit(solution)/shard_map/ppermute | solution.py:542
  28.1 4.3 %collective-permute-start.3 = (bf16[128,1152]{1,0:T(8,128)(2,1)}, bf16[128,1152]{1,0:T(8,128)(2,1)}, u32[]{:S(2)}, u32[]{:S(2)}) collective-permute-start(bf16[128,1152]{1,0:T(8,128)(2,1)} %get-tuple-element.41), channel_id=1, source_target_pairs={{16,0},{17,1},{18,2},{19,3},{20,4},{21,5},{22,6},{23,7},{24,8},{25... | collective-permute-start | bytes 884744 | tf_op jit(solution)/shard_map/ppermute | solution.py:542
  32.4 10.9 %shard_map.100.qkv_core = bf16[576,3456]{1,0:T(8,128)(2,1)} custom-call(bf16[576,1152]{1,0:T(8,128)(2,1)} %bitcast.33, f32[1,1152]{1,0:T(1,128)} %get-tuple-element.57.shift_ref, f32[1,1152]{1,0:T(1,128)} %get-tuple-element.56.scale_ref, bf16[1152,3456]{1,0:T(8,128)(2,1)} %w_hbm.3), custom_call_target="tpu_custom_call" | custom-call | flops 4586471424 | bytes 13271040 | tf_op jit(solution)/shard_map/pallas_call | solution.py:276
  43.2 0.0 all-to-all-done
  43.3 1.5 %copy.11 = bf16[2,16,72,384]{3,2,1,0:T(8,128)(2,1)} copy(bf16[2,16,72,384]{3,2,0,1:T(8,128)(2,1)S(1)} %bitcast.21) | data formatting | bytes 3538944 | tf_op jit(solution)/shard_map/transpose | solution.py:583
  44.7 0.0 collective-permute-done.2.top
  44.7 0.0 collective-permute-done.3.bottom
  44.7 43.1 %shard_map.101 = (f32[768,1152]{1,0:T(8,128)}, bf16[768,1152]{1,0:T(8,128)(2,1)}, bf16[128,1152]{1,0:T(8,128)(2,1)}, bf16[128,1152]{1,0:T(8,128)(2,1)}) custom-call(bf16[576,1152]{1,0:T(8,128)(2,1)} %bitcast.34, bf16[96,1152]{1,0:T(8,128)(2,1)} %collective-permute-done.left, bf16[96,1152]{1,0:T(8,128)(2,1)} %collective-permute-done.1.right, ...), custom_call_target="tpu_custom_call" | custom-call | flops 28330426368 | bytes 24330240 | tf_op jit(solution)/shard_map/pallas_call | solution.py:425
  87.8 1.9 %collective-permute-start.4 = (bf16[128,1152]{1,0:T(8,128)(2,1)}, bf16[128,1152]{1,0:T(8,128)(2,1)S(1)}, u32[]{:S(2)}, u32[]{:S(2)}) collective-permute-start(bf16[128,1152]{1,0:T(8,128)(2,1)} %get-tuple-element.45), channel_id=1, source_target_pairs={{0,16},{1,17},{2,18},{3,19},{4,20},{5,21},{6,22},{7,23},{8,24},{9,... | collective-permute-start | bytes 884744 | tf_op jit(solution)/shard_map/ppermute | solution.py:542
  89.7 5.7 %collective-permute-start.5 = (bf16[128,1152]{1,0:T(8,128)(2,1)}, bf16[128,1152]{1,0:T(8,128)(2,1)S(1)}, u32[]{:S(2)}, u32[]{:S(2)}) collective-permute-start(bf16[128,1152]{1,0:T(8,128)(2,1)} %get-tuple-element.46), channel_id=1, source_target_pairs={{16,0},{17,1},{18,2},{19,3},{20,4},{21,5},{22,6},{23,7},{24,8},{25... | collective-permute-start | bytes 884744 | tf_op jit(solution)/shard_map/ppermute | solution.py:542
  95.4 9.1 %shard_map.103 = bf16[384,1152]{1,0:T(8,128)(2,1)} custom-call(f32[768,1152]{1,0:T(8,128)} %get-tuple-element.43.h1, bf16[768,1152]{1,0:T(8,128)(2,1)} %get-tuple-element.44.cq, bf16[2,1152,384]{2,1,0:T(8,128)(2,1)} %bitcast.23, bf16[1152,1152]{1,0:T(8,128)(2,1)} %wc_hbm.5), custom_call_target="tpu_custom_call" | custom-call | flops 3737124864 | bytes 7962624 | tf_op jit(solution)/shard_map/pallas_call | solution.py:482
  104.6 0.0 collective-permute-done.4.rest_0_
  104.6 0.0 copy-start.4
  104.6 1.7 %fusion.3 = bf16[384,1152]{1,0:T(8,128)(2,1)} fusion(bf16[384,1152]{1,0:T(8,128)(2,1)} %shard_map.103, bf16[128,1152]{1,0:T(8,128)(2,1)S(1)} %collective-permute-done.4.rest_0_), kind=kLoop, calls=%fused_computation.8 | loop fusion | flops 294912 | bytes 442368 | tf_op jit(solution)/shard_map/scatter-add | solution.py:602
  106.3 0.0 collective-permute-done.5.rest_1_
  106.3 0.0 copy-start.5
  106.3 1.7 %fusion.2 = bf16[384,1152]{1,0:T(8,128)(2,1)} fusion(bf16[384,1152]{1,0:T(8,128)(2,1)} %fusion.3, bf16[128,1152]{1,0:T(8,128)(2,1)S(1)} %collective-permute-done.5.rest_1_), kind=kLoop, calls=%fused_computation.6 | loop fusion | flops 294912 | bytes 442368 | tf_op jit(solution)/shard_map/scatter-add | solution.py:603
  108.0 1.8 %collective-permute-start.6 = (bf16[384,1152]{1,0:T(8,128)(2,1)}, bf16[384,1152]{1,0:T(8,128)(2,1)S(1)}, u32[]{:S(2)}, u32[]{:S(2)}) collective-permute-start(bf16[384,1152]{1,0:T(8,128)(2,1)} %fusion.2), channel_id=1, source_target_pairs={{0,15},{1,0},{2,1},{3,2},{4,3},{5,4},{6,5},{7,6},{8,7},{9,8},{10,9... | collective-permute-start | bytes 2654216 | tf_op jit(solution)/shard_map/ppermute | solution.py:542
  109.8 0.0 copy-done.4
  109.8 0.0 copy-done.5
  109.8 10.2 %shard_map.102 = bf16[384,1152]{1,0:T(8,128)(2,1)} custom-call(f32[768,1152]{1,0:T(8,128)} %get-tuple-element.43.h1, bf16[768,1152]{1,0:T(8,128)(2,1)} %get-tuple-element.44.cq, bf16[2,1152,384]{2,1,0:T(8,128)(2,1)} %bitcast.24, bf16[1152,1152]{1,0:T(8,128)(2,1)} %wc_hbm.5, bf16[128,1152]{1,0:T(8,128)(2,1)} %copy-done.4, bf16[128,1152]{1,0:T(8,128)(2,1)} %copy-done.5), custom_call_target="tpu_custom_call" | custom-call | flops 3737124864 | bytes 7962624 | tf_op jit(solution)/shard_map/pallas_call | solution.py:482
  120.0 3.3 %collective-permute-done.6 = bf16[384,1152]{1,0:T(8,128)(2,1)S(1)} collective-permute-done((bf16[384,1152]{1,0:T(8,128)(2,1)}, bf16[384,1152]{1,0:T(8,128)(2,1)S(1)}, u32[]{:S(2)}, u32[]{:S(2)}) %collective-permute-start.6) | collective-permute-done | bytes 884768 | tf_op jit(solution)/shard_map/ppermute | solution.py:542
  123.3 1.0 copy-done.3
  124.3 3.4 %shard_map.104 = bf16[24,24,1152]{2,1,0:T(8,128)(2,1)} custom-call(s32[1]{0:T(128)} %bitcast.lat_ref, bf16[24,16,1152]{2,1,0:T(8,128)(2,1)} %bitcast.28, bf16[24,16,1152]{2,1,0:T(8,128)(2,1)} %bitcast.27), custom_call_target="tpu_custom_call" | custom-call | flops 2654208 | bytes 5308416 | tf_op jit(solution)/shard_map/pallas_call | solution.py:522
  (6 shorter events, 0.1 us)
Async XLA Ops:
  0.0 20.7 %copy-start = (bf16[256,3456]{1,0:T(8,128)(2,1)S(1)}, bf16[256,3456]{1,0:T(8,128)(2,1)}, u32[]{:S(2)}) copy-start(bf16[256,3456]{1,0:T(8,128)(2,1)} %param.17) | copy-start | bytes 5308420
  3.8 18.6 %collective-permute-start = (bf16[96,1152]{1,0:T(8,128)(2,1)}, bf16[96,1152]{1,0:T(8,128)(2,1)}, u32[]{:S(2)}, u32[]{:S(2)}) collective-permute-start(bf16[96,1152]{1,0:T(8,128)(2,1)} %reshape.108), channel_id=1, source_target_pairs={{0,1},{1,2},{2,3},{3,4},{4,5},{5,6},{6,7},{7,8},{8,9},{9,10},{10,1... | collective-permute-start | bytes 663560 | tf_op jit(solution)/shard_map/ppermute | solution.py:542
  7.8 15.4 %collective-permute-start.1 = (bf16[96,1152]{1,0:T(8,128)(2,1)}, bf16[96,1152]{1,0:T(8,128)(2,1)}, u32[]{:S(2)}, u32[]{:S(2)}) collective-permute-start(bf16[96,1152]{1,0:T(8,128)(2,1)} %reshape.110), channel_id=1, source_target_pairs={{0,15},{1,0},{2,1},{3,2},{4,3},{5,4},{6,5},{7,6},{8,7},{9,8},{10,9... | collective-permute-start | bytes 663560 | tf_op jit(solution)/shard_map/ppermute | solution.py:542
  9.3 34.0 %all-to-all-start = ((bf16[16,2,72,384]{3,2,1,0:T(8,128)(2,1)}), bf16[16,2,72,384]{3,2,1,0:T(8,128)(2,1)S(1)}, u32[]{:S(2)}, u32[]{:S(2)}) async-start(bf16[16,2,72,384]{3,2,1,0:T(8,128)(2,1)} %broadcast_in_dim.7), calls=%async_computation | async-start | bytes 3538944 | tf_op jit(solution)/shard_map/all_to_all | solution.py:571
  20.7 3.3 %copy-start.1 = (bf16[4,24,1152]{2,1,0:T(8,128)(2,1)S(1)}, bf16[4,24,1152]{2,1,0:T(8,128)(2,1)}, u32[]{:S(2)}) copy-start(bf16[4,24,1152]{2,1,0:T(8,128)(2,1)} %get-tuple-element.47) | copy-start | bytes 663556
  20.7 3.3 %copy-start.2 = (bf16[4,24,1152]{2,1,0:T(8,128)(2,1)S(1)}, bf16[4,24,1152]{2,1,0:T(8,128)(2,1)}, u32[]{:S(2)}) copy-start(bf16[4,24,1152]{2,1,0:T(8,128)(2,1)} %get-tuple-element.48) | copy-start | bytes 663556
  24.9 19.8 %collective-permute-start.2 = (bf16[128,1152]{1,0:T(8,128)(2,1)}, bf16[128,1152]{1,0:T(8,128)(2,1)}, u32[]{:S(2)}, u32[]{:S(2)}) collective-permute-start(bf16[128,1152]{1,0:T(8,128)(2,1)} %get-tuple-element.40), channel_id=1, source_target_pairs={{0,16},{1,17},{2,18},{3,19},{4,20},{5,21},{6,22},{7,23},{8,24},{9,... | collective-permute-start | bytes 884744 | tf_op jit(solution)/shard_map/ppermute | solution.py:542
  28.1 16.7 %collective-permute-start.3 = (bf16[128,1152]{1,0:T(8,128)(2,1)}, bf16[128,1152]{1,0:T(8,128)(2,1)}, u32[]{:S(2)}, u32[]{:S(2)}) collective-permute-start(bf16[128,1152]{1,0:T(8,128)(2,1)} %get-tuple-element.41), channel_id=1, source_target_pairs={{16,0},{17,1},{18,2},{19,3},{20,4},{21,5},{22,6},{23,7},{24,8},{25... | collective-permute-start | bytes 884744 | tf_op jit(solution)/shard_map/ppermute | solution.py:542
  87.8 16.8 %collective-permute-start.4 = (bf16[128,1152]{1,0:T(8,128)(2,1)}, bf16[128,1152]{1,0:T(8,128)(2,1)S(1)}, u32[]{:S(2)}, u32[]{:S(2)}) collective-permute-start(bf16[128,1152]{1,0:T(8,128)(2,1)} %get-tuple-element.45), channel_id=1, source_target_pairs={{0,16},{1,17},{2,18},{3,19},{4,20},{5,21},{6,22},{7,23},{8,24},{9,... | collective-permute-start | bytes 884744 | tf_op jit(solution)/shard_map/ppermute | solution.py:542
  89.7 16.6 %collective-permute-start.5 = (bf16[128,1152]{1,0:T(8,128)(2,1)}, bf16[128,1152]{1,0:T(8,128)(2,1)S(1)}, u32[]{:S(2)}, u32[]{:S(2)}) collective-permute-start(bf16[128,1152]{1,0:T(8,128)(2,1)} %get-tuple-element.46), channel_id=1, source_target_pairs={{16,0},{17,1},{18,2},{19,3},{20,4},{21,5},{22,6},{23,7},{24,8},{25... | collective-permute-start | bytes 884744 | tf_op jit(solution)/shard_map/ppermute | solution.py:542
  104.6 5.2 %copy-start.4 = (bf16[128,1152]{1,0:T(8,128)(2,1)}, bf16[128,1152]{1,0:T(8,128)(2,1)S(1)}, u32[]{:S(2)}) copy-start(bf16[128,1152]{1,0:T(8,128)(2,1)S(1)} %collective-permute-done.4.rest_0_) | copy-start | bytes 884740
  106.3 3.5 %copy-start.5 = (bf16[128,1152]{1,0:T(8,128)(2,1)}, bf16[128,1152]{1,0:T(8,128)(2,1)S(1)}, u32[]{:S(2)}) copy-start(bf16[128,1152]{1,0:T(8,128)(2,1)S(1)} %collective-permute-done.5.rest_1_) | copy-start | bytes 884740
  108.0 15.3 %collective-permute-start.6 = (bf16[384,1152]{1,0:T(8,128)(2,1)}, bf16[384,1152]{1,0:T(8,128)(2,1)S(1)}, u32[]{:S(2)}, u32[]{:S(2)}) collective-permute-start(bf16[384,1152]{1,0:T(8,128)(2,1)} %fusion.2), channel_id=1, source_target_pairs={{0,15},{1,0},{2,1},{3,2},{4,3},{5,4},{6,5},{7,6},{8,7},{9,8},{10,9... | collective-permute-start | bytes 2654216 | tf_op jit(solution)/shard_map/ppermute | solution.py:542
  123.3 1.0 copy-start.3

commit v4 on v3

--- a/solution.py
+++ b/solution.py
@@ -15,6 +15,7 @@
 WIN = 256
 TEXT_PAD = 384
 VMEM = 60 * 1024 * 1024
+SMALL = 30 * 1024 * 1024
 NN = (((1,), (0,)), ((), ()))
 NT = (((1,), (1,)), ((), ()))
 BF16, F32 = jnp.bfloat16, jnp.float32
@@ -22,15 +23,12 @@
 LOCAL = pl.BlockSpec(memory_space=pltpu.VMEM)
 
 
-def modulation(timestep, time_weight, modulation_bias):
-    half = time_weight.shape[0] // 2
+def embedding(timestep, size):
+    half = size // 2
     freqs = jnp.exp(-math.log(10000.0) * jnp.arange(half, dtype=F32) / half)
     angle = timestep.astype(F32)[:, None] * freqs[None, :]
     embed = jnp.concatenate([jnp.cos(angle), jnp.sin(angle)], axis=1)
-    embed = jax.nn.silu(embed).astype(BF16)
-    mixed = jnp.dot(embed, time_weight, preferred_element_type=F32) + modulation_bias.reshape(-1)[None, :]
-    width = modulation_bias.shape[1]
-    return (mixed[:, :width], mixed[:, width : 2 * width], mixed[:, 2 * width :])
+    return jax.nn.silu(embed).astype(BF16)
 
 
 def begin(pairs, sems, first):
@@ -210,10 +208,10 @@
 
 
 def attend_text(channels, text, q_ref, kv_ref, p_refs, bad_ref, rows, out_ref):
-    n = kv_ref.shape[2]
+    n = kv_ref.shape[1] // 2
 
     def scores(t, start, part, p_ref):
-        k = kv_ref[0, pl.ds(pair_start(t), WIN), :]
+        k = kv_ref[pl.ds(pair_start(t), WIN), :n]
         pair = [
             k * band(start + j * channels, start + (j + 1) * channels, (WIN, 1), 0) for j in range(2)
         ]
@@ -226,7 +224,7 @@
         p_ref[part, :] = jnp.exp2(s).astype(BF16)
 
     def values(t, start):
-        v = kv_ref[1, pl.ds(pair_start(t), WIN), :]
+        v = kv_ref[pl.ds(pair_start(t), WIN), n:]
         valid = band(0, text, (1, n), 1)
         spare = spare_columns(t, channels)
         pair = [
@@ -244,13 +242,74 @@
         heads_shifted(
             channels,
             q_ref,
-            lambda start: kv_ref[0, pl.ds(start, WIN), :],
+            lambda start: kv_ref[pl.ds(start, WIN), :n],
             NN,
-            lambda start: kv_ref[1, pl.ds(start, WIN), :],
+            lambda start: kv_ref[pl.ds(start, WIN), n:],
             NT,
             text,
             out_ref,
         )
+
+
+def prepare_kernel(emb, tw_ref, bias_ref, context_ref, kv_ref, heads_out, shift_ref, scale_ref, gate_ref, own_s, sems):
+    width = bias_ref.shape[1]
+    text = context_ref.shape[0]
+    lanes = own_s.shape[1] // 2
+    own_s[...] = jnp.zeros_like(own_s)
+    for j in range(2):
+        made = jnp.dot(context_ref[...], kv_ref[j], preferred_element_type=F32)
+        own_s[:, j * lanes : j * lanes + text] = made.T.astype(BF16)
+    sent = begin([(own_s, heads_out.at[h]) for h in range(heads_out.shape[0])], sems, 0)
+    for j, out in enumerate((shift_ref, scale_ref, gate_ref)):
+        cols = slice(j * width, (j + 1) * width)
+        out[...] = jnp.dot(emb[...], tw_ref[:, cols], preferred_element_type=F32) + bias_ref[j : j + 1, :]
+    finish_all(sent)
+
+
+def prepare(copies, emb, time_weight, bias, context, cross_kv):
+    width = bias.shape[1]
+    channels = cross_kv.shape[2]
+    return pl.pallas_call(
+        prepare_kernel,
+        out_shape=[jax.ShapeDtypeStruct((copies, channels, 2 * TEXT_PAD), BF16)]
+        + [jax.ShapeDtypeStruct((1, width), F32)] * 3,
+        in_specs=[LOCAL] * 5,
+        out_specs=[ANY] + [LOCAL] * 3,
+        scratch_shapes=[
+            pltpu.VMEM((channels, 2 * TEXT_PAD), BF16),
+            pltpu.SemaphoreType.DMA((copies,)),
+        ],
+        compiler_params=pltpu.CompilerParams(vmem_limit_bytes=SMALL),
+        cost_estimate=pl.CostEstimate(
+            flops=4 * context.shape[0] * width * channels, bytes_accessed=6 * 1024 * 1024, transcendentals=0
+        ),
+    )(emb, time_weight, bias, context, cross_kv)
+
+
+def pack_kernel(x_ref, top_ref, bottom_ref, first_out, last_out, first_s, last_s):
+    rim, core = top_ref.shape[0], x_ref.shape[0]
+    rows = [(top_ref, a) for a in range(rim)] + [(x_ref, r) for r in range(core)]
+    rows += [(bottom_ref, a) for a in range(rim)]
+    for n, (ref, r) in enumerate(rows):
+        tokens = ref[r].astype(F32)
+        first_s[rim * n : rim * (n + 1), :] = tokens[:rim]
+        last_s[rim * n : rim * (n + 1), :] = tokens[core - rim :]
+    first_out[...] = first_s[...].astype(BF16)
+    last_out[...] = last_s[...].astype(BF16)
+
+
+def pack(x, top, bottom):
+    rim, core, width = top.shape
+    count = rim * (core + 2 * rim)
+    return pl.pallas_call(
+        pack_kernel,
+        out_shape=[jax.ShapeDtypeStruct((count, width), BF16)] * 2,
+        in_specs=[LOCAL] * 3,
+        out_specs=[LOCAL] * 2,
+        scratch_shapes=[pltpu.VMEM((count, width), F32)] * 2,
+        compiler_params=pltpu.CompilerParams(vmem_limit_bytes=SMALL),
+        cost_estimate=pl.CostEstimate(flops=0, bytes_accessed=3 * 1024 * 1024, transcendentals=0),
+    )(x, top, bottom)
 
 
 QKV_PART = 512
@@ -295,9 +354,10 @@
 
 def regroup(core, rim, source_ref, target_ref):
     half = core // 2
-    inner = core * core
-    side = core * rim
-    edge = side + 2 * rim * rim
+    left = core * core
+    right = left + rim * (core + 2 * rim)
+    top = right + rim * (core + 2 * rim)
+    bottom = top + rim * core
     at = 0
 
     def take(*pieces):
@@ -306,15 +366,15 @@
             target_ref[at : at + n, :] = source_ref[start : start + n, :]
             at += n
 
-    for base in (inner + 2 * side, inner + 2 * side + edge):
+    for base, row in ((top, 0), (bottom, rim + core)):
         for a in range(rim):
-            take((base + rim * a, rim), (base + rim * rim + core * a, half))
+            take((left + rim * (row + a), rim), (base + core * a, half))
         for a in range(rim):
-            take((base + rim * rim + core * a + half, half), (base + rim * rim + side + rim * a, rim))
+            take((base + core * a + half, half), (right + rim * (row + a), rim))
     for r in range(core):
-        take((inner + rim * r, rim), (core * r, half))
+        take((left + rim * (rim + r), rim), (core * r, half))
     for r in range(core):
-        take((core * r + half, half), (inner + side + rim * r, rim))
+        take((core * r + half, half), (right + rim * (rim + r), rim))
 
 
 def tile_kernel(
@@ -407,7 +467,7 @@
     waits_h += begin([(x_s.at[kept], cq_out)], sems, 19)
     outer_rows = pl.ds(0, edges)
     found = attn_s.at[outer_rows]
-    room = (outer_rows, pl.ds(0, 2 * kv_s.shape[2]))
+    room = (outer_rows, pl.ds(0, kv_s.shape[1]))
     attend_text(channels, text, x_s.at[outer_rows], kv_s, (p_a.at[room], p_b.at[room]), bad_s, edges, found)
     made = hg_s[:edges, :] + jnp.dot(found[...], wc_s[...], preferred_element_type=F32)
     top_out[...] = made[: edges // 2].astype(BF16)
@@ -478,7 +538,7 @@
 
 def tile_text(text, first, count, h1, cq, text_kv, weight, *added):
     width = h1.shape[1]
-    padded = text_kv.shape[2]
+    padded = text_kv.shape[1] // 2
     return pl.pallas_call(
         functools.partial(text_kernel, text, first),
         out_shape=jax.ShapeDtypeStruct((count, width), BF16),
@@ -487,7 +547,7 @@
         scratch_shapes=[
             pltpu.VMEM((count, width), BF16),
             pltpu.VMEM((count, width), F32),
-            pltpu.VMEM((2, width, padded), BF16),
+            pltpu.VMEM(text_kv.shape, BF16),
             pltpu.VMEM((width, width), BF16),
             pltpu.VMEM((count, 2 * padded), BF16),
             pltpu.VMEM((count, 2 * padded), BF16),
@@ -504,27 +564,69 @@
     )(h1, cq, text_kv, weight, *added)
 
 
-def merge_kernel(lat_count, rim, lat_ref, near, far, out_ref):
+def patch_kernel(low, high, main_in, main_out, first_s, last_s, sems):
+    del main_in
+    n = first_s.shape[0]
+    count = main_out.shape[0]
+    ends = [(main_out.at[pl.ds(0, n)], first_s, low), (main_out.at[pl.ds(count - n, n)], last_s, high)]
+    finish_all(begin([(ref, room) for ref, room, _ in ends], sems, 0))
+    for _, room, add in ends:
+        room[...] = (room[...].astype(F32) + add[:n, :].astype(F32)).astype(BF16)
+    finish_all(begin([(room, ref) for ref, room, _ in ends], sems, 2))
+
+
+def patch(low, high, main):
+    n, width = low.shape[0] // 2, low.shape[1]
+    return pl.pallas_call(
+        patch_kernel,
+        out_shape=jax.ShapeDtypeStruct(main.shape, BF16),
+        in_specs=[LOCAL, LOCAL, ANY],
+        out_specs=ANY,
+        input_output_aliases={2: 0},
+        scratch_shapes=[
+            pltpu.VMEM((n, width), BF16),
+            pltpu.VMEM((n, width), BF16),
+            pltpu.SemaphoreType.DMA((4,)),
+        ],
+        compiler_params=pltpu.CompilerParams(vmem_limit_bytes=SMALL),
+        cost_estimate=pl.CostEstimate(flops=0, bytes_accessed=8 * n * width, transcendentals=0),
+    )(low, high, main)
+
+
+def merge_kernel(lat_count, rim, lat_ref, near, far, out_hbm, near_s, out_s, sems):
     lat = lat_ref[0]
-    rows = near.shape[0]
-    ids = lax.broadcasted_iota(jnp.int32, (rows, 1, 1), 0) + pl.program_id(0) * rows
-    core = pl.num_programs(0) * rows
-    shared = ((ids < rim) & (lat > 0)) | ((ids >= core - rim) & (lat < lat_count - 1))
-    scale = jnp.where(shared, 0.5, 1.0)
-    a, b = near[...].astype(F32) * scale, far[...].astype(F32) * scale
-    out_ref[...] = jnp.concatenate([a[:, :8], (a[:, 8:] + b[:, :8]) * 0.5, b[:, 8:]], axis=1).astype(BF16)
+    core = near.shape[0]
+    rows = 8
+    steps = range(core // rows)
+    waits = begin([(near.at[pl.ds(i * rows, rows)], near_s.at[pl.ds(i * rows, rows)]) for i in steps], sems, 0)
+    sent = []
+    for i in steps:
+        waits[i].wait()
+        part = slice(i * rows, (i + 1) * rows)
+        ids = lax.broadcasted_iota(jnp.int32, (rows, 1, 1), 0) + i * rows
+        shared = ((ids < rim) & (lat > 0)) | ((ids >= core - rim) & (lat < lat_count - 1))
+        scale = jnp.where(shared, 0.5, 1.0)
+        a, b = near_s[part].astype(F32) * scale, far[part].astype(F32) * scale
+        made = jnp.concatenate([a[:, :8], (a[:, 8:] + b[:, :8]) * 0.5, b[:, 8:]], axis=1)
+        out_s[part] = made.astype(BF16)
+        here = pl.ds(i * rows, rows)
+        sent += begin([(out_s.at[here], out_hbm.at[here])], sems, len(steps) + i)
+    finish_all(sent)
 
 
 def merge(lat_count, lat, rim, near, far):
     core, span, width = near.shape
-    rows = 8
-    part = pl.BlockSpec((rows, span, width), lambda i: (i, 0, 0))
     return pl.pallas_call(
         functools.partial(merge_kernel, lat_count, rim),
         out_shape=jax.ShapeDtypeStruct((core, core, width), BF16),
-        grid=(core // rows,),
-        in_specs=[pl.BlockSpec(memory_space=pltpu.SMEM), part, part],
-        out_specs=pl.BlockSpec((rows, core, width), lambda i: (i, 0, 0)),
+        in_specs=[pl.BlockSpec(memory_space=pltpu.SMEM), ANY, LOCAL],
+        out_specs=ANY,
+        scratch_shapes=[
+            pltpu.VMEM((core, span, width), BF16),
+            pltpu.VMEM((core, core, width), BF16),
+            pltpu.SemaphoreType.DMA((6,)),
+        ],
+        compiler_params=pltpu.CompilerParams(vmem_limit_bytes=SMALL),
         cost_estimate=pl.CostEstimate(
             flops=4 * core * core * width, bytes_accessed=8 * core * core * width, transcendentals=0
         ),
@@ -563,24 +665,20 @@
     to = functools.partial(send, mesh_sizes=sizes)
     q_factor = math.log2(math.e) / math.sqrt(width // HEADS)
 
-    padded = jnp.pad(context[0], ((0, TEXT_PAD - text), (0, 0)))
-    own_head = jnp.einsum("td,sde->set", padded, cross_kv, preferred_element_type=F32).astype(BF16)
     x = hidden[0]
-    x, own_head = lax.optimization_barrier((x, own_head))
-    copies = jnp.broadcast_to(own_head[None], (lon_count,) + own_head.shape)
-    all_heads = lax.all_to_all(copies, "lon", 0, 0, tiled=True)
-    left = to(x[:, core - rim :].reshape(-1, width), down=0, right=1)
-    right = to(x[:, :rim].reshape(-1, width), down=0, right=-1)
-    shift, scale, gate = modulation(timestep, time_weight, modulation_bias)
-    corner = rim * rim
-    low_edge = jnp.concatenate([left[-corner:], x[core - rim :].reshape(-1, width), right[-corner:]], axis=0)
-    high_edge = jnp.concatenate([left[:corner], x[:rim].reshape(-1, width), right[:corner]], axis=0)
-    x, low_edge, high_edge = lax.optimization_barrier((x, low_edge, high_edge))
-    top = to(low_edge, down=1, right=0)
-    bottom = to(high_edge, down=-1, right=0)
-    x_core = x.reshape(core * core, width)
+    flat = lambda a: a.reshape(-1, width)
+    top = to(flat(x[core - rim :]), down=1, right=0)
+    bottom = to(flat(x[:rim]), down=-1, right=0)
+    emb = embedding(timestep, time_weight.shape[0])
+    copies, shift, scale, gate = prepare(lon_count, emb, time_weight, modulation_bias, context[0], cross_kv)
+    text_kv = lax.all_to_all(copies, "lon", 0, 0, tiled=True).reshape(width, 2 * TEXT_PAD)
+    rows = lambda a: a.reshape(rim, core, width)
+    first, last = pack(x, rows(top), rows(bottom))
+    left = to(last, down=0, right=1)
+    right = to(first, down=0, right=-1)
+    x, first, last = lax.optimization_barrier((x, first, last))
+    x_core = flat(x)
     qkv_core = core_qkv(q_factor, x_core, shift, scale, qkv_weight)
-    text_kv = jnp.transpose(all_heads, (1, 0, 2, 3)).reshape(2, width, TEXT_PAD)
 
     h1, cq, top_made, bottom_made = tile_self(
         core,
@@ -595,13 +693,11 @@
         text_kv,
     )
     span = half + rim
-    block, edge = core * span, rim * span
+    block = core * span
     high = to(top_made, down=-1, right=0)
     low = to(bottom_made, down=1, right=0)
     main = tile_text(text, 0, block, h1, cq, text_kv, cross_output_projection)
-    main = main.at[:edge].add(low[:edge])
-    main = main.at[block - edge :].add(high[:edge])
-    far = to(main, down=0, right=-1)
+    far = to(patch(low, high, main), down=0, right=-1)
     near = tile_text(text, block, block, h1, cq, text_kv, cross_output_projection, low, high)
     shape = lambda a: a.reshape(core, span, width)
     lat = lax.axis_index("lat").astype(jnp.int32)[None]

time: 129 us -> 132 us (1.023)
  waiting for transfers between devices: 3.29 us -> 9.64 us
  starting transfers between devices: 27.6 us -> 33 us
  other arithmetic: 4.38 us -> 0.06 us
  local copies, waits for them, and re-layouts: 12.1 us -> 8.36 us
  matrix products: 2.81 us -> 0 us
  Pallas kernels: 76.7 us -> 78.8 us
    unnamed x12 -> x29, local copies, waits for them, and re-layouts: 1 us -> 8.33 us
    ppermute x7, waiting for transfers between devices: 3.29 us -> 9.64 us  [send(): return lax.ppermute(value, ('lat', 'lon'), pairs)]
    slice x5 -> x1, local copies, waits for them, and re-layouts: 5.35 us -> 0.04 us  [local(): bottom = to(flat(x[:rim]), down=-1, right=0)]
    ppermute x7, starting transfers between devices: 20 us -> 25.3 us  [send(): return lax.ppermute(value, ('lat', 'lon'), pairs)]
    pallas_call x0 -> x3, Pallas kernels: none -> 4.3 us  [the longest x1 2.09 us: prepare(): pl.pallas_call(prepare_kernel, out_shape=[jax.ShapeDtypeStruct((copies, c...]
    scatter-add x2 -> x0, other arithmetic: 3.43 us -> none  [the longest x1 1.72 us: local(): main = main.at[:edge].add(low[:edge])]
    pallas_call x1, Pallas kernels: 3.44 us -> 1.36 us  [merge(): pl.pallas_call(functools.partial(merge_kernel, lat_count, rim), out_shape...]
    unnamed x1 -> x0, matrix products: 1.73 us -> none
  transfers between devices with their start and end apart: 8 -> 8, of which waited for: 1 -> 2; matrix products, arithmetic and copies ran while one was open for 10% -> 0% of each run, Pallas kernels for 24% -> 23%
where the time goes in v4:
time: 132 us; the launch traced here: 131 us
  Pallas kernels  78.8 us (60%)
  starting transfers between devices  33 us (25%)
  waiting for transfers between devices  9.64 us (7%)
  local copies, waits for them, and re-layouts  8.36 us (6%)
    pallas_call x1, Pallas kernels, tile_self(): pl.pallas_call(functools.partial(tile_kernel, core, rim, 512, text, q_fac...  42.9 us
    ppermute x7, starting transfers between devices, send(): return lax.ppermute(value, ('lat', 'lon'), pairs)  25.3 us
    pallas_call x2, Pallas kernels, tile_text(): pl.pallas_call(functools.partial(text_kernel, text, first), out_shape=jax...  19.3 us
    pallas_call x1, Pallas kernels, core_qkv(): pl.pallas_call(functools.partial(core_kernel, q_factor), out_shape=jax.Sh...  10.9 us
    ppermute x7, waiting for transfers between devices, send(): return lax.ppermute(value, ('lat', 'lon'), pairs)  9.64 us
    unnamed x29, local copies, waits for them, and re-layouts  8.33 us
    all_to_all x1, starting transfers between devices, local(): lax.all_to_all(copies, 'lon', 0, 0, tiled=True).reshape(width, 2 * TEXT_PAD)  7.7 us
  transfers between devices with their start and end apart: 8, of which 2 were waited for; matrix products, arithmetic and copies ran while one was open for 0% of the time, Pallas kernels for 23%

profile of v4, /device:TPU:33, one launch (start us, length us, event | category | flops | bytes accessed | tf_op | source)
XLA Modules:
  0.0 131.0 jit_solution(16400970367827929859)
XLA Ops:
  0.7 1.3 copy.12.kv_ref
  2.0 0.0 copy-start.1
  2.0 1.5 %copy-done.1 = bf16[256,3456]{1,0:T(8,128)(2,1)S(1)} copy-done((bf16[256,3456]{1,0:T(8,128)(2,1)S(1)}, bf16[256,3456]{1,0:T(8,128)(2,1)}, u32[]{:S(2)}) %copy-start.1) | copy-done | bytes 1769496
  3.5 0.0 copy-start.3
  3.5 1.1 copy-done.3
  4.6 0.0 copy-start.8
  4.6 0.7 copy-done.8
  5.3 2.1 %shard_map.101 = (bf16[16,72,768]{2,1,0:T(8,128)(2,1)}, f32[1,1152]{1,0:T(1,128)S(1)}, f32[1,1152]{1,0:T(1,128)S(1)}, f32[1,1152]{1,0:T(1,128)S(1)}) custom-call(bf16[1,256]{1,0:T(2,128)(2,1)S(1)} %fusion.emb, bf16[256,3456]{1,0:T(8,128)(2,1)S(1)} %copy-done.1, f32[3,1152]{1,0:T(4,128)S(1)} %copy-done.8, bf16[300,1152]{1,0:T(8,128)(2,1)S(1)} %bitcast.22, ...), custom_call_target="tpu_custom_call" | custom-call | flops 99532800 | bytes 6291456 | tf_op jit(solution)/shard_map/pallas_call | solution.py:272
  7.4 0.0 copy-start.9
  7.4 0.6 copy-done.9
  8.0 0.0 copy-start.10
  8.0 0.6 copy-done.10
  8.6 0.6 copy-done.11
  9.2 7.7 %all-to-all-start = ((bf16[16,72,768]{2,1,0:T(8,128)(2,1)}), bf16[16,72,768]{2,1,0:T(8,128)(2,1)}, u32[]{:S(2)}, u32[]{:S(2)}) async-start(bf16[16,72,768]{2,1,0:T(8,128)(2,1)} %get-tuple-element.22), calls=%async_computation | async-start | bytes 3538944 | tf_op jit(solution)/shard_map/all_to_all | solution.py:674
  16.9 0.0 copy-done
  17.0 3.1 %collective-permute-start = (bf16[96,1152]{1,0:T(8,128)(2,1)S(1)}, bf16[96,1152]{1,0:T(8,128)(2,1)S(1)}, u32[]{:S(2)}, u32[]{:S(2)}) collective-permute-start(bf16[96,1152]{1,0:T(8,128)(2,1)S(1)} %bitcast.26), channel_id=1, source_target_pairs={{0,16},{1,17},{2,18},{3,19},{4,20},{5,21},{6,22},{7,23},{8,24},{9,... | collective-permute-start | bytes 663560 | tf_op jit(solution)/shard_map/ppermute | solution.py:644
  20.1 4.3 %collective-permute-start.1 = (bf16[96,1152]{1,0:T(8,128)(2,1)S(1)}, bf16[96,1152]{1,0:T(8,128)(2,1)S(1)}, u32[]{:S(2)}, u32[]{:S(2)}) collective-permute-start(bf16[96,1152]{1,0:T(8,128)(2,1)S(1)} %bitcast.25), channel_id=1, source_target_pairs={{16,0},{17,1},{18,2},{19,3},{20,4},{21,5},{22,6},{23,7},{24,8},{25... | collective-permute-start | bytes 663560 | tf_op jit(solution)/shard_map/ppermute | solution.py:644
  24.4 6.9 %collective-permute-done.top = bf16[96,1152]{1,0:T(8,128)(2,1)S(1)} collective-permute-done((bf16[96,1152]{1,0:T(8,128)(2,1)S(1)}, bf16[96,1152]{1,0:T(8,128)(2,1)S(1)}, u32[]{:S(2)}, u32[]{:S(2)}) %collective-permute-start) | collective-permute-done | bytes 221216 | tf_op jit(solution)/shard_map/ppermute | solution.py:644
  31.2 0.0 collective-permute-done.1.bottom
  31.3 0.2 shard_map.100
  31.5 6.7 %collective-permute-start.2 = (bf16[128,1152]{1,0:T(8,128)(2,1)S(1)}, bf16[128,1152]{1,0:T(8,128)(2,1)S(1)}, u32[]{:S(2)}, u32[]{:S(2)}) collective-permute-start(bf16[128,1152]{1,0:T(8,128)(2,1)S(1)} %get-tuple-element.17), channel_id=1, source_target_pairs={{0,1},{1,2},{2,3},{3,4},{4,5},{5,6},{6,7},{7,8},{8,9},{9,10},{10,1... | collective-permute-start | bytes 884744 | tf_op jit(solution)/shard_map/ppermute | solution.py:644
  38.2 0.0 collective-permute-start.3
  38.2 10.9 %shard_map.102.qkv_core = bf16[576,3456]{1,0:T(8,128)(2,1)} custom-call(bf16[576,1152]{1,0:T(8,128)(2,1)} %bitcast.17, f32[1,1152]{1,0:T(1,128)} %copy-done.9, f32[1,1152]{1,0:T(1,128)} %copy-done.10, bf16[1152,3456]{1,0:T(8,128)(2,1)} %w_hbm.3), custom_call_target="tpu_custom_call" | custom-call | flops 4586471424 | bytes 13271040 | tf_op jit(solution)/shard_map/pallas_call | solution.py:335
  49.1 0.0 copy-done.6
  49.1 0.0 copy-done.7
  49.1 0.0 collective-permute-done.2.left
  49.2 0.0 copy-start.12
  49.2 0.0 collective-permute-done.3.right
  49.2 0.0 copy-start.13
  49.2 0.0 all-to-all-done
  49.2 0.7 copy-done.12
  49.9 0.1 copy-done.13
  50.0 42.9 %shard_map.103 = (f32[768,1152]{1,0:T(8,128)}, bf16[768,1152]{1,0:T(8,128)(2,1)}, bf16[128,1152]{1,0:T(8,128)(2,1)}, bf16[128,1152]{1,0:T(8,128)(2,1)}) custom-call(bf16[576,1152]{1,0:T(8,128)(2,1)} %bitcast.18, bf16[128,1152]{1,0:T(8,128)(2,1)} %copy-done.12, bf16[128,1152]{1,0:T(8,128)(2,1)} %copy-done.13, bf16[96,1152]{1,0:T(8,128)(2,1)} %copy-done.6, ...), custom_call_target="tpu_custom_call" | custom-call | flops 28330426368 | bytes 24330240 | tf_op jit(solution)/shard_map/pallas_call | solution.py:485
  92.9 2.2 %collective-permute-start.4 = (bf16[128,1152]{1,0:T(8,128)(2,1)}, bf16[128,1152]{1,0:T(8,128)(2,1)S(1)}, u32[]{:S(2)}, u32[]{:S(2)}) collective-permute-start(bf16[128,1152]{1,0:T(8,128)(2,1)} %get-tuple-element.25), channel_id=1, source_target_pairs={{0,16},{1,17},{2,18},{3,19},{4,20},{5,21},{6,22},{7,23},{8,24},{9,... | collective-permute-start | bytes 884744 | tf_op jit(solution)/shard_map/ppermute | solution.py:644
  95.1 7.4 %collective-permute-start.5 = (bf16[128,1152]{1,0:T(8,128)(2,1)}, bf16[128,1152]{1,0:T(8,128)(2,1)S(1)}, u32[]{:S(2)}, u32[]{:S(2)}) collective-permute-start(bf16[128,1152]{1,0:T(8,128)(2,1)} %get-tuple-element.26), channel_id=1, source_target_pairs={{16,0},{17,1},{18,2},{19,3},{20,4},{21,5},{22,6},{23,7},{24,8},{25... | collective-permute-start | bytes 884744 | tf_op jit(solution)/shard_map/ppermute | solution.py:644
  102.5 9.2 %shard_map.105.main_in = bf16[384,1152]{1,0:T(8,128)(2,1)} custom-call(f32[768,1152]{1,0:T(8,128)} %get-tuple-element.23.h1, bf16[768,1152]{1,0:T(8,128)(2,1)} %get-tuple-element.24.cq, bf16[1152,768]{1,0:T(8,128)(2,1)} %bitcast.11.kv_hbm, bf16[1152,1152]{1,0:T(8,128)(2,1)} %wc_hbm.5), custom_call_target="tpu_custom_call" | custom-call | flops 3737124864 | bytes 7962624 | tf_op jit(solution)/shard_map/pallas_call | solution.py:542
  111.7 0.0 collective-permute-done.4.rest_0_.low
  111.7 0.0 copy-start.4
  111.7 0.0 collective-permute-done.5.rest_1_.high
  111.7 0.0 copy-start.5
  111.8 2.0 %shard_map.106 = bf16[384,1152]{1,0:T(8,128)(2,1)} custom-call(bf16[128,1152]{1,0:T(8,128)(2,1)S(1)} %collective-permute-done.4.rest_0_.low, bf16[128,1152]{1,0:T(8,128)(2,1)S(1)} %collective-permute-done.5.rest_1_.high, bf16[384,1152]{1,0:T(8,128)(2,1)} %shard_map.105.main_in), custom_call_target="tpu_custom_call", output_to_operand_aliasing={{}: (2, {})} | custom-call | bytes 589824 | tf_op jit(solution)/shard_map/pallas_call | solution.py:580
  113.7 1.6 %collective-permute-start.6 = (bf16[384,1152]{1,0:T(8,128)(2,1)}, bf16[384,1152]{1,0:T(8,128)(2,1)S(1)}, u32[]{:S(2)}, u32[]{:S(2)}) collective-permute-start(bf16[384,1152]{1,0:T(8,128)(2,1)} %shard_map.106), channel_id=1, source_target_pairs={{0,15},{1,0},{2,1},{3,2},{4,3},{5,4},{6,5},{7,6},{8,7},{9,8},{10,9... | collective-permute-start | bytes 2654216 | tf_op jit(solution)/shard_map/ppermute | solution.py:644
  115.3 0.0 copy-done.4
  115.3 0.0 copy-done.5
  115.3 10.2 %shard_map.104 = bf16[384,1152]{1,0:T(8,128)(2,1)} custom-call(f32[768,1152]{1,0:T(8,128)} %get-tuple-element.23.h1, bf16[768,1152]{1,0:T(8,128)(2,1)} %get-tuple-element.24.cq, bf16[1152,768]{1,0:T(8,128)(2,1)} %bitcast.11.kv_hbm, bf16[1152,1152]{1,0:T(8,128)(2,1)} %wc_hbm.5, bf16[128,1152]{1,0:T(8,128)(2,1)} %copy-done.4, bf16[128,1152]{1,0:T(8,128)(2,1)} %copy-done.5), custom_call_target="tpu_custom_call" | custom-call | flops 3737124864 | bytes 7962624 | tf_op jit(solution)/shard_map/pallas_call | solution.py:542
  125.5 2.8 %collective-permute-done.6 = bf16[384,1152]{1,0:T(8,128)(2,1)S(1)} collective-permute-done((bf16[384,1152]{1,0:T(8,128)(2,1)}, bf16[384,1152]{1,0:T(8,128)(2,1)S(1)}, u32[]{:S(2)}, u32[]{:S(2)}) %collective-permute-start.6) | collective-permute-done | bytes 884768 | tf_op jit(solution)/shard_map/ppermute | solution.py:644
  128.3 1.2 copy-done.2
  129.4 1.4 %shard_map.107 = bf16[24,24,1152]{2,1,0:T(8,128)(2,1)} custom-call(s32[1]{0:T(128)} %bitcast.lat_ref, bf16[24,16,1152]{2,1,0:T(8,128)(2,1)S(1)} %bitcast.21, bf16[24,16,1152]{2,1,0:T(8,128)(2,1)S(1)} %bitcast.20), custom_call_target="tpu_custom_call" | custom-call | flops 2654208 | bytes 5308416 | tf_op jit(solution)/shard_map/pallas_call | solution.py:619
  (8 shorter events, 0.1 us)
Async XLA Ops:
  2.0 1.5 %copy-start.1 = (bf16[256,3456]{1,0:T(8,128)(2,1)S(1)}, bf16[256,3456]{1,0:T(8,128)(2,1)}, u32[]{:S(2)}) copy-start(bf16[256,3456]{1,0:T(8,128)(2,1)} %tw_ref.1) | copy-start | bytes 5308420
  3.5 1.1 copy-start.3
  4.6 0.7 copy-start.8
  7.4 0.6 copy-start.9
  8.0 0.6 copy-start.10
  8.6 0.6 copy-start.11
  9.2 7.7 %copy-start = (bf16[1,24,24,1152]{3,2,1,0:T(8,128)(2,1)S(1)}, bf16[1,24,24,1152]{3,2,1,0:T(8,128)(2,1)}, u32[]{:S(2)}) copy-start(bf16[1,24,24,1152]{3,2,1,0:T(8,128)(2,1)} %param.10) | copy-start | bytes 3981316
  9.2 40.0 %all-to-all-start = ((bf16[16,72,768]{2,1,0:T(8,128)(2,1)}), bf16[16,72,768]{2,1,0:T(8,128)(2,1)}, u32[]{:S(2)}, u32[]{:S(2)}) async-start(bf16[16,72,768]{2,1,0:T(8,128)(2,1)} %get-tuple-element.22), calls=%async_computation | async-start | bytes 3538944 | tf_op jit(solution)/shard_map/all_to_all | solution.py:674
  17.0 14.3 %collective-permute-start = (bf16[96,1152]{1,0:T(8,128)(2,1)S(1)}, bf16[96,1152]{1,0:T(8,128)(2,1)S(1)}, u32[]{:S(2)}, u32[]{:S(2)}) collective-permute-start(bf16[96,1152]{1,0:T(8,128)(2,1)S(1)} %bitcast.26), channel_id=1, source_target_pairs={{0,16},{1,17},{2,18},{3,19},{4,20},{5,21},{6,22},{7,23},{8,24},{9,... | collective-permute-start | bytes 663560 | tf_op jit(solution)/shard_map/ppermute | solution.py:644
  20.1 11.2 %collective-permute-start.1 = (bf16[96,1152]{1,0:T(8,128)(2,1)S(1)}, bf16[96,1152]{1,0:T(8,128)(2,1)S(1)}, u32[]{:S(2)}, u32[]{:S(2)}) collective-permute-start(bf16[96,1152]{1,0:T(8,128)(2,1)S(1)} %bitcast.25), channel_id=1, source_target_pairs={{16,0},{17,1},{18,2},{19,3},{20,4},{21,5},{22,6},{23,7},{24,8},{25... | collective-permute-start | bytes 663560 | tf_op jit(solution)/shard_map/ppermute | solution.py:644
  31.2 17.9 %copy-start.6 = (bf16[96,1152]{1,0:T(8,128)(2,1)}, bf16[96,1152]{1,0:T(8,128)(2,1)S(1)}, u32[]{:S(2)}) copy-start(bf16[96,1152]{1,0:T(8,128)(2,1)S(1)} %collective-permute-done.top) | copy-start | bytes 663556
  31.2 17.9 %copy-start.7 = (bf16[96,1152]{1,0:T(8,128)(2,1)}, bf16[96,1152]{1,0:T(8,128)(2,1)S(1)}, u32[]{:S(2)}) copy-start(bf16[96,1152]{1,0:T(8,128)(2,1)S(1)} %collective-permute-done.1.bottom) | copy-start | bytes 663556
  31.5 17.7 %collective-permute-start.2 = (bf16[128,1152]{1,0:T(8,128)(2,1)S(1)}, bf16[128,1152]{1,0:T(8,128)(2,1)S(1)}, u32[]{:S(2)}, u32[]{:S(2)}) collective-permute-start(bf16[128,1152]{1,0:T(8,128)(2,1)S(1)} %get-tuple-element.17), channel_id=1, source_target_pairs={{0,1},{1,2},{2,3},{3,4},{4,5},{5,6},{6,7},{7,8},{8,9},{9,10},{10,1... | collective-permute-start | bytes 884744 | tf_op jit(solution)/shard_map/ppermute | solution.py:644
  38.2 11.0 %collective-permute-start.3 = (bf16[128,1152]{1,0:T(8,128)(2,1)S(1)}, bf16[128,1152]{1,0:T(8,128)(2,1)S(1)}, u32[]{:S(2)}, u32[]{:S(2)}) collective-permute-start(bf16[128,1152]{1,0:T(8,128)(2,1)S(1)} %get-tuple-element.16), channel_id=1, source_target_pairs={{0,15},{1,0},{2,1},{3,2},{4,3},{5,4},{6,5},{7,6},{8,7},{9,8},{10,9... | collective-permute-start | bytes 884744 | tf_op jit(solution)/shard_map/ppermute | solution.py:644
  49.2 0.7 copy-start.12
  49.2 0.8 copy-start.13
  92.9 18.8 %collective-permute-start.4 = (bf16[128,1152]{1,0:T(8,128)(2,1)}, bf16[128,1152]{1,0:T(8,128)(2,1)S(1)}, u32[]{:S(2)}, u32[]{:S(2)}) collective-permute-start(bf16[128,1152]{1,0:T(8,128)(2,1)} %get-tuple-element.25), channel_id=1, source_target_pairs={{0,16},{1,17},{2,18},{3,19},{4,20},{5,21},{6,22},{7,23},{8,24},{9,... | collective-permute-start | bytes 884744 | tf_op jit(solution)/shard_map/ppermute | solution.py:644
  95.1 16.6 %collective-permute-start.5 = (bf16[128,1152]{1,0:T(8,128)(2,1)}, bf16[128,1152]{1,0:T(8,128)(2,1)S(1)}, u32[]{:S(2)}, u32[]{:S(2)}) collective-permute-start(bf16[128,1152]{1,0:T(8,128)(2,1)} %get-tuple-element.26), channel_id=1, source_target_pairs={{16,0},{17,1},{18,2},{19,3},{20,4},{21,5},{22,6},{23,7},{24,8},{25... | collective-permute-start | bytes 884744 | tf_op jit(solution)/shard_map/ppermute | solution.py:644
  111.7 3.6 %copy-start.4 = (bf16[128,1152]{1,0:T(8,128)(2,1)}, bf16[128,1152]{1,0:T(8,128)(2,1)S(1)}, u32[]{:S(2)}) copy-start(bf16[128,1152]{1,0:T(8,128)(2,1)S(1)} %collective-permute-done.4.rest_0_.low) | copy-start | bytes 884740
  111.7 3.6 %copy-start.5 = (bf16[128,1152]{1,0:T(8,128)(2,1)}, bf16[128,1152]{1,0:T(8,128)(2,1)S(1)}, u32[]{:S(2)}) copy-start(bf16[128,1152]{1,0:T(8,128)(2,1)S(1)} %collective-permute-done.5.rest_1_.high) | copy-start | bytes 884740
  113.7 14.5 %collective-permute-start.6 = (bf16[384,1152]{1,0:T(8,128)(2,1)}, bf16[384,1152]{1,0:T(8,128)(2,1)S(1)}, u32[]{:S(2)}, u32[]{:S(2)}) collective-permute-start(bf16[384,1152]{1,0:T(8,128)(2,1)} %shard_map.106), channel_id=1, source_target_pairs={{0,15},{1,0},{2,1},{3,2},{4,3},{5,4},{6,5},{7,6},{8,7},{9,8},{10,9... | collective-permute-start | bytes 2654216 | tf_op jit(solution)/shard_map/ppermute | solution.py:644
  128.3 1.2 copy-start.2
